TPU v7x, 32 devices: a whole 2x2x4 slice. The times are simulated.
32 devices in a mesh: blk: 8 (over y, x, core), gene: 4 (over z).
Axes of the slice: x: 2, y: 2, z: 4, core: 2. Of those that a mesh axis runs over, the one named last changes fastest.
Arguments:
- logits: float32 [11264, 1024], P(None, 'blk'), may hold values from -6 to 6
- expression: float32 [11264, 2048], P('blk', 'gene'), may hold values from 0.05 to 5
- spatial: float32 [1024, 2048], P('blk', 'gene'), may hold values from 0.05 to 5
- density: float32 [11264], replicated, may hold values from 0.1 to 10
- gene_mask: int32 [4, 2048], P(None, 'gene'), may hold values 0 or 1
- gene_counts: int32 [2048], P('gene'), may hold values from 1 to 10
- slide_ids: int32 [1024], P('blk'), may hold values from 0 to 3
Outputs:
- loss: float32 [], replicated
- logit_grad: float32 [11264, 1024], P(None, 'blk')
- expr_grad: float32 [11264, 2048], P('blk', 'gene')
- rms_map: float32 [], replicated
- rms_pred: float32 [], replicated
All inputs are finite; a program needn't handle non-finite values. No bound on the sum of `gene_mask` on one device may be relied on, other than what follows from the above.
Results may differ from a plain program's by a relative error of at most 0.0003.
Values sent between devices are 32-bit elements; how exact they have to be, the bound alone decides.
No kernel may reach another device: no remote copies, remote signals or barrier semaphores. Data moves between devices by JAX's collectives and lax.ppermute only.
A program may use at most 320 MiB of HBM per device.

v0:
```python
import jax
import jax.numpy as jnp
from jax import lax
from jax.sharding import PartitionSpec as P

GENES = 2048
SLIDES = 4


HIGH = lax.Precision.HIGHEST


def shards(logits, expression, spatial, density, gene_mask, gene_counts, slide_ids):
    n_blk = lax.axis_size("blk")
    n_gene = lax.axis_size("gene")
    cells = logits.shape[0]
    spot_dev = logits.shape[1]
    spots = spot_dev * n_blk
    peak = jnp.max(logits, axis=0, keepdims=True)
    expo = jnp.exp(logits - peak)
    mapping = expo / jnp.sum(expo, axis=0, keepdims=True)
    rows = mapping
    pred = lax.dot_general(
        rows,
        lax.all_gather(expression, "blk", axis=0, tiled=True),
        (((0,), (0,)), ((), ())),
        precision=HIGH,
        preferred_element_type=jnp.float32,
    )
    onehot = (slide_ids[None, :] == jnp.arange(SLIDES, dtype=jnp.int32)[:, None]).astype(
        jnp.float32
    )
    part_a = jnp.dot(onehot, pred * spatial, precision=HIGH)
    part_b = jnp.dot(onehot, pred * pred, precision=HIGH)
    part_c = jnp.dot(onehot, spatial * spatial, precision=HIGH)
    part_q = jnp.sum(mapping, axis=1) / spots
    sum_a, sum_b, sum_c, cell_q = lax.psum((part_a, part_b, part_c, part_q), "blk")
    sum_e, sum_f, sum_h = lax.psum(
        (
            jnp.sum(pred * spatial, axis=1),
            jnp.sum(pred * pred, axis=1),
            jnp.sum(spatial * spatial, axis=1),
        ),
        "gene",
    )
    inv_g = lax.rsqrt(sum_b * sum_c + 1e-06)
    gcos = sum_a * inv_g
    weights = (gene_mask * gene_counts[None, :]).astype(jnp.float32)
    inv_s = lax.rsqrt(sum_f * sum_h + 1e-06)
    scos = sum_e * inv_s
    target = density / jnp.sum(density)
    kl_term = jnp.sum(target * (jnp.log(target) - jnp.log(cell_q)))
    partials = jnp.stack(
        [
            jnp.sum(weights * gcos) / n_blk,
            jnp.sum(weights) / n_blk,
            jnp.sum(scos) / n_gene,
            jnp.sum(sum_f) / n_gene,
            jnp.sum(mapping * mapping) / n_gene,
        ]
    )
    totals = lax.psum(partials, ("blk", "gene"))
    wsum = totals[1]
    loss = -totals[0] / wsum - totals[2] / spots + kl_term
    rms_map = jnp.sqrt(totals[4] / (cells * spots))
    rms_pred = jnp.sqrt(totals[3] / (spots * GENES))
    share = weights / wsum
    grad_a = -share * inv_g
    grad_b = 0.5 * share * sum_a * sum_c * inv_g * inv_g * inv_g
    spread_a = lax.dot_general(onehot, grad_a, (((0,), (0,)), ((), ())), precision=HIGH)
    spread_b = lax.dot_general(onehot, grad_b, (((0,), (0,)), ((), ())), precision=HIGH)
    dpred = spread_a * spatial + 2.0 * spread_b * pred
    dpred = (
        dpred
        - (inv_s[:, None] * spatial - (sum_e * sum_h * inv_s * inv_s * inv_s)[:, None] * pred)
        / spots
    )
    dmap_part = lax.dot_general(
        lax.all_gather(expression, "blk", axis=0, tiled=True),
        dpred,
        (((1,), (1,)), ((), ())),
        precision=HIGH,
        preferred_element_type=jnp.float32,
    )
    rows = mapping
    expr_grad = (
        lax.psum_scatter(
            jnp.dot(rows, dpred, precision=HIGH, preferred_element_type=jnp.float32),
            "blk",
            scatter_dimension=0,
            tiled=True,
        )
        * cells
    )
    dmap = lax.psum(dmap_part, "gene")
    dmap = dmap - (target / cell_q / spots)[:, None]
    logit_grad = mapping * (dmap - jnp.sum(mapping * dmap, axis=0, keepdims=True)) * cells
    return (loss, logit_grad, expr_grad, rms_map, rms_pred)


def solution(mesh):
    placed = (
        P(None, "blk"),
        P("blk", "gene"),
        P("blk", "gene"),
        P(),
        P(None, "gene"),
        P("gene"),
        P("blk"),
    )
    return jax.shard_map(
        shards,
        mesh=mesh,
        in_specs=placed,
        out_specs=(P(), P(None, "blk"), P("blk", "gene"), P(), P()),
        check_vma=False,
    )
```

profile of v0, /device:TPU:0, one launch (start us, length us, event | category | flops | bytes accessed | tf_op | source)
XLA Modules:
  0.0 652.3 jit_solution(7434232229372759890)
XLA Ops:
  7.9 6.2 copy.12
  14.2 3.4 reduce_max.9
  17.6 4.7 fusion.1
  22.3 1.5 copy-done
  23.8 3.9 fusion.23
  28.4 0.8 fusion.5
  29.9 99.2 %all-gather.2.cloned.1.call-done = f32[11264,512]{1,0:T(8,128)} async-done(((f32[1408,512]{1,0:T(8,128)}), f32[11264,512]{1,0:T(8,128)}) %all-gather.2.cloned.1.call-update) | async-done | bytes 23068688 | tf_op jit(solution)/shard_map/all_gather | solution.py:25
  129.1 16.5 %multiply_reduce_fusion.2 = (f32[128]{0:T(128)S(1)}, f32[128]{0:T(128)S(1)}, f32[128]{0:T(128)S(1)}, f32[128,512]{1,0:T(8,128)S(1)}) fusion(f32[128,512]{1,0:T(8,128)S(1)} %copy-done.2, f32[11264,128]{0,1:T(8,128)} %get-tuple-element.26, f32[11264,512]{1,0:T(8,128)} %all-gather.2.cloned.1.call-done), kind=kOutput, calls=%fused_computation.13 | convolution fusion | flops 8858763264 | bytes 29361664 | tf_op jit(solution)/shard_map/dot_general | solution.py:23
  146.4 0.8 fusion.9
  147.2 11.7 %all-reduce.1 = (f32[128]{0:T(128)S(1)}, f32[128]{0:T(128)S(1)}, f32[128]{0:T(128)S(1)}) all-reduce(f32[128]{0:T(128)S(1)} %get-tuple-element.13, f32[128]{0:T(128)S(1)} %get-tuple-element.14, f32[128]{0:T(128)S(1)} %get-tuple-element.12), channel_id=1, replica_groups=mesh['blk'=8,'gene'=4] {'gene'}, use_global_device_ids=true, to_apply=%region_8.0 | all-reduce | flops 384 | bytes 3072 | tf_op jit(solution)/shard_map/psum | solution.py:38
  161.5 45.8 %all-reduce.7.cloned.1.call-done = (f32[4,512]{1,0:T(4,128)}, f32[4,512]{1,0:T(4,128)}, f32[4,512]{1,0:T(4,128)}, f32[11264]{0:T(1024)}) async-done(((f32[4,512]{1,0:T(4,128)}, f32[4,512]{1,0:T(4,128)}, f32[4,512]{1,0:T(4,128)}, f32[11264]{0:T(1024)}), (f32[4,512]{1,0:T(4,128)}, f32[4,512]{1,0:T(4,128)}, f32[4,512]{1,0:T(4,128)}, f32[11264]{0:T(1024)})) %all-reduce.7.cloned.1.call-update) | async-done | bytes 69648 | tf_op jit(solution)/shard_map/psum | solution.py:37
  207.2 1.4 convert_reduce_fusion
  210.0 40.5 %psum.69 = f32[5]{0:T(128)S(1)} all-reduce(f32[5]{0:T(128)S(1)} %stack.23), channel_id=1, replica_groups=mesh['blk'=8,'gene'=4] {'blk','gene'}, use_global_device_ids=true, to_apply=%region_16.0 | all-reduce | flops 5 | bytes 40 | tf_op jit(solution)/shard_map/psum | solution.py:62
  251.2 1.7 fusion.3
  252.9 1.7 fusion.4
  254.6 29.2 %convolution_bitcast_fusion = f32[11264,128]{0,1:T(8,128)} fusion(f32[128,512]{1,0:T(8,128)S(1)} %fusion.4, f32[11264,512]{1,0:T(8,128)} %all-gather.2.cloned.1.call-done), kind=kOutput, calls=%fused_computation | convolution fusion | flops 8858370048 | bytes 29097984 | tf_op jit(solution)/shard_map/dot_general | solution.py:78
  284.1 22.7 %fusion.26 = f32[11264,512]{1,0:T(8,128)} fusion(f32[11264,128]{0,1:T(8,128)} %get-tuple-element.26, f32[128,512]{1,0:T(8,128)S(1)} %fusion.4), kind=kOutput, calls=%fused_computation.48 | convolution fusion | flops 8858370048 | bytes 29097984 | tf_op jit(solution)/shard_map/dot_general | solution.py:88
  311.6 1.2 divide_multiply_fusion
  313.5 176.3 %all-reduce.5.cloned.1.call-done = f32[11264,128]{0,1:T(8,128)} async-done(((f32[11264,128]{0,1:T(8,128)}), f32[11264,128]{0,1:T(8,128)}) %all-reduce.5.cloned.1.call-update) | async-done | bytes 5767184 | tf_op jit(solution)/shard_map/psum | solution.py:95
  489.8 5.2 multiply_reduce_fusion
  495.8 7.4 %multiply_multiply_fusion = f32[11264,128]{0,1:T(8,128)} fusion(f32[11264,128]{0,1:T(8,128)} %get-tuple-element.26, f32[11264,128]{0,1:T(8,128)S(1)} %copy-done.1, f32[128]{0:T(128)S(1)} %multiply_reduce_fusion, f32[11264]{0:T(1024)S(1)} %get-tuple-element.27), kind=kLoop, calls=%fused_computation.1 | loop fusion | flops 5767168 | bytes 17347072 | tf_op jit(solution)/shard_map/mul | solution.py:97
  503.2 7.1 %copy.13 = f32[11264,128]{1,0:T(8,128)} copy(f32[11264,128]{0,1:T(8,128)} %multiply_multiply_fusion) | data formatting | bytes 11534336
  510.3 128.3 %reduce-scatter.2.cloned.1.call-done = f32[1408,512]{1,0:T(8,128)} async-done(((f32[11264,512]{1,0:T(8,128)}), f32[1408,512]{1,0:T(8,128)}) %reduce-scatter.2.cloned.1.call-update) | async-done | bytes 2883600 | tf_op jit(solution)/shard_map/reduce_scatter | solution.py:87
  638.6 3.7 broadcast_multiply_fusion
  (30 shorter events, 6.6 us)
Async XLA Ops:
  7.2 121.9 %all-gather.2.cloned.1.call-start = ((), (), s32[]{:S(2)}) async-start(), calls=%async_computation.1 | async-start | bytes 25952256 | tf_op jit(solution)/shard_map/all_gather | solution.py:25
  7.9 199.3 %all-reduce.7.cloned.1.call-start = ((), (), s32[]{:S(2)}) async-start(), calls=%async_computation.4 | async-start | bytes 139264 | tf_op jit(solution)/shard_map/psum | solution.py:37
  17.6 6.2 copy-start
  23.8 4.6 copy-start.2
  23.8 4.6 copy-start.7
  129.1 78.2 %copy-start.4 = (s32[4,512]{1,0:T(4,128)S(1)}, s32[4,512]{1,0:T(4,128)}, u32[]{:S(2)}) copy-start(s32[4,512]{1,0:T(4,128)} %param.11) | copy-start | bytes 24580
  129.1 78.2 %copy-start.6 = (s32[512]{0:T(512)S(1)}, s32[512]{0:T(512)}, u32[]{:S(2)}) copy-start(s32[512]{0:T(512)} %param.12) | copy-start | bytes 6148
  159.5 330.3 %all-reduce.5.cloned.1.call-start = ((), (), s32[]{:S(2)}) async-start(), calls=%async_computation.2 | async-start | bytes 11534336 | tf_op jit(solution)/shard_map/psum | solution.py:95
  283.9 354.8 %reduce-scatter.2.cloned.1.call-start = ((), (), s32[]{:S(2)}) async-start(), calls=%async_computation.3 | async-start | bytes 25952256 | tf_op jit(solution)/shard_map/reduce_scatter | solution.py:87
  306.8 0.8 copy-start.3
  306.8 4.8 copy-start.5
  489.8 6.0 copy-start.1
Sparse Core Ops, SparseCore 0:
  9.9 119.1 all-gather.1
  159.6 47.5 all-reduce.6
  284.0 205.7 all-reduce.4
  493.7 144.8 reduce-scatter.1
where the time goes:
time: 653 us; the launch traced here: 652 us
  waiting for transfers between devices  450 us (69%)
  matrix products  74.2 us (11%)
  blocking collectives  52.2 us (8%)
  other arithmetic  33.5 us (5%)
  between operations  24.5 us (4%)
  local copies, waits for them, and re-layouts  17.1 us (3%)
    psum x1, waiting for transfers between devices, shards(): dmap = lax.psum(dmap_part, 'gene')  176 us
    reduce_scatter x1, waiting for transfers between devices, shards(): lax.psum_scatter(jnp.dot(rows, dpred, precision=HIGH, preferred_element_t...  128 us
    all_gather x1, waiting for transfers between devices, shards(): lax.all_gather(expression, 'blk', axis=0, tiled=True)  99.2 us
    psum x1, waiting for transfers between devices, shards(): lax.psum((part_a, part_b, part_c, part_q), 'blk')  45.8 us
    psum x1, blocking collectives, shards(): totals = lax.psum(partials, ('blk', 'gene'))  40.5 us
    dot_general x1, matrix products, shards(): lax.dot_general(lax.all_gather(expression, 'blk', axis=0, tiled=True), dp...  29.2 us
    dot_general x1, matrix products, shards(): jnp.dot(rows, dpred, precision=HIGH, preferred_element_type=jnp.float32)  22.7 us
    dot_general x1, matrix products, shards(): lax.dot_general(rows, lax.all_gather(expression, 'blk', axis=0, tiled=Tru...  16.5 us
  transfers between devices with their start and end apart: 4, of which 4 were waited for; matrix products, arithmetic and copies ran while one was open for 10% of the time, Pallas kernels for 0%

commit v1 on v0

v1 whole, which is shorter than its diff:
```python
import functools

import jax
import jax.numpy as jnp
from jax import lax
from jax.experimental import pallas as pl
from jax.experimental.pallas import tpu as pltpu
from jax.sharding import PartitionSpec as P

GENES = 2048
SLIDES = 4
LANES = 128
F32 = jnp.float32
BF16 = jnp.bfloat16
PAIR = [(0, 1), (1, 0), (2, 3), (3, 2)]
MIDDLE = [(1, 2), (2, 1)]
LIMIT = pltpu.CompilerParams(vmem_limit_bytes=40 * 1024 * 1024)


class Order:
    def __init__(self):
        self.last = None

    def __call__(self, step, *inputs, wait=()):
        if self.last is not None or wait:
            gate = [x for x in (self.last, *wait) if x is not None]
            inputs = lax.optimization_barrier((*inputs, *gate))[: len(inputs)]
        out = step(*inputs)
        self.last = out[0] if isinstance(out, (tuple, list)) else out
        return out


def split(x):
    high = x.astype(BF16)
    return high, (x - high.astype(F32)).astype(BF16)


def three(a, b, dims):
    def dot(u, v):
        return lax.dot_general(u, v, (dims, ((), ())), preferred_element_type=F32)

    return dot(a[0], b[0]) + (dot(a[0], b[1]) + dot(a[1], b[0]))


def exact(a, b, dims):
    return lax.dot_general(a, b, (dims, ((), ())), precision=lax.Precision.HIGHEST, preferred_element_type=F32)


def cost(flops, size):
    return pl.CostEstimate(flops=int(flops), bytes_accessed=int(size), transcendentals=0)


def pred_kernel(at_ref, l_ref, x_ref, acc_ref, o_ref):
    @pl.when(pl.program_id(0) == 0)
    def _():
        o_ref[...] = acc_ref[...]

    o_ref[...] += three(split(jnp.exp(l_ref[...])), split(x_ref[...]), ((0,), (0,)))


def pred_part(at, l, x, acc, step):
    count, width = l.shape
    genes = x.shape[1]
    return pl.pallas_call(
        pred_kernel,
        grid_spec=pltpu.PrefetchScalarGridSpec(
            num_scalar_prefetch=1,
            grid=(count // step,),
            in_specs=[
                pl.BlockSpec((step, width), lambda i, at: (i, 0)),
                pl.BlockSpec((step, genes), lambda i, at: (at[0] + i, 0)),
                pl.BlockSpec((width, genes), lambda i, at: (0, 0)),
            ],
            out_specs=pl.BlockSpec((width, genes), lambda i, at: (0, 0)),
        ),
        out_shape=jax.ShapeDtypeStruct((width, genes), F32),
        compiler_params=LIMIT,
        cost_estimate=cost(6 * count * width * genes, 4 * count * (width + genes)),
    )(at, l, x, acc)


def column_of(row):
    return jnp.transpose(jnp.broadcast_to(row, (LANES, row.shape[1])))


def sums_kernel(n_parts, *refs):
    parts, (inv_ref, spatial_ref, ids_ref, weights_ref, pred_ref, slide_ref, spot_ref) = refs[:n_parts], refs[n_parts:]
    pred = parts[0][...]
    for part in parts[1:]:
        pred = pred + part[...]
    spatial = spatial_ref[...]
    genes = pred.shape[1]
    pred = pred * jnp.concatenate([column_of(inv_ref[...])] * (genes // LANES), axis=1)
    pred_ref[...] = pred
    onehot = (lax.broadcasted_iota(jnp.int32, (8, LANES), 0) == ids_ref[...]).astype(F32)
    ones = jnp.ones((8, genes), F32)
    rows = lax.broadcasted_iota(jnp.int32, (8, LANES), 0)
    spot = jnp.where(rows == 3, jnp.sum(weights_ref[...]), 0.0)
    for k, product in enumerate((pred * spatial, pred * pred, spatial * spatial)):
        slide_ref[8 * k : 8 * k + 8, :] = exact(onehot, product, ((1,), (0,)))
        spot = jnp.where(rows == k, exact(ones, product, ((1,), (1,))), spot)
    spot_ref[...] = spot


def pred_sums(parts, inv, spatial, ids, weights):
    width, genes = spatial.shape
    return pl.pallas_call(
        functools.partial(sums_kernel, len(parts)),
        out_shape=(
            jax.ShapeDtypeStruct((width, genes), F32),
            jax.ShapeDtypeStruct((24, genes), F32),
            jax.ShapeDtypeStruct((8, width), F32),
        ),
        compiler_params=LIMIT,
        cost_estimate=cost(10 * width * genes * 48, 4 * width * genes * 6),
    )(*parts, inv, spatial, ids, weights)


def dpred_kernel(spots, slide_ref, spot_ref, pred_ref, spatial_ref, ids_ref, weights_ref, inv_ref, d_ref, own_ref, tot_ref):
    genes = pred_ref.shape[1]
    a, b, c = (slide_ref[8 * k : 8 * k + 8, :] for k in range(3))
    e, f, h, wsum = (spot_ref[k : k + 1, :] for k in range(4))
    wsum = jnp.max(wsum)
    gain = weights_ref[...] / wsum
    inv_g = lax.rsqrt(b * c + 1e-06)
    inv_s = lax.rsqrt(f * h + 1e-06)
    grad_a = -gain * inv_g
    grad_b = gain * a * c * inv_g * inv_g * inv_g
    onehot = (lax.broadcasted_iota(jnp.int32, (8, LANES), 0) == ids_ref[...]).astype(F32)
    wide = functools.partial(jnp.concatenate, axis=1)
    by_spatial = exact(onehot, grad_a, ((0,), (0,))) - wide([column_of(inv_s / spots)] * (genes // LANES))
    by_pred = exact(onehot, grad_b, ((0,), (0,))) + wide(
        [column_of(e * h * inv_s * inv_s * inv_s / spots)] * (genes // LANES)
    )
    pred = pred_ref[...]
    dpred = by_spatial * spatial_ref[...] + by_pred * pred
    inv = inv_ref[...]
    d_ref[...] = dpred * wide([column_of(inv)] * (genes // LANES))
    own_ref[...] = exact(jnp.ones((8, genes), F32), pred * dpred, ((1,), (1,))) * inv
    rows = lax.broadcasted_iota(jnp.int32, (8, LANES), 0)
    tot = jnp.where(rows == 0, jnp.sum(weights_ref[...] * a * inv_g), 0.0)
    tot = jnp.where(rows == 1, jnp.sum(e * inv_s), tot)
    tot_ref[...] = jnp.where(rows == 2, jnp.sum(f), tot)


def dpred_scaled(spots, slide, spot, pred, spatial, ids, weights, inv):
    width, genes = spatial.shape
    return pl.pallas_call(
        functools.partial(dpred_kernel, spots),
        out_shape=(
            jax.ShapeDtypeStruct((width, genes), F32),
            jax.ShapeDtypeStruct((8, width), F32),
            jax.ShapeDtypeStruct((8, width), F32),
        ),
        compiler_params=LIMIT,
        cost_estimate=cost(10 * width * genes * 48, 4 * width * genes * 6),
    )(slide, spot, pred, spatial, ids, weights, inv)


def dmap_kernel(x_ref, d_ref, o_ref):
    o_ref[...] = three(split(x_ref[...]), split(d_ref[...]), ((1,), (1,)))


def dmap_block(x, d, step):
    count, genes = x.shape
    width = d.shape[0]
    return pl.pallas_call(
        dmap_kernel,
        grid=(count // step,),
        in_specs=[
            pl.BlockSpec((step, genes), lambda i: (i, 0)),
            pl.BlockSpec((width, genes), lambda i: (0, 0)),
        ],
        out_specs=pl.BlockSpec((step, width), lambda i: (i, 0)),
        out_shape=jax.ShapeDtypeStruct((count, width), F32),
        compiler_params=LIMIT,
        cost_estimate=cost(6 * count * width * genes, 4 * count * (width + genes)),
    )(x, d)


def egrad_kernel(scale, kinds, plane_ref, *refs):
    n = len(kinds)
    ls, ds, (o_ref, dh_ref, dl_ref) = refs[: sum(kinds)], refs[sum(kinds) : sum(kinds) + n], refs[sum(kinds) + n :]

    @pl.when(pl.program_id(0) == 0)
    def _():
        for k, d in enumerate(ds):
            dh_ref[k * LANES : (k + 1) * LANES, :], dl_ref[k * LANES : (k + 1) * LANES, :] = split(d[...])

    blocks, at = [], 0
    for kind in kinds:
        l = ls[at][...]
        if kind == 2:
            l = jnp.where(plane_ref[0] == pl.program_id(0), l, ls[at + 1][...])
        at += kind
        blocks.append(jnp.exp(l))
    e = split(jnp.concatenate(blocks, axis=1))
    o_ref[...] = three(e, (dh_ref[...], dl_ref[...]), ((1,), (0,))) * scale


def egrad_part(plane, held, grads, rows, scale):
    half = rows // 2
    width, genes = grads[0].shape
    flat, specs, kinds = [], [], []
    for pieces in held:
        kinds.append(len(pieces))
        for piece in pieces:
            flat.append(piece)
            whole = len(pieces) == 1
            specs.append(pl.BlockSpec((half, width), (lambda i, p: (i, 0)) if whole else (lambda i, p: (0, 0))))
    specs += [pl.BlockSpec((width, genes), lambda i, p: (0, 0))] * len(grads)
    deep = width * len(grads)
    return pl.pallas_call(
        functools.partial(egrad_kernel, scale, tuple(kinds)),
        grid_spec=pltpu.PrefetchScalarGridSpec(
            num_scalar_prefetch=1,
            grid=(2,),
            in_specs=specs,
            out_specs=pl.BlockSpec((half, genes), lambda i, p: (i, 0)),
            scratch_shapes=[pltpu.VMEM((deep, genes), BF16), pltpu.VMEM((deep, genes), BF16)],
        ),
        out_shape=jax.ShapeDtypeStruct((rows, genes), F32),
        compiler_params=LIMIT,
        cost_estimate=cost(6 * rows * deep * genes, 4 * rows * (deep + genes)),
    )(plane, *flat, *grads)


def ratio_kernel(l_ref, ratio_ref, inv_ref, o_ref, sum_ref):
    @pl.when(pl.program_id(0) == 0)
    def _():
        sum_ref[...] = jnp.zeros_like(sum_ref)

    first = (lax.broadcasted_iota(jnp.int32, (8, LANES), 0) == 0).astype(F32)
    ratio = jnp.broadcast_to(ratio_ref[0], (8, ratio_ref.shape[2]))
    column = exact(ratio, first, ((0,), (0,)))
    inv = inv_ref[...]
    o_ref[...] = column * inv
    sum_ref[...] += jnp.sum(jnp.exp(l_ref[...]) * column, axis=0, keepdims=True) * (inv * inv)


def ratio_part(logits, ratio, inv, step):
    cells, width = logits.shape
    steps = cells // step
    return pl.pallas_call(
        ratio_kernel,
        grid=(steps,),
        in_specs=[
            pl.BlockSpec((step, width), lambda i: (i, 0)),
            pl.BlockSpec((1, 1, step), lambda i: (i, 0, 0)),
            pl.BlockSpec((1, width), lambda i: (0, 0)),
        ],
        out_specs=(
            pl.BlockSpec((step, width), lambda i: (i, 0)),
            pl.BlockSpec((8, width), lambda i: (0, 0)),
        ),
        out_shape=(
            jax.ShapeDtypeStruct((cells, width), F32),
            jax.ShapeDtypeStruct((8, width), F32),
        ),
        compiler_params=LIMIT,
        cost_estimate=cost(cells * width * 100, 8 * cells * width),
    )(logits, ratio.reshape(steps, 1, step), inv)


def shards(logits, expression, spatial, density, gene_mask, gene_counts, slide_ids):
    n_blk = lax.axis_size("blk")
    n_gene = lax.axis_size("gene")
    me = lax.axis_index("blk")
    plane = lax.axis_index("gene")
    cells, width = logits.shape
    rows, genes = expression.shape
    half = rows // 2
    spots = width * n_blk
    order = Order()

    def swap(x, m):
        return lax.ppermute(x, "blk", [(i, i ^ m) for i in range(n_blk)])

    def across(x, m):
        return lax.ppermute(x, "gene", [(i, i ^ m) for i in range(n_gene)])

    def cut(r, first, size):
        return lax.dynamic_slice_in_dim(logits, (me ^ r) * rows + first, size, 0)

    far = sorted(range(2, n_blk, 2), key=lambda m: (m.bit_count(), m))
    helped = (3, 5, 6, 7) if n_blk == 8 and n_gene == 4 else ()
    side = plane % 2
    zero = jnp.zeros((1,), jnp.int32)
    shift = jnp.reshape(side, (1,)).astype(jnp.int32)

    other = swap(expression, 1)
    sent, held = {}, {}
    for r in helped:
        sent[r] = swap(cut(r, side * half, half), r & ~1)
    for r in range(2, n_blk):
        if r not in helped:
            held[r] = swap(cut(r, 0, rows), r & ~1)
    held[0], held[1] = cut(0, 0, rows), cut(1, 0, rows)

    total = order(lambda l: jnp.sum(jnp.exp(l), axis=0), logits)
    inv = (1.0 / total)[None, :]
    weights = (gene_mask * gene_counts[None, :]).astype(F32)
    weights = jnp.concatenate([weights, jnp.zeros((8 - SLIDES, genes), F32)], axis=0)
    ids = slide_ids[None, :]
    acc = {}
    none = jnp.zeros((width, genes), F32)

    def add_pred(r, l, at=zero):
        x = expression if r % 2 == 0 else other
        acc[r & ~1] = order(
            lambda l, x, s: pred_part(at, l, x, s, min(half, l.shape[0])), l, x, acc.get(r & ~1, none)
        )

    add_pred(0, held[0])
    passed = {}
    for r in helped[:2]:
        passed[r] = across(sent[r], 1)
    for r in helped[:2]:
        add_pred(r, sent[r], shift)

    def statistics(l, inv):
        share = jnp.exp(l) * inv
        part = jnp.sum(share, axis=1) / spots
        return part, jnp.sum(share * share)

    part_q, square = order(statistics, logits, inv)
    add_pred(1, held[1])
    for r in helped[2:]:
        passed[r] = across(sent[r], 1)
    for r in helped[2:]:
        add_pred(r, sent[r], shift)
    for r in helped[:2]:
        add_pred(r, passed[r], 1 - shift)
    for r in range(n_blk - 1, 1, -1):
        if r in held:
            add_pred(r, held[r])
    for r in helped[2:]:
        add_pred(r, passed[r], 1 - shift)

    parts = [acc[0]] + [swap(acc[m], m) for m in far]
    pred, slide, spot = order(
        lambda *a: pred_sums(a[:-4], *a[-4:]), *parts, inv, spatial, ids, weights
    )
    spot = spot + (across(spot, 1) + (across(spot, 2) + across(spot, 3)))
    wide = jnp.concatenate(
        [slide.reshape(-1, LANES), part_q.reshape(-1, LANES), jnp.full((8, LANES), square)], axis=0
    )
    m = 1
    while m < n_blk:
        wide = wide + swap(wide, m)
        m *= 2
    n_slide = 24 * genes // LANES
    slide = wide[:n_slide].reshape(24, genes)
    cell_q = wide[n_slide : n_slide + cells // LANES].reshape(cells)
    square = wide[-1, 0]
    grad, own, tot = order(
        functools.partial(dpred_scaled, spots), slide, spot, pred, spatial, ids, weights, inv
    )
    own = own[:1]

    grads = {0: grad}
    for m in far:
        grads[m] = swap(grad, m)
    back = {}

    def dmap(r):
        x = expression if r % 2 == 0 else other
        d = order(lambda x, d: dmap_block(x, d, half), x, grads[r & ~1])
        back[r] = d if r < 2 else swap(d, r & ~1)

    dmap(0)
    dmap(1)
    target = density / jnp.sum(density)
    ratio = target / cell_q / spots
    kl_term = jnp.sum(target * (jnp.log(target) - jnp.log(cell_q)))

    near = [0, 1] + [r for m in far for r in (m, m + 1)]
    if n_blk == 8:
        near = [0, 1, 2, 4, 3, 5, 6, 7]
    pieces = [(r, k * half) for r in near for k in range(2)]
    count, lag = len(pieces), 3
    mine, part, total_of, mid, got = {}, {}, {}, {}, {}
    is_end = (plane == 0) | (plane == n_gene - 1)
    state = {"grad": jnp.zeros((cells, width), F32)}

    def own_piece(t):
        r, first = pieces[t]
        return back[r][first : first + half]

    def send(t):
        if t >= count + lag:
            return
        if t >= lag:
            total_of[t - lag] = order(lambda s, y: s + y, part[t - lag], mid[t - lag])
        if t < lag:
            mine[t] = order(lambda b, o: b - o, own_piece(t), own)
            buffer = mine[t]
        elif t < count:
            mine[t], buffer = order(
                lambda b, o, s: (b - o, jnp.where(is_end, b - o, s)), own_piece(t), own, total_of[t - lag]
            )
        else:
            buffer = total_of[t - lag]
        got[t] = lax.ppermute(buffer, "gene", PAIR)

    def finish(t):
        r, first = pieces[t]
        at = (me ^ r) * rows + first
        l = lax.dynamic_slice_in_dim(logits, at, half, 0)
        w = lax.dynamic_slice_in_dim(state["ratio"], at, half, 0)

        def last(rx, s, l, w, rs, g):
            value = jnp.exp(l) * (jnp.where(is_end, rx, s) - w + rs) * cells
            return lax.dynamic_update_slice_in_dim(g, value, at, 0)

        state["grad"] = order(last, got[t + lag], total_of[t], l, w, state["ratio_sum"], state["grad"])

    def extra(t):
        if t == 0:
            state["ratio"], ratio_sum = order(
                lambda l, q, i: ratio_part(l, q, i, rows), logits, ratio, inv
            )
            state["ratio_sum"] = ratio_sum[:1]
        if t == 1:
            for r in near[2:4]:
                dmap(r)
        if t == 2:
            for r in near[4:6]:
                dmap(r)
        if t == 4:
            for r in near[6:]:
                dmap(r)
        if t == 6:
            pick = lambda r: (sent[r], passed[r]) if r in helped else (held[r],)
            ms = [0] + far
            gs = [grads[m] for m in ms]
            for odd in (1, 0):
                flat = [p for m in ms for p in pick(m + odd)]
                kinds = [len(pick(m + odd)) for m in ms]

                def part_of(*a):
                    ls, out = list(a[: len(flat)]), []
                    for k in kinds:
                        out.append(tuple(ls[:k]))
                        ls = ls[k:]
                    return egrad_part(shift, out, a[len(flat) :], rows, cells)

                state[odd] = order(part_of, *flat, *gs)
                if odd:
                    state["swapped"] = swap(state[1], 1)
        if t == 8:
            state["expr"] = order(lambda a, b: a + b, state[0], state["swapped"])
        if t == 10:
            x = tot * jnp.array([1.0 / n_blk, 1.0 / n_gene, 1.0 / n_gene, 0, 0, 0, 0, 0], F32)[:, None]
            x = x + across(x, 1)
            state["tot"] = x + across(x, 2)
        if t == 12:
            x = state["tot"]
            m = 1
            while m < n_blk:
                x = x + swap(x, m)
                m *= 2
            state["tot"] = x

    send(0)
    for t in range(count + lag):
        extra(t)
        send(t + 1)
        if t < count:
            part[t] = order(lambda a, b: a + b, mine[t], got[t])
            mid[t] = lax.ppermute(part[t], "gene", MIDDLE)
        if t >= lag:
            finish(t - lag)

    tot = state["tot"]
    loss = -tot[0, 0] / spot[3, 0] - tot[1, 0] / spots + kl_term
    rms_map = jnp.sqrt(square / (cells * spots))
    rms_pred = jnp.sqrt(tot[2, 0] / (spots * GENES))
    return (loss, state["grad"], state["expr"], rms_map, rms_pred)


def solution(mesh):
    placed = (
        P(None, "blk"),
        P("blk", "gene"),
        P("blk", "gene"),
        P(),
        P(None, "gene"),
        P("gene"),
        P("blk"),
    )
    return jax.shard_map(
        shards,
        mesh=mesh,
        in_specs=placed,
        out_specs=(P(), P(None, "blk"), P("blk", "gene"), P(), P()),
        check_vma=False,
    )
```

time: 653 us -> 361 us (0.55)
  waiting for transfers between devices: 450 us -> 128 us
  starting transfers between devices: 0.38 us -> 117 us
  matrix products: 74.2 us -> 0 us
  blocking collectives: 52.2 us -> 0 us
  Pallas kernels: 0 us -> 37.7 us
  local copies, waits for them, and re-layouts: 17.1 us -> 34.4 us
  between operations: 24.5 us -> 9.24 us
    psum x2 -> x0, waiting for transfers between devices: 222 us -> none  [the longest x1 176 us: shards(): dmap = lax.psum(dmap_part, 'gene')]
    reduce_scatter x1 -> x0, waiting for transfers between devices: 128 us -> none  [shards(): lax.psum_scatter(jnp.dot(rows, dpred, precision=HIGH, preferred_element_t...]
    ppermute x0 -> x70, waiting for transfers between devices: none -> 128 us  [the longest x26 63.8 us: swap(): return lax.ppermute(x, 'blk', [(i, i ^ m) for i in range(n_blk)])]
    ppermute x0 -> x70, starting transfers between devices: none -> 117 us  [the longest x19 60.6 us: send(): got[t] = lax.ppermute(buffer, 'gene', PAIR)]
    all_gather x1 -> x0, waiting for transfers between devices: 99.2 us -> none  [shards(): lax.all_gather(expression, 'blk', axis=0, tiled=True)]
    dot_general x8 -> x0, matrix products: 74.2 us -> none  [the longest x1 29.2 us: shards(): lax.dot_general(lax.all_gather(expression, 'blk', axis=0, tiled=True), dp...]
    psum x2 -> x0, blocking collectives: 52.2 us -> none  [the longest x1 40.5 us: shards(): totals = lax.psum(partials, ('blk', 'gene'))]
    pallas_call x0 -> x25, Pallas kernels: none -> 37.7 us  [the longest x8 12.1 us: dmap_block(): pl.pallas_call(dmap_kernel, grid=(count // step,), in_specs=[pl.BlockSpec...]
  transfers between devices with their start and end apart: 4 -> 70, of which waited for: 4 -> 29; matrix products, arithmetic and copies ran while one was open for 10% -> 14% of each run, Pallas kernels for 0% -> 10%
where the time goes in v1:
time: 361 us; the launch traced here: 359 us
  waiting for transfers between devices  128 us (35%)
  starting transfers between devices  117 us (32%)
  Pallas kernels  37.7 us (10%)
  local copies, waits for them, and re-layouts  34.4 us (10%)
  other arithmetic  33.5 us (9%)
  between operations  9.24 us (3%)
    ppermute x26, waiting for transfers between devices, swap(): return lax.ppermute(x, 'blk', [(i, i ^ m) for i in range(n_blk)])  63.8 us
    ppermute x19, starting transfers between devices, send(): got[t] = lax.ppermute(buffer, 'gene', PAIR)  60.6 us
    ppermute x19, waiting for transfers between devices, send(): got[t] = lax.ppermute(buffer, 'gene', PAIR)  41.4 us
    ppermute x26, starting transfers between devices, swap(): return lax.ppermute(x, 'blk', [(i, i ^ m) for i in range(n_blk)])  30.4 us
    ppermute x9, waiting for transfers between devices, across(): return lax.ppermute(x, 'gene', [(i, i ^ m) for i in range(n_gene)])  22.6 us
    ppermute x9, starting transfers between devices, across(): return lax.ppermute(x, 'gene', [(i, i ^ m) for i in range(n_gene)])  13.7 us
    dynamic_update_slice x16, other arithmetic, last(): return lax.dynamic_update_slice_in_dim(g, value, at, 0)  13.6 us
    pallas_call x8, Pallas kernels, dmap_block(): pl.pallas_call(dmap_kernel, grid=(count // step,), in_specs=[pl.BlockSpec...  12.1 us
  transfers between devices with their start and end apart: 70, of which 29 were waited for; matrix products, arithmetic and copies ran while one was open for 14% of the time, Pallas kernels for 10%

profile of v1, /device:TPU:0, one launch (start us, length us, event | category | flops | bytes accessed | tf_op | source)
XLA Modules:
  0.0 359.3 jit_solution(6315371656098148446)
XLA Ops:
  1.1 5.6 %constant_dynamic-slice_fusion.1 = (f32[704,128]{1,0:T(8,128)}, f32[704,128]{1,0:T(8,128)}, f32[704,128]{1,0:T(8,128)}, f32[704,128]{1,0:T(8,128)}, f32[704,128]...) fusion(f32[11264,128]{1,0:T(8,128)} %l_ref, ...), kind=kLoop, calls=%fused_computation.57 | loop fusion | bytes 12976200 | tf_op jit(solution)/shard_map/dynamic_slice | solution.py:409
  29.7 6.2 %collective-permute-done.2.l_ref.refs_1_ = f32[704,128]{1,0:T(8,128)S(1)} collective-permute-done((f32[704,128]{1,0:T(8,128)S(1)}, f32[704,128]{1,0:T(8,128)S(1)}, u32[]{:S(2)}, u32[]{:S(2)}) %collective-permute-start.2) | collective-permute-done | bytes 360480 | tf_op jit(solution)/shard_map/ppermute | solution.py:277
  38.0 9.2 %collective-permute-done.3.l_ref.refs_2_ = f32[704,128]{1,0:T(8,128)S(1)} collective-permute-done((f32[704,128]{1,0:T(8,128)S(1)}, f32[704,128]{1,0:T(8,128)S(1)}, u32[]{:S(2)}, u32[]{:S(2)}) %collective-permute-start.3) | collective-permute-done | bytes 360480 | tf_op jit(solution)/shard_map/ppermute | solution.py:280
  63.3 5.0 %collective-permute-done.11.l_ref.refs_6_ = f32[704,128]{1,0:T(8,128)S(1)} collective-permute-done((f32[704,128]{1,0:T(8,128)}, f32[704,128]{1,0:T(8,128)S(1)}, u32[]{:S(2)}, u32[]{:S(2)}) %collective-permute-start.11) | collective-permute-done | bytes 360480 | tf_op jit(solution)/shard_map/ppermute | solution.py:280
  114.5 6.6 %shard_map.135 = (f32[11264,128]{1,0:T(8,128)S(1)}, f32[8,128]{1,0:T(8,128)S(1)}) custom-call(f32[11264,128]{1,0:T(8,128)S(1)} %copy-done.3, f32[8,1,1408]{2,1,0:T(1,128)S(1)} %bitcast.55, f32[1,128]{1,0:T(1,128)S(1)} %copy-done.32), custom_call_target="tpu_custom_call" | custom-call | flops 144179200 | bytes 11534336 | tf_op jit(solution)/shard_map/pallas_call | solution.py:244
  131.0 4.5 %collective-permute-start.34 = (f32[704,128]{1,0:T(8,128)S(1)}, f32[704,128]{1,0:T(8,128)S(1)}, u32[]{:S(2)}, u32[]{:S(2)}) collective-permute-start(f32[704,128]{1,0:T(8,128)S(1)} %broadcast_subtract_fusion.13), channel_id=1, source_target_pairs={{0,1},{1,0},{2,3},{3,2},{4,5},{5,4},{6,7},{7,6},{8,9},{9,8},{10,11... | collective-permute-start | bytes 1081352 | tf_op jit(solution)/shard_map/ppermute | solution.py:404
  145.2 5.2 %collective-permute-start.31 = (f32[704,128]{1,0:T(8,128)S(1)}, f32[704,128]{1,0:T(8,128)S(1)}, u32[]{:S(2)}, u32[]{:S(2)}) collective-permute-start(f32[704,128]{1,0:T(8,128)S(1)} %get-tuple-element.645), channel_id=1, source_target_pairs={{0,1},{1,0},{2,3},{3,2},{4,5},{5,4},{6,7},{7,6},{8,9},{9,8},{10,11... | collective-permute-start | bytes 1081352 | tf_op jit(solution)/shard_map/ppermute | solution.py:404
  150.5 8.4 %collective-permute-done.38 = f32[1408,128]{1,0:T(8,128)S(1)} collective-permute-done((f32[1408,128]{1,0:T(8,128)S(1)}, f32[1408,128]{1,0:T(8,128)S(1)}, u32[]{:S(2)}, u32[]{:S(2)}) %collective-permute-start.38) | collective-permute-done | bytes 720928 | tf_op jit(solution)/shard_map/ppermute | solution.py:277
  178.0 4.0 %shard_map.142 = f32[1408,512]{1,0:T(8,128)S(1)} custom-call(s32[1]{0:T(128)} %bitcast.at_ref.plane_ref, f32[1408,128]{1,0:T(8,128)S(1)} %copy-done.7, f32[704,128]{1,0:T(8,128)S(1)} %copy-done.16, f32[704,128]{1,0:T(8,128)S(1)} %copy-done.20, f32[704,128]{1,0:T(8,128)S(1)} %copy-done.18, f32[704,128]{1,0:T(8,128)S(1)} %copy-done.22, ...), custom_call_target="tpu_custom_call" | custom-call | flops 2214592512 | bytes 5767168 | tf_op jit(solution)/shard_map/pallas_call | solution.py:213
  189.1 27.0 %collective-permute-done.50 = f32[1408,128]{1,0:T(8,128)S(1)} collective-permute-done((f32[1408,128]{1,0:T(8,128)S(1)}, f32[1408,128]{1,0:T(8,128)S(1)}, u32[]{:S(2)}, u32[]{:S(2)}) %collective-permute-start.50) | collective-permute-done | bytes 720928 | tf_op jit(solution)/shard_map/ppermute | solution.py:277
  221.5 4.2 %collective-permute-start.42 = (f32[704,128]{1,0:T(8,128)}, f32[704,128]{1,0:T(8,128)S(1)}, u32[]{:S(2)}, u32[]{:S(2)}) collective-permute-start(f32[704,128]{1,0:T(8,128)} %get-tuple-element.641), channel_id=1, source_target_pairs={{0,1},{1,0},{2,3},{3,2},{4,5},{5,4},{6,7},{7,6},{8,9},{9,8},{10,11... | collective-permute-start | bytes 1081352 | tf_op jit(solution)/shard_map/ppermute | solution.py:404
  225.7 9.2 %collective-permute-done.35 = f32[1408,128]{1,0:T(8,128)} collective-permute-done((f32[1408,128]{1,0:T(8,128)S(1)}, f32[1408,128]{1,0:T(8,128)}, u32[]{:S(2)}, u32[]{:S(2)}) %collective-permute-start.35) | collective-permute-done | bytes 720928 | tf_op jit(solution)/shard_map/ppermute | solution.py:277
  242.2 4.1 %collective-permute-done.47 = f32[704,128]{1,0:T(8,128)S(1)} collective-permute-done((f32[704,128]{1,0:T(8,128)S(1)}, f32[704,128]{1,0:T(8,128)S(1)}, u32[]{:S(2)}, u32[]{:S(2)}) %collective-permute-start.47) | collective-permute-done | bytes 360480 | tf_op jit(solution)/shard_map/ppermute | solution.py:404
  252.9 4.8 %collective-permute-start.49 = (f32[704,128]{1,0:T(8,128)S(1)}, f32[704,128]{1,0:T(8,128)S(1)}, u32[]{:S(2)}, u32[]{:S(2)}) collective-permute-start(f32[704,128]{1,0:T(8,128)S(1)} %get-tuple-element.635), channel_id=1, source_target_pairs={{0,1},{1,0},{2,3},{3,2},{4,5},{5,4},{6,7},{7,6},{8,9},{9,8},{10,11... | collective-permute-start | bytes 1081352 | tf_op jit(solution)/shard_map/ppermute | solution.py:404
  259.2 7.7 %collective-permute-done.49 = f32[704,128]{1,0:T(8,128)S(1)} collective-permute-done((f32[704,128]{1,0:T(8,128)S(1)}, f32[704,128]{1,0:T(8,128)S(1)}, u32[]{:S(2)}, u32[]{:S(2)}) %collective-permute-start.49) | collective-permute-done | bytes 360480 | tf_op jit(solution)/shard_map/ppermute | solution.py:404
  271.5 4.5 %collective-permute-start.58 = (f32[704,128]{1,0:T(8,128)S(1)}, f32[704,128]{1,0:T(8,128)S(1)}, u32[]{:S(2)}, u32[]{:S(2)}) collective-permute-start(f32[704,128]{1,0:T(8,128)S(1)} %get-tuple-element.627), channel_id=1, source_target_pairs={{0,1},{1,0},{2,3},{3,2},{4,5},{5,4},{6,7},{7,6},{8,9},{9,8},{10,11... | collective-permute-start | bytes 1081352 | tf_op jit(solution)/shard_map/ppermute | solution.py:404
  277.0 4.5 %collective-permute-done.58 = f32[704,128]{1,0:T(8,128)S(1)} collective-permute-done((f32[704,128]{1,0:T(8,128)S(1)}, f32[704,128]{1,0:T(8,128)S(1)}, u32[]{:S(2)}, u32[]{:S(2)}) %collective-permute-start.58) | collective-permute-done | bytes 360480 | tf_op jit(solution)/shard_map/ppermute | solution.py:404
  282.4 4.5 %collective-permute-start.56 = (f32[704,128]{1,0:T(8,128)S(1)}, f32[704,128]{1,0:T(8,128)S(1)}, u32[]{:S(2)}, u32[]{:S(2)}) collective-permute-start(f32[704,128]{1,0:T(8,128)S(1)} %get-tuple-element.629), channel_id=1, source_target_pairs={{0,1},{1,0},{2,3},{3,2},{4,5},{5,4},{6,7},{7,6},{8,9},{9,8},{10,11... | collective-permute-start | bytes 1081352 | tf_op jit(solution)/shard_map/ppermute | solution.py:404
  287.9 5.2 %collective-permute-done.56 = f32[704,128]{1,0:T(8,128)S(1)} collective-permute-done((f32[704,128]{1,0:T(8,128)S(1)}, f32[704,128]{1,0:T(8,128)S(1)}, u32[]{:S(2)}, u32[]{:S(2)}) %collective-permute-start.56) | collective-permute-done | bytes 360480 | tf_op jit(solution)/shard_map/ppermute | solution.py:404
  298.7 5.0 %collective-permute-start.64 = (f32[704,128]{1,0:T(8,128)S(1)}, f32[704,128]{1,0:T(8,128)S(1)}, u32[]{:S(2)}, u32[]{:S(2)}) collective-permute-start(f32[704,128]{1,0:T(8,128)S(1)} %get-tuple-element.621), channel_id=1, source_target_pairs={{0,1},{1,0},{2,3},{3,2},{4,5},{5,4},{6,7},{7,6},{8,9},{9,8},{10,11... | collective-permute-start | bytes 1081352 | tf_op jit(solution)/shard_map/ppermute | solution.py:404
  304.7 6.8 %collective-permute-done.64 = f32[704,128]{1,0:T(8,128)S(1)} collective-permute-done((f32[704,128]{1,0:T(8,128)S(1)}, f32[704,128]{1,0:T(8,128)S(1)}, u32[]{:S(2)}, u32[]{:S(2)}) %collective-permute-start.64) | collective-permute-done | bytes 360480 | tf_op jit(solution)/shard_map/ppermute | solution.py:404
  320.4 4.6 %collective-permute-done.21 = f32[8,128]{1,0:T(8,128)S(1)} collective-permute-done((f32[8,128]{1,0:T(8,128)S(1)}, f32[8,128]{1,0:T(8,128)S(1)}, u32[]{:S(2)}, u32[]{:S(2)}) %collective-permute-start.21) | collective-permute-done | bytes 4128 | tf_op jit(solution)/shard_map/ppermute | solution.py:280
  335.0 5.2 %collective-permute-start.69 = (f32[704,128]{1,0:T(8,128)S(1)}, f32[704,128]{1,0:T(8,128)S(1)}, u32[]{:S(2)}, u32[]{:S(2)}) collective-permute-start(f32[704,128]{1,0:T(8,128)S(1)} %add.561), channel_id=1, source_target_pairs={{0,1},{1,0},{2,3},{3,2},{4,5},{5,4},{6,7},{7,6},{8,9},{9,8},{10,11... | collective-permute-start | bytes 1081352 | tf_op jit(solution)/shard_map/ppermute | solution.py:404
  341.2 7.0 %collective-permute-start.68 = (f32[704,128]{1,0:T(8,128)S(1)}, f32[704,128]{1,0:T(8,128)S(1)}, u32[]{:S(2)}, u32[]{:S(2)}) collective-permute-start(f32[704,128]{1,0:T(8,128)S(1)} %add.565), channel_id=1, source_target_pairs={{0,1},{1,0},{2,3},{3,2},{4,5},{5,4},{6,7},{7,6},{8,9},{9,8},{10,11... | collective-permute-start | bytes 1081352 | tf_op jit(solution)/shard_map/ppermute | solution.py:404
  (374 shorter events, 191.3 us)
Async XLA Ops:
  0.6 48.2 %collective-permute-start = (f32[1408,512]{1,0:T(8,128)}, f32[1408,512]{1,0:T(8,128)S(1)}, u32[]{:S(2)}, u32[]{:S(2)}) collective-permute-start(f32[1408,512]{1,0:T(8,128)} %x_ref.8), channel_id=1, source_target_pairs={{0,4},{4,0},{8,12},{12,8},{16,20},{20,16},{24,28},{28,24},{1,5},{5... | collective-permute-start | bytes 8650760 | tf_op jit(solution)/shard_map/ppermute | solution.py:277
  12.4 23.5 %collective-permute-start.2 = (f32[704,128]{1,0:T(8,128)S(1)}, f32[704,128]{1,0:T(8,128)S(1)}, u32[]{:S(2)}, u32[]{:S(2)}) collective-permute-start(f32[704,128]{1,0:T(8,128)S(1)} %get-tuple-element.682), channel_id=1, source_target_pairs={{0,8},{4,12},{8,0},{12,4},{16,24},{20,28},{24,16},{28,20},{1,9},{5... | collective-permute-start | bytes 1081352 | tf_op jit(solution)/shard_map/ppermute | solution.py:277
  14.3 23.2 %collective-permute-start.7 = (f32[704,128]{1,0:T(8,128)}, f32[704,128]{1,0:T(8,128)S(1)}, u32[]{:S(2)}, u32[]{:S(2)}) collective-permute-start(f32[704,128]{1,0:T(8,128)} %get-tuple-element.678), channel_id=1, source_target_pairs={{0,16},{4,20},{8,24},{12,28},{16,0},{20,4},{24,8},{28,12},{1,17},{... | collective-permute-start | bytes 1081352 | tf_op jit(solution)/shard_map/ppermute | solution.py:277
  19.9 36.3 %collective-permute-start.6 = (f32[1408,128]{1,0:T(8,128)S(1)}, f32[1408,128]{1,0:T(8,128)S(1)}, u32[]{:S(2)}, u32[]{:S(2)}) collective-permute-start(f32[1408,128]{1,0:T(8,128)S(1)} %get-tuple-element.683), channel_id=1, source_target_pairs={{0,16},{4,20},{8,24},{12,28},{16,0},{20,4},{24,8},{28,12},{1,17},{... | collective-permute-start | bytes 2162696 | tf_op jit(solution)/shard_map/ppermute | solution.py:277
  27.7 30.6 %collective-permute-start.1 = (f32[1408,128]{1,0:T(8,128)S(1)}, f32[1408,128]{1,0:T(8,128)S(1)}, u32[]{:S(2)}, u32[]{:S(2)}) collective-permute-start(f32[1408,128]{1,0:T(8,128)S(1)} %get-tuple-element.684), channel_id=1, source_target_pairs={{0,8},{4,12},{8,0},{12,4},{16,24},{20,28},{24,16},{28,20},{1,9},{5... | collective-permute-start | bytes 2162696 | tf_op jit(solution)/shard_map/ppermute | solution.py:277
  48.8 19.4 %collective-permute-start.11 = (f32[704,128]{1,0:T(8,128)}, f32[704,128]{1,0:T(8,128)S(1)}, u32[]{:S(2)}, u32[]{:S(2)}) collective-permute-start(f32[704,128]{1,0:T(8,128)} %collective-permute-done.4.l_ref.refs_5_), channel_id=1, source_target_pairs={{0,1},{1,0},{2,3},{3,2},{4,5},{5,4},{6,7},{7,6},{8,9},{9,8},{10,11... | collective-permute-start | bytes 1081352 | tf_op jit(solution)/shard_map/ppermute | solution.py:280
  102.9 21.6 %collective-permute-start.29 = (f32[128,512]{1,0:T(8,128)S(1)}, f32[128,512]{1,0:T(8,128)S(1)}, u32[]{:S(2)}, u32[]{:S(2)}) collective-permute-start(f32[128,512]{1,0:T(8,128)S(1)} %get-tuple-element.464.d_ref.refs_7_.refs_5_), channel_id=1, source_target_pairs={{0,8},{4,12},{8,0},{12,4},{16,24},{20,28},{24,16},{28,20},{1,9},{5... | collective-permute-start | bytes 786440 | tf_op jit(solution)/shard_map/ppermute | solution.py:277
  103.5 25.9 %collective-permute-start.28 = (f32[128,512]{1,0:T(8,128)S(1)}, f32[128,512]{1,0:T(8,128)S(1)}, u32[]{:S(2)}, u32[]{:S(2)}) collective-permute-start(f32[128,512]{1,0:T(8,128)S(1)} %get-tuple-element.464.d_ref.refs_7_.refs_5_), channel_id=1, source_target_pairs={{0,16},{4,20},{8,24},{12,28},{16,0},{20,4},{24,8},{28,12},{1,17},{... | collective-permute-start | bytes 786440 | tf_op jit(solution)/shard_map/ppermute | solution.py:277
  126.1 19.1 %collective-permute-start.32 = (f32[1408,128]{1,0:T(8,128)S(1)}, f32[1408,128]{1,0:T(8,128)S(1)}, u32[]{:S(2)}, u32[]{:S(2)}) collective-permute-start(f32[1408,128]{1,0:T(8,128)S(1)} %shard_map.136), channel_id=1, source_target_pairs={{0,8},{4,12},{8,0},{12,4},{16,24},{20,28},{24,16},{28,20},{1,9},{5... | collective-permute-start | bytes 2162696 | tf_op jit(solution)/shard_map/ppermute | solution.py:277
  127.2 38.0 %collective-permute-start.25 = (f32[128,512]{1,0:T(8,128)S(1)}, f32[128,512]{1,0:T(8,128)S(1)}, u32[]{:S(2)}, u32[]{:S(2)}) collective-permute-start(f32[128,512]{1,0:T(8,128)S(1)} %get-tuple-element.464.d_ref.refs_7_.refs_5_), channel_id=1, source_target_pairs={{0,24},{4,28},{8,16},{12,20},{16,8},{20,12},{24,0},{28,4},{1,25},{... | collective-permute-start | bytes 786440 | tf_op jit(solution)/shard_map/ppermute | solution.py:277
  139.3 19.6 %collective-permute-start.38 = (f32[1408,128]{1,0:T(8,128)S(1)}, f32[1408,128]{1,0:T(8,128)S(1)}, u32[]{:S(2)}, u32[]{:S(2)}) collective-permute-start(f32[1408,128]{1,0:T(8,128)S(1)} %shard_map.137), channel_id=1, source_target_pairs={{0,16},{4,20},{8,24},{12,28},{16,0},{20,4},{24,8},{28,12},{1,17},{... | collective-permute-start | bytes 2162696 | tf_op jit(solution)/shard_map/ppermute | solution.py:277
  140.9 43.9 %collective-permute-start.37 = (f32[1408,128]{1,0:T(8,128)S(1)}, f32[1408,128]{1,0:T(8,128)}, u32[]{:S(2)}, u32[]{:S(2)}) collective-permute-start(f32[1408,128]{1,0:T(8,128)S(1)} %shard_map.138), channel_id=1, source_target_pairs={{0,8},{4,12},{8,0},{12,4},{16,24},{20,28},{24,16},{28,20},{1,9},{5... | collective-permute-start | bytes 2162696 | tf_op jit(solution)/shard_map/ppermute | solution.py:277
  142.5 25.9 %collective-permute-start.41 = (f32[704,128]{1,0:T(8,128)S(1)}, f32[704,128]{1,0:T(8,128)S(1)}, u32[]{:S(2)}, u32[]{:S(2)}) collective-permute-start(f32[704,128]{1,0:T(8,128)S(1)} %add.477), channel_id=1, source_target_pairs={{1,2},{2,1},{5,6},{6,5},{9,10},{10,9},{13,14},{14,13},{17,18},{18,... | collective-permute-start | bytes 1081352 | tf_op jit(solution)/shard_map/ppermute | solution.py:471
  182.0 65.8 %collective-permute-start.46 = (f32[1408,512]{1,0:T(8,128)S(1)}, f32[1408,512]{1,0:T(8,128)S(1)}, u32[]{:S(2)}, u32[]{:S(2)}) collective-permute-start(f32[1408,512]{1,0:T(8,128)S(1)} %shard_map.142), channel_id=1, source_target_pairs={{0,4},{4,0},{8,12},{12,8},{16,20},{20,16},{24,28},{28,24},{1,5},{5... | collective-permute-start | bytes 8650760 | tf_op jit(solution)/shard_map/ppermute | solution.py:277
  182.1 34.0 %collective-permute-start.50 = (f32[1408,128]{1,0:T(8,128)S(1)}, f32[1408,128]{1,0:T(8,128)S(1)}, u32[]{:S(2)}, u32[]{:S(2)}) collective-permute-start(f32[1408,128]{1,0:T(8,128)S(1)} %shard_map.139), channel_id=1, source_target_pairs={{0,16},{4,20},{8,24},{12,28},{16,0},{20,4},{24,8},{28,12},{1,17},{... | collective-permute-start | bytes 2162696 | tf_op jit(solution)/shard_map/ppermute | solution.py:277
  182.7 134.4 %collective-permute-start.20 = (f32[8,128]{1,0:T(8,128)S(1)}, f32[8,128]{1,0:T(8,128)S(1)}, u32[]{:S(2)}, u32[]{:S(2)}) collective-permute-start(f32[8,128]{1,0:T(8,128)S(1)} %broadcast_multiply_fusion), channel_id=1, source_target_pairs={{0,1},{1,0},{2,3},{3,2},{4,5},{5,4},{6,7},{7,6},{8,9},{9,8},{10,11... | collective-permute-start | bytes 12296 | tf_op jit(solution)/shard_map/ppermute | solution.py:280
  185.9 35.6 %collective-permute-start.36 = (f32[1408,128]{1,0:T(8,128)S(1)}, f32[1408,128]{1,0:T(8,128)S(1)}, u32[]{:S(2)}, u32[]{:S(2)}) collective-permute-start(f32[1408,128]{1,0:T(8,128)S(1)} %shard_map.140), channel_id=1, source_target_pairs={{0,24},{4,28},{8,16},{12,20},{16,8},{20,12},{24,0},{28,4},{1,25},{... | collective-permute-start | bytes 2162696 | tf_op jit(solution)/shard_map/ppermute | solution.py:277
  188.4 32.1 %collective-permute-start.43 = (f32[704,128]{1,0:T(8,128)S(1)}, f32[704,128]{1,0:T(8,128)S(1)}, u32[]{:S(2)}, u32[]{:S(2)}) collective-permute-start(f32[704,128]{1,0:T(8,128)S(1)} %add.486), channel_id=1, source_target_pairs={{1,2},{2,1},{5,6},{6,5},{9,10},{10,9},{13,14},{14,13},{17,18},{18,... | collective-permute-start | bytes 1081352 | tf_op jit(solution)/shard_map/ppermute | solution.py:471
  216.2 18.8 %collective-permute-start.35 = (f32[1408,128]{1,0:T(8,128)S(1)}, f32[1408,128]{1,0:T(8,128)}, u32[]{:S(2)}, u32[]{:S(2)}) collective-permute-start(f32[1408,128]{1,0:T(8,128)S(1)} %shard_map.141), channel_id=1, source_target_pairs={{0,24},{4,28},{8,16},{12,20},{16,8},{20,12},{24,0},{28,4},{1,25},{... | collective-permute-start | bytes 2162696 | tf_op jit(solution)/shard_map/ppermute | solution.py:277
  220.6 19.1 %collective-permute-start.48 = (f32[704,128]{1,0:T(8,128)S(1)}, f32[704,128]{1,0:T(8,128)S(1)}, u32[]{:S(2)}, u32[]{:S(2)}) collective-permute-start(f32[704,128]{1,0:T(8,128)S(1)} %add.491), channel_id=1, source_target_pairs={{1,2},{2,1},{5,6},{6,5},{9,10},{10,9},{13,14},{14,13},{17,18},{18,... | collective-permute-start | bytes 1081352 | tf_op jit(solution)/shard_map/ppermute | solution.py:471
  298.0 19.0 %collective-permute-start.63 = (f32[704,128]{1,0:T(8,128)S(1)}, f32[704,128]{1,0:T(8,128)S(1)}, u32[]{:S(2)}, u32[]{:S(2)}) collective-permute-start(f32[704,128]{1,0:T(8,128)S(1)} %add.542), channel_id=1, source_target_pairs={{1,2},{2,1},{5,6},{6,5},{9,10},{10,9},{13,14},{14,13},{17,18},{18,... | collective-permute-start | bytes 1081352 | tf_op jit(solution)/shard_map/ppermute | solution.py:471
  311.5 23.5 %collective-permute-start.67 = (f32[704,128]{1,0:T(8,128)S(1)}, f32[704,128]{1,0:T(8,128)S(1)}, u32[]{:S(2)}, u32[]{:S(2)}) collective-permute-start(f32[704,128]{1,0:T(8,128)S(1)} %add.549), channel_id=1, source_target_pairs={{1,2},{2,1},{5,6},{6,5},{9,10},{10,9},{13,14},{14,13},{17,18},{18,... | collective-permute-start | bytes 1081352 | tf_op jit(solution)/shard_map/ppermute | solution.py:471
  312.2 21.1 %collective-permute-start.62 = (f32[704,128]{1,0:T(8,128)S(1)}, f32[704,128]{1,0:T(8,128)S(1)}, u32[]{:S(2)}, u32[]{:S(2)}) collective-permute-start(f32[704,128]{1,0:T(8,128)S(1)} %get-tuple-element.623), channel_id=1, source_target_pairs={{0,1},{1,0},{2,3},{3,2},{4,5},{5,4},{6,7},{7,6},{8,9},{9,8},{10,11... | collective-permute-start | bytes 1081352 | tf_op jit(solution)/shard_map/ppermute | solution.py:404
  317.0 23.2 %collective-permute-start.66 = (f32[704,128]{1,0:T(8,128)S(1)}, f32[704,128]{1,0:T(8,128)S(1)}, u32[]{:S(2)}, u32[]{:S(2)}) collective-permute-start(f32[704,128]{1,0:T(8,128)S(1)} %add.553), channel_id=1, source_target_pairs={{0,1},{1,0},{2,3},{3,2},{4,5},{5,4},{6,7},{7,6},{8,9},{9,8},{10,11... | collective-permute-start | bytes 1081352 | tf_op jit(solution)/shard_map/ppermute | solution.py:404
  (108 other events, 1621.3 us)

commit v2 on v0

v2 whole, which is shorter than its diff:
```python
import functools

import jax
import jax.numpy as jnp
from jax import lax
from jax.experimental import pallas as pl
from jax.experimental.pallas import tpu as pltpu
from jax.sharding import PartitionSpec as P

GENES = 2048
SLIDES = 4
LANES = 128
F32 = jnp.float32
BF16 = jnp.bfloat16
PAIR = [(0, 1), (1, 0), (2, 3), (3, 2)]
MIDDLE = [(1, 2), (2, 1)]


def room(mib):
    return pltpu.CompilerParams(vmem_limit_bytes=mib * 1024 * 1024)


class Order:
    def __init__(self):
        self.last = None

    def __call__(self, step, fresh, const=(), wait=()):
        gate = [*wait] if self.last is None else [self.last, *wait]
        if gate:
            fresh = lax.optimization_barrier((*fresh, *gate))[: len(fresh)]
        out = step(*fresh, *const)
        self.last = out[0] if isinstance(out, (tuple, list)) else out
        return out

    def here(self, x):
        return lax.optimization_barrier((x, self.last))[0]


def split(x):
    high = x.astype(BF16)
    return high, (x - high.astype(F32)).astype(BF16)


def three(a, b, dims):
    def dot(u, v):
        return lax.dot_general(u, v, (dims, ((), ())), preferred_element_type=F32)

    return dot(a[0], b[0]) + (dot(a[0], b[1]) + dot(a[1], b[0]))


def exact(a, b, dims):
    return lax.dot_general(a, b, (dims, ((), ())), precision=lax.Precision.HIGHEST, preferred_element_type=F32)


def cost(flops, size):
    del flops, size
    return pl.CostEstimate(flops=1, bytes_accessed=1, transcendentals=0)


def big(*arrays):
    return sum(x.size for x in arrays) * 4 // 2**20 + 1


VMEM = pl.BlockSpec(memory_space=pltpu.VMEM)
SMEM = pl.BlockSpec(memory_space=pltpu.SMEM)
HBM = pl.BlockSpec(memory_space=pltpu.HBM)


def at_rows(i, step, count=1):
    start = i * step
    return pl.ds(start if isinstance(i, int) else pl.multiple_of(start, 16), step * count)


def cut_kernel(layout, step, at_ref, l_ref, *refs):
    outs, sems = refs[:-1], refs[-1]
    copies = []
    for out, places in zip(outs, layout, strict=True):
        for k, place in enumerate(places):
            copies.append(
                pltpu.make_async_copy(
                    l_ref.at[at_rows(at_ref[place], step)], out.at[at_rows(k, step)], sems.at[len(copies)]
                )
            )
    for copy in copies:
        copy.start()
    for copy in copies:
        copy.wait()


def cut_blocks(layout, step, at, logits):
    width = logits.shape[1]
    count = sum(len(places) for places in layout)
    return pl.pallas_call(
        functools.partial(cut_kernel, layout, step),
        in_specs=[SMEM, VMEM],
        out_specs=(HBM,) * len(layout),
        out_shape=tuple(jax.ShapeDtypeStruct((len(places) * step, width), F32) for places in layout),
        scratch_shapes=[pltpu.SemaphoreType.DMA((count,))],
        name="cut",
        compiler_params=room(big(logits) + 2),
        cost_estimate=cost(0, 8 * count * step * width),
    )(at, logits)


def softmax_kernel(spots, scale, l_ref, inv_ref, cell_ref, o_ref, buffer, sem):
    cells, width = l_ref.shape
    genes = cell_ref.shape[1]
    n_q = cells // genes

    def column(k, total):
        e = jnp.exp(l_ref[at_rows(k, genes), :])
        return total + jnp.sum(e.reshape(genes // 8, 8, width), axis=0)

    total = lax.fori_loop(0, n_q, column, jnp.zeros((8, width), F32))
    inv = 1.0 / jnp.sum(total, axis=0, keepdims=True)
    inv_ref[...] = inv
    ones = jnp.ones((16, width), BF16)

    def row(k, square):
        e = jnp.exp(l_ref[at_rows(k, genes), :])
        share = e * inv
        buffer[at_rows(k, genes), :] = e * scale
        pltpu.make_async_copy(buffer.at[at_rows(k, genes)], o_ref.at[at_rows(k, genes)], sem).start()
        high, low = split(share)
        sums = [lax.dot_general(ones, x, (((1,), (1,)), ((), ())), preferred_element_type=F32) for x in (high, low)]
        cell_ref[pl.ds(k, 1), :] = (sums[0] + sums[1])[0:1, :] * (1.0 / spots)
        return square + jnp.sum((share * share).reshape(genes // 8, 8, width), axis=0)

    square = lax.fori_loop(0, n_q, row, jnp.zeros((8, width), F32))
    cell_ref[n_q:, :] = jnp.full((cell_ref.shape[0] - n_q, genes), jnp.sum(square), F32)
    pltpu.make_async_copy(buffer, o_ref, sem).wait()


def softmax_sums(spots, genes, logits):
    cells, width = logits.shape
    n_cells = -(-(cells // genes + 1) // 8) * 8
    return pl.pallas_call(
        functools.partial(softmax_kernel, spots, float(cells)),
        in_specs=[VMEM],
        out_specs=(VMEM, VMEM, HBM),
        out_shape=(
            jax.ShapeDtypeStruct((1, width), F32),
            jax.ShapeDtypeStruct((n_cells, genes), F32),
            pltpu.HBM((cells, width), F32),
        ),
        scratch_shapes=[pltpu.VMEM((cells, width), F32), pltpu.SemaphoreType.DMA],
        name="softmax",
        compiler_params=room(2 * big(logits) + 4),
        cost_estimate=cost(0, 0),
    )(logits)


def parts_kernel(step, x_ref, high_ref, low_ref, buffer, sems):
    count = x_ref.shape[0] // step

    def copy(k):
        return pltpu.make_async_copy(x_ref.at[at_rows(k, step)], buffer.at[at_rows(k, step)], sems.at[k])

    for k in range(count):
        copy(k).start()
    for k in range(count):
        copy(k).wait()
        high_ref[at_rows(k, step), :], low_ref[at_rows(k, step), :] = split(buffer[at_rows(k, step), :])


def parts_of(x, step):
    return pl.pallas_call(
        functools.partial(parts_kernel, step),
        in_specs=[HBM],
        out_specs=(VMEM, VMEM),
        out_shape=(pltpu.VMEM(x.shape, BF16), pltpu.VMEM(x.shape, BF16)),
        scratch_shapes=[pltpu.VMEM(x.shape, F32), pltpu.SemaphoreType.DMA((x.shape[0] // step,))],
        name="parts",
        compiler_params=room(12),
        cost_estimate=cost(4 * x.size, 8 * x.size),
    )(x)


def pred_kernel(jobs, n_acc, step, tail, at_ref, *refs):
    n_l = 1 + max(job[2] for job in jobs)
    n_given = max(job[1] for job in jobs)
    ls, xs, given, outs = refs[:n_l], refs[n_l : n_l + 4], refs[n_l + 4 :][:n_given], refs[-n_acc:]
    place = lambda at: at_ref[at[0]] if isinstance(at, list) else at
    for k in range(n_acc):
        acc = None
        for _, g, l, l_at, x, x_at, count in [job for job in jobs if job[0] == k]:
            if g:
                acc = given[g - 1][...]
            for c in range(count):
                e = split(jnp.exp(ls[l][at_rows(place(l_at) + c, step), :]))
                rows = at_rows(place(x_at) + c, step)
                term = three(e, (xs[2 * x][rows, :], xs[2 * x + 1][rows, :]), ((0,), (0,)))
                acc = term if acc is None else acc + term
        outs[k][: acc.shape[0], :] = acc
        if tail:
            outs[k][acc.shape[0] :, :] = refs[-n_acc - 1][...]


def pred_sums_of(jobs, n_acc, step, at, ls, xs, given, tail=()):
    width, genes = ls[0].shape[1], xs[0].shape[1]
    steps = sum(job[-1] for job in jobs)
    return pl.pallas_call(
        functools.partial(pred_kernel, jobs, n_acc, step, len(tail)),
        in_specs=[SMEM] + [VMEM] * (len(ls) + len(xs) + len(given) + len(tail)),
        out_specs=(VMEM,) * n_acc,
        out_shape=(jax.ShapeDtypeStruct((width + sum(x.shape[0] for x in tail), genes), F32),) * n_acc,
        name="pred",
        compiler_params=room(16),
        cost_estimate=cost(6 * steps * step * width * genes, 4 * steps * step * (width + genes)),
    )(at, *ls, *xs, *given, *tail)


def weights_of(mask_ref, counts_ref):
    weights = (mask_ref[...] * counts_ref[...]).astype(F32)
    return jnp.concatenate([weights, jnp.zeros((8 - SLIDES, weights.shape[1]), F32)], axis=0)


def column_of(row):
    return jnp.transpose(jnp.broadcast_to(row, (LANES, row.shape[1])))


def sums_kernel(n_parts, *refs):
    parts, (cells_ref, inv_ref, spatial_ref, ids_ref, mask_ref, counts_ref, pred_ref, wide_ref, spot_ref, q_ref) = (
        refs[:n_parts],
        refs[n_parts:],
    )
    spatial = spatial_ref[...]
    pred, q = parts[0][...], cells_ref[...]
    for part in parts[1:]:
        pred = pred + part[: pred.shape[0], :]
        q = q + part[pred.shape[0] :, :]
    q_ref[...] = q
    genes = pred.shape[1]
    pred = pred * jnp.concatenate([column_of(inv_ref[...])] * (genes // LANES), axis=1)
    pred_ref[...] = pred
    onehot = (lax.broadcasted_iota(jnp.int32, (8, LANES), 0) == ids_ref[...]).astype(F32)
    ones = jnp.ones((8, genes), F32)
    rows = lax.broadcasted_iota(jnp.int32, (8, LANES), 0)
    spot = jnp.where(rows == 3, jnp.sum(weights_of(mask_ref, counts_ref)), 0.0)
    for k, product in enumerate((pred * spatial, pred * pred, spatial * spatial)):
        wide_ref[8 * k : 8 * k + 8, :] = exact(onehot, product, ((1,), (0,)))
        spot = jnp.where(rows == k, exact(ones, product, ((1,), (1,))), spot)
    spot_ref[...] = spot


def pred_sums(n_parts, *args):
    parts, (by_cell, inv, spatial, ids, mask, counts) = args[:n_parts], args[n_parts:]
    width, genes = spatial.shape
    return pl.pallas_call(
        functools.partial(sums_kernel, n_parts),
        out_shape=(
            jax.ShapeDtypeStruct((width, genes), F32),
            jax.ShapeDtypeStruct((24, genes), F32),
            jax.ShapeDtypeStruct((8, width), F32),
            jax.ShapeDtypeStruct(by_cell.shape, F32),
        ),
        name="sums",
        compiler_params=room(12),
        cost_estimate=cost(10 * width * genes * 48, 4 * width * genes * 6),
    )(*parts, by_cell, inv, spatial, ids, mask, counts)


def dpred_kernel(spots, share_blk, share_gene, *refs):
    wides, spot, refs = refs[:2], refs[2][...] + refs[3][...], refs[4:]
    pred_ref, spatial_ref, ids_ref, mask_ref, counts_ref, inv_ref, d_ref, tot_ref = refs
    weights = weights_of(mask_ref, counts_ref)
    genes = pred_ref.shape[1]
    a, b, c = (wides[0][8 * k : 8 * k + 8, :] + wides[1][8 * k : 8 * k + 8, :] for k in range(3))
    e, f, h, wsum = (spot[k : k + 1, :] for k in range(4))
    wsum = jnp.max(wsum)
    gain = weights / wsum
    inv_g = lax.rsqrt(b * c + 1e-06)
    inv_s = lax.rsqrt(f * h + 1e-06)
    grad_a = -gain * inv_g
    grad_b = gain * a * c * inv_g * inv_g * inv_g
    onehot = (lax.broadcasted_iota(jnp.int32, (8, LANES), 0) == ids_ref[...]).astype(F32)
    wide = functools.partial(jnp.concatenate, axis=1)
    by_spatial = exact(onehot, grad_a, ((0,), (0,))) - wide([column_of(inv_s / spots)] * (genes // LANES))
    by_pred = exact(onehot, grad_b, ((0,), (0,))) + wide(
        [column_of(e * h * inv_s * inv_s * inv_s / spots)] * (genes // LANES)
    )
    pred = pred_ref[...]
    dpred = by_spatial * spatial_ref[...] + by_pred * pred
    inv = inv_ref[...]
    d_ref[:LANES, :] = dpred * wide([column_of(inv)] * (genes // LANES))
    own = exact(jnp.ones((8, genes), F32), pred * dpred, ((1,), (1,))) * inv
    d_ref[LANES:, :] = wide([own] * (genes // LANES))
    rows = lax.broadcasted_iota(jnp.int32, (8, LANES), 0)
    tot = jnp.where(rows == 0, jnp.sum(weights * a * inv_g) * share_blk, 0.0)
    tot = jnp.where(rows == 1, jnp.sum(e * inv_s) * share_gene, tot)
    tot = jnp.where(rows == 2, jnp.sum(f) * share_gene, tot)
    tot_ref[...] = jnp.where(rows == 3, wsum, tot)


def dpred_scaled(spots, share_blk, share_gene, *args):
    spatial = args[5]
    width, genes = spatial.shape
    return pl.pallas_call(
        functools.partial(dpred_kernel, spots, share_blk, share_gene),
        out_shape=(
            jax.ShapeDtypeStruct((width + 8, genes), F32),
            jax.ShapeDtypeStruct((8, width), F32),
        ),
        name="dpred",
        compiler_params=room(12),
        cost_estimate=cost(10 * width * genes * 48, 4 * width * genes * 6),
    )(*args)


def dmap_kernel(rows, step, n, *refs):
    xs, ds, outs = refs[:4], refs[4 : 4 + n], refs[4 + n :]
    parts = [split(d[:LANES, :]) for d in ds]
    d = tuple(jnp.concatenate([part[i] for part in parts], axis=0) for i in range(2))
    own = jnp.concatenate([d[LANES : LANES + 1, :LANES] for d in ds], axis=1)
    for k, (x, first) in enumerate(rows):
        here = at_rows(first, step)
        value = three((xs[2 * x][here, :], xs[2 * x + 1][here, :]), d, ((1,), (1,))) - own
        for i, out in enumerate(outs):
            out[at_rows(k, step), :] = value[:, i * LANES : (i + 1) * LANES]


def dmap_blocks(rows, step, ds, xs):
    genes = ds[0].shape[1]
    width = ds[0].shape[0] - 8
    return pl.pallas_call(
        functools.partial(dmap_kernel, rows, step, len(ds)),
        in_specs=[VMEM] * (4 + len(ds)),
        out_specs=(VMEM,) * len(ds),
        out_shape=(jax.ShapeDtypeStruct((len(rows) * step, width), F32),) * len(ds),
        name="dmap",
        compiler_params=room(16),
        cost_estimate=cost(0, 0),
    )(*xs, *ds)


def egrad_kernel(scale, ks, step, wheres, n_add, at_ref, *refs):
    n = len(wheres)
    counts = [2 if isinstance(where, tuple) else 1 for where in wheres]
    ls, ds, adds, o_ref = refs[: sum(counts)], refs[sum(counts) : sum(counts) + n], refs[sum(counts) + n : -1], refs[-1]
    parts = [split(d[:LANES, :]) for d in ds]
    d = tuple(jnp.concatenate([part[i] for part in parts], axis=0) for i in range(2))
    for j, k in enumerate(ks):
        es, at = [], 0
        for where, number in zip(wheres, counts, strict=True):
            if number == 2:
                mine, others = (ls[at + i][at_rows(where[i], step), :] for i in range(2))
                l = jnp.where(at_ref[0] == k, mine, others)
            else:
                l = ls[at][at_rows(where + k, step), :]
            at += number
            es.append(jnp.exp(l))
        value = three(split(jnp.concatenate(es, axis=1)), d, ((1,), (0,))) * scale
        o_ref[at_rows(j, step), :] = value + adds[j][...] if n_add else value


def egrad_part(ks, step, wheres, scale, at, ls, ds, adds=()):
    genes = ds[0].shape[1]
    return pl.pallas_call(
        functools.partial(egrad_kernel, scale, ks, step, wheres, len(adds)),
        in_specs=[SMEM] + [VMEM] * (len(ls) + len(ds) + len(adds)),
        out_specs=VMEM,
        out_shape=jax.ShapeDtypeStruct((len(ks) * step, genes), F32),
        name="egrad",
        compiler_params=room(big(*ls, *ds, *adds) + 24),
        cost_estimate=cost(0, 0),
    )(at, *ls, *ds, *adds)


def ratio_kernel(spots, lo, hi, block, scale, *refs):
    more = lo > 0
    cell_ref, density_ref, inv_ref, a_ref = refs[:4]
    b_ref, given_ref = refs[4:6] if more else (None, None)
    _, o_ref, sum_ref, kl_ref, a, b, sems = refs[-7:]
    inv = inv_ref[...]
    width = a_ref.shape[1]
    n_q, genes = density_ref.shape
    step = block * genes

    def load(k):
        return pltpu.make_async_copy(a_ref.at[at_rows(lo + k, step)], a.at[at_rows(k, step)], sems.at[k])

    def store(k):
        return pltpu.make_async_copy(b.at[at_rows(k, step)], o_ref.at[at_rows(lo + k, step)], sems.at[hi - lo + k])

    for k in range(hi - lo):
        load(k).start()
    density = density_ref[...]
    target = density / jnp.sum(density)
    q = cell_ref[:n_q, :]
    ratios = target / q / spots
    kl_ref[...] = jnp.full(kl_ref.shape, jnp.sum(target * (jnp.log(target) - jnp.log(q))))
    rows = lax.broadcasted_iota(jnp.int32, (16, genes), 0)
    ones = (lax.broadcasted_iota(jnp.int32, (16, LANES), 0) < 3).astype(BF16)
    total = jnp.zeros((8, width), F32)
    for k in range(hi - lo):
        load(k).wait()
        for i in range(block):
            ratio = ratios[(lo + k) * block + i : (lo + k) * block + i + 1, :]
            high = ratio.astype(BF16).astype(F32)
            mid = (ratio - high).astype(BF16).astype(F32)
            terms = jnp.where(rows == 0, high, jnp.where(rows == 1, mid, jnp.where(rows == 2, ratio - high - mid, 0.0)))
            column = lax.dot_general(terms.astype(BF16), ones, (((0,), (0,)), ((), ())), preferred_element_type=F32)
            here = at_rows(k * block + i, genes)
            product = a[here, :] * column
            total = total + jnp.sum(product.reshape(genes // 8, 8, width), axis=0)
            b[here, :] = -product * inv
        store(k).start()
    total = jnp.sum(total, axis=0, keepdims=True) * (inv * inv * (1.0 / scale))
    sum_ref[...] = jnp.broadcast_to(total, sum_ref.shape) + (given_ref[...] if more else 0.0)
    for k in range(hi - lo):
        store(k).wait()


def ratio_part(spots, lo, hi, block, by_cell, density, inv, a, b=None, given=None):
    cells, width = a.shape
    genes = density.shape[1]
    size = (hi - lo) * block * genes
    more = () if b is None else (b, given)
    return pl.pallas_call(
        functools.partial(ratio_kernel, spots, lo, hi, block, float(cells)),
        in_specs=[VMEM, VMEM, VMEM, HBM] + [HBM, VMEM][: len(more)],
        out_specs=(HBM, HBM, VMEM, VMEM),
        out_shape=(
            pltpu.HBM((cells, width), F32),
            pltpu.HBM((cells, width), F32),
            jax.ShapeDtypeStruct((8, width), F32),
            jax.ShapeDtypeStruct((8, width), F32),
        ),
        scratch_shapes=[pltpu.VMEM((size, width), F32)] * 2 + [pltpu.SemaphoreType.DMA((2 * (hi - lo),))],
        input_output_aliases={3: 0, 4: 1} if more else {3: 0},
        name="ratio",
        compiler_params=room(2 * (size * width * 4 // 2**20 + 1) + 6),
        cost_estimate=cost(0, 0),
    )(by_cell, density, inv, a, *more)


def join_kernel(a_ref, b_ref, o_ref):
    half = a_ref.shape[0]
    o_ref[:half, :] = a_ref[...]
    o_ref[half:, :] = b_ref[...]


def join(a, b):
    return pl.pallas_call(
        join_kernel,
        in_specs=[VMEM, VMEM],
        out_specs=VMEM,
        out_shape=jax.ShapeDtypeStruct((2 * a.shape[0], a.shape[1]), F32),
        name="join",
        compiler_params=room(8),
        cost_estimate=cost(0, 0),
    )(a, b)


def add_kernel(first, a_ref, b_ref, o_ref):
    o_ref[...] = a_ref[pl.ds(first, o_ref.shape[0]), :] + b_ref[...]


def add(first, a, b):
    return pl.pallas_call(
        functools.partial(add_kernel, first),
        in_specs=[VMEM, VMEM],
        out_specs=VMEM,
        out_shape=jax.ShapeDtypeStruct(b.shape, F32),
        name="add",
        compiler_params=room(8),
        cost_estimate=cost(0, 0),
    )(a, b)


def add_all_kernel(*refs):
    total = refs[0][...]
    for ref in refs[1:-1]:
        total = total + ref[...]
    refs[-1][...] = total


def add_all(*arrays):
    return pl.pallas_call(
        add_all_kernel,
        in_specs=[VMEM] * len(arrays),
        out_specs=VMEM,
        out_shape=jax.ShapeDtypeStruct(arrays[0].shape, F32),
        name="add_all",
        compiler_params=room(8),
        cost_estimate=cost(0, 0),
    )(*arrays)


def next_kernel(first, at_ref, s_ref, y_ref, b_ref, t_ref, o_ref):
    total = s_ref[...] + y_ref[...]
    t_ref[...] = total
    o_ref[...] = jnp.where(at_ref[0] == 1, b_ref[pl.ds(first, o_ref.shape[0]), :], total)


def next_piece(first, end, s, y, b):
    return pl.pallas_call(
        functools.partial(next_kernel, first),
        in_specs=[SMEM, VMEM, VMEM, VMEM],
        out_specs=(VMEM, VMEM),
        out_shape=(jax.ShapeDtypeStruct(s.shape, F32), jax.ShapeDtypeStruct(s.shape, F32)),
        name="next",
        compiler_params=room(8),
        cost_estimate=cost(0, 0),
    )(end, s, y, b)


def final_kernel(place, n, end_ref, at_ref, *refs):
    rxs, ss, (sum_ref, a_ref, g_ref, _, o_ref, a, b, sems) = refs[:n], refs[n : 2 * n], refs[2 * n :]
    step = a.shape[0] // n
    here = at_rows(at_ref[place], step, n)
    loads = [
        pltpu.make_async_copy(a_ref.at[here], a, sems.at[0]),
        pltpu.make_async_copy(g_ref.at[here], b, sems.at[1]),
    ]
    for load in loads:
        load.start()
    for load in loads:
        load.wait()
    stores = []
    for k in range(n):
        there, rows = at_rows(at_ref[place] + k, step), at_rows(k, step)
        whole = jnp.where(end_ref[0] == 1, rxs[k][...], ss[k][...])
        b[rows, :] = a[rows, :] * (whole + sum_ref[0:1, :]) + b[rows, :]
        stores.append(pltpu.make_async_copy(b.at[rows], o_ref.at[there], sems.at[2 + k]))
        stores[-1].start()
    for store in stores:
        store.wait()


def final_pieces(place, end, at, rxs, ss, ratio_sum, a, grad):
    step, width = ss[0].shape
    n = len(ss)
    return pl.pallas_call(
        functools.partial(final_kernel, place, n),
        in_specs=[SMEM, SMEM] + [VMEM] * (2 * n + 1) + [HBM, HBM],
        out_specs=(HBM, HBM),
        out_shape=(pltpu.HBM(a.shape, F32), pltpu.HBM(grad.shape, F32)),
        scratch_shapes=[pltpu.VMEM((n * step, width), F32)] * 2 + [pltpu.SemaphoreType.DMA((2 + n,))],
        input_output_aliases={3 + 2 * n: 0, 4 + 2 * n: 1},
        name="final",
        compiler_params=room(8),
        cost_estimate=cost(0, 0),
    )(end, at, *rxs, *ss, ratio_sum, a, grad)


def shards(logits, expression, spatial, density, gene_mask, gene_counts, slide_ids):
    n_blk = lax.axis_size("blk")
    n_gene = lax.axis_size("gene")
    me = lax.axis_index("blk")
    plane = lax.axis_index("gene")
    cells, width = logits.shape
    rows, genes = expression.shape
    half = rows // 2
    spots = width * n_blk
    order = Order()

    def swap(x, m):
        return lax.ppermute(x, "blk", [(i, i ^ m) for i in range(n_blk)])

    def across(x, m):
        return lax.ppermute(x, "gene", [(i, i ^ m) for i in range(n_gene)])

    def cut(l, r, first, size):
        return lax.dynamic_slice_in_dim(l, (me ^ r) * rows + first, size, 0)

    far = sorted(range(2, n_blk, 2), key=lambda m: (m.bit_count(), m))
    side = plane % 2
    at = jnp.stack([side, 1 - side, *[(me ^ r) * 2 + k for r in range(n_blk) for k in range(2)]]
        + [(me ^ r) * 2 + side for r in range(n_blk)]).astype(jnp.int32)

    def whole(r):
        return (2 + 2 * r, 3 + 2 * r)

    def mine(r):
        return (2 + 2 * n_blk + r,)

    sent, passed, held = {}, {}, {}

    other = swap(expression, 1)
    constants = (slide_ids[None, :], gene_mask, gene_counts[None, :])
    n_q = cells // genes

    def add_pred(jobs, n_acc, ls, given=(), tail=()):
        n, g = len(ls), len(given)

        def run(*a):
            return pred_sums_of(jobs, n_acc, half, at, a[:n], a[n + g : n + g + 4], a[n : n + g], a[n + g + 4 :])

        return order(run, (*ls, *given), (*own_x, *other_x, *tail))

    def cuts(*layout):
        return order(lambda l: cut_blocks(layout, half, at, l), (logits,))

    if n_blk == 8 and n_gene == 4:
        near3, near5 = cuts(mine(3), mine(5))
        sent[3], sent[5] = swap(near3, 2), swap(near5, 4)
        own_x = order(lambda x: parts_of(x, half), (expression,))
        both, near2, near4, stay = cuts(mine(6) + mine(7), whole(2), whole(4), whole(0) + whole(1))
        passed[3] = across(order(join, (sent[3], sent[5])), 1)
        sent[6], sent[2], sent[4] = swap(order.here(both), 6), swap(order.here(near2), 2), swap(order.here(near4), 4)
        inv, by_cell, scale = order(functools.partial(softmax_sums, spots, genes), (logits,))
        other_x = order(lambda x: parts_of(x, half), (other,))
        by_cell = order(functools.partial(add, 0), (by_cell, swap(by_cell, 1)))
        (acc0,) = add_pred(((0, 0, 0, 0, 0, 0, 2), (0, 0, 0, 2, 1, 0, 2)), 1, (stay,))
        acc2, acc4 = add_pred(((0, 0, 0, 0, 1, [0], 1), (1, 0, 1, 0, 1, [0], 1)), 2, (sent[3], sent[5]))
        passed[6] = across(order.here(sent[6]), 1)
        (acc6,) = add_pred(((0, 0, 0, 0, 0, [0], 1), (0, 0, 0, 1, 1, [0], 1)), 1, (sent[6],))
        acc2, acc4 = add_pred(
            ((0, 1, 0, 0, 1, [1], 1), (1, 2, 0, 1, 1, [1], 1)), 2, (passed[3],), (acc2, acc4)
        )
        (acc2,) = add_pred(((0, 1, 0, 0, 0, 0, 2),), 1, (sent[2],), (acc2,), (by_cell,))
        moved = {2: swap(acc2, 2)}
        (acc4,) = add_pred(((0, 1, 0, 0, 0, 0, 2),), 1, (sent[4],), (acc4,), (by_cell,))
        moved[4] = swap(acc4, 4)
        (acc6,) = add_pred(((0, 1, 0, 0, 0, [1], 1), (0, 0, 0, 1, 1, [1], 1)), 1, (passed[6],), (acc6,), (by_cell,))
        moved[6] = swap(acc6, 6)
        held = {
            2: ((sent[2],), 0),
            3: ((sent[3], passed[3]), (0, 0)),
            4: ((sent[4],), 0),
            5: ((sent[5], passed[3]), (0, 1)),
            6: ((sent[6], passed[6]), (0, 0)),
            7: ((sent[6], passed[6]), (1, 1)),
        }
    else:
        inv, by_cell, scale = order(functools.partial(softmax_sums, spots, genes), (logits,))
        by_cell = order(functools.partial(add, 0), (by_cell, swap(by_cell, 1)))
        own_x = order(lambda x: parts_of(x, half), (expression,))
        other_x = order(lambda x: parts_of(x, half), (other,))
        (stay,) = cuts(whole(0) + whole(1))
        (acc0,) = add_pred(((0, 0, 0, 0, 0, 0, 2), (0, 0, 0, 2, 1, 0, 2)), 1, (stay,))
        moved = {}
        for m in far:
            blocks = cuts(whole(m), whole(m + 1))
            for r in (m, m + 1):
                sent[r] = swap(blocks[r - m], m)
                held[r] = ((sent[r],), 0)
            (acc,) = add_pred(((0, 0, 0, 0, 0, 0, 2), (0, 0, 1, 0, 1, 0, 2)), 1, (sent[m], sent[m + 1]), (), (by_cell,))
            moved[m] = swap(acc, m)
    held[0], held[1] = ((stay,), 0), ((stay,), 2)

    parts = [acc0] + [moved[m] for m in far]
    pred, wide, spot, by_cell = order(
        functools.partial(pred_sums, len(parts)), parts, (by_cell, inv, spatial, *constants)
    )
    density = density.reshape(n_q, genes)
    blocks = n_q // 2
    state = {"scale": scale}

    def kl_part(lo, hi):
        more = (state["grad"], state["ratio_sum"]) if lo else ()
        state["scale"], state["grad"], state["ratio_sum"], state["kl"] = order(
            functools.partial(ratio_part, spots, lo, hi, 2), (by_cell,), (density, inv, state["scale"], *more)
        )

    spot_moved = across(spot, 1)
    m = 1
    while 2 * m < n_blk:
        wide = order(functools.partial(add, 0), (wide, swap(wide, m)))
        m *= 2
        if m == 2:
            spot = order(add_all, (spot, spot_moved))
            spot_moved = across(spot, 2)
    wide_moved = swap(wide, m)
    grad, tot = order(
        functools.partial(dpred_scaled, spots, 1.0 / n_blk, 1.0 / n_gene),
        (wide, wide_moved, spot, spot_moved),
        (pred, spatial, *constants, inv),
    )
    grads = {0: grad}
    for m in far:
        grads[m] = swap(grad, m)
    back = {}

    def dmap(ms, rows, wait=()):
        outs = order(
            lambda *a: dmap_blocks(rows, half, a[: len(ms)], a[len(ms) :]),
            [grads[m] for m in ms],
            (*own_x, *other_x),
            wait,
        )
        for m, d in zip(ms, outs, strict=True):
            d = swap(d, m) if m else d
            for k, (odd, first) in enumerate(rows):
                back[m + odd, first] = (d, k * half)

    if n_blk == 8:
        places = [(0, 0), (0, 1), (1, 0), (1, 1), (2, 0), (4, 0), (2, 1), (4, 1)]
        places += [(r, k) for r in (3, 5, 6, 7) for k in range(2)]
    else:
        places = [(r, k) for m in [0, *far] for r in (m, m + 1) for k in range(2)]
    count, lag = len(places), 3
    part, total_of, mid, got = {}, {}, {}, {}
    end = jnp.reshape((plane == 0) | (plane == n_gene - 1), (1,)).astype(jnp.int32)

    def send(t):
        if t >= count + lag:
            return
        if t < count:
            block, first = back[places[t]]
        if t < lag:
            buffer = block if block.shape[0] == half else order(lambda b: b[first : first + half], (block,))
        elif t < count:
            total_of[t - lag], buffer = order(
                lambda s, y, b: next_piece(first, end, s, y, b), (part[t - lag], mid[t - lag], block)
            )
        else:
            buffer = total_of[t - lag] = order(functools.partial(add, 0), (part[t - lag], mid[t - lag]))
        got[t] = lax.ppermute(buffer, "gene", PAIR)

    def finish(*ts):
        r, k = places[ts[0]]
        n = len(ts)
        state["scale"], state["grad"] = order(
            lambda *a: final_pieces(2 + 2 * r + k, end, at, a[:n], a[n : 2 * n], *a[2 * n :]),
            (*[got[t + lag] for t in ts], *[total_of[t] for t in ts]),
            (state["ratio_sum"], state["scale"], state["grad"]),
        )

    def expr_part(odd, ks, adds=()):
        ms = [0, *far]
        ls = [l for m in ms for l in held[m + odd][0]]
        wheres = [held[m + odd][1] for m in ms]
        n, m = len(ls), len(adds)
        return order(
            lambda d, *a: egrad_part(ks, half, wheres, float(cells), at, a[m : m + n], (d, *a[m + n :]), a[:m]),
            (grads[0], *adds),
            (*ls, *[grads[m] for m in far]),
        )

    all_rows = ((0, 0), (0, 1), (1, 0), (1, 1))

    def extra(t):
        if t == 0:
            dmap((0,), ((1, 0),))
            dmap((0,), ((1, 1),))
            if n_blk == 8:
                dmap((2, 4), ((0, 0),))
            else:
                for m in far:
                    dmap((m,), all_rows)
        if n_blk == 8:
            if t == 2:
                dmap((2, 4), ((0, 1), (1, 0), (1, 1)), (back[2, 0][0], back[4, 0][0]))
            if t == 6:
                dmap((6,), all_rows, (back[3, 0][0], back[5, 0][0]))
        if 0 <= t < 4:
            kl_part(blocks * t // 4, blocks * (t + 1) // 4)
        for step, (move, m) in enumerate(stages):
            if t == first_stage + 2 * step + 2:
                state["tot"] = order(functools.partial(add, 0), (state.get("tot", tot), state["moving"]))
        for step, (move, m) in enumerate(stages):
            if t == first_stage + 2 * step:
                state["moving"] = move(order.here(state.get("tot", tot)), m)
        if t in (15, 16):
            state["swapped", t] = swap(expr_part(1, (t - 15,)), 1)
        if t == 18:
            state["expr"] = expr_part(0, (0, 1), (state["swapped", 15], state["swapped", 16]))

    stages, m = [(across, 1), (across, 2)], 1
    while m < n_blk:
        stages.append((swap, m))
        m *= 2
    first_stage = 16 - 2 * len(stages)

    def joins(t):
        return t + 1 < count and places[t][0] == places[t + 1][0] and places[t][1] == 0

    ready = []
    dmap((0,), ((0, 0),))
    send(0)
    dmap((0,), ((0, 1),))
    for t in range(count + lag):
        send(t + 1)
        extra(t)
        done = t - lag
        if done > 0:
            ready.append(done - 1)
        while ready and (len(ready) > 1 or places[ready[0]][1] == 0 and not joins(ready[0])):
            n = 2 if joins(ready[0]) else 1
            finish(*ready[:n])
            del ready[:n]
        if t < count:
            block, first = back[places[t]]
            part[t] = order(functools.partial(add, first), (block, got[t]))
            mid[t] = lax.ppermute(part[t], "gene", MIDDLE)
    for t in (*ready, count - 1):
        finish(t)

    sums = state["tot"]
    loss = -sums[0, 0] / tot[3, 0] - sums[1, 0] / spots + state["kl"][0, 0]
    rms_map = jnp.sqrt(by_cell[n_q, 0] / (cells * spots))
    rms_pred = jnp.sqrt(sums[2, 0] / (spots * GENES))
    return (loss, state["grad"], state["expr"], rms_map, rms_pred)


def solution(mesh):
    placed = (
        P(None, "blk"),
        P("blk", "gene"),
        P("blk", "gene"),
        P(),
        P(None, "gene"),
        P("gene"),
        P("blk"),
    )
    return jax.shard_map(
        shards,
        mesh=mesh,
        in_specs=placed,
        out_specs=(P(), P(None, "blk"), P("blk", "gene"), P(), P()),
        check_vma=False,
    )
```

time: 653 us -> 289 us (0.44)
  waiting for transfers between devices: 450 us -> 59.6 us
  starting transfers between devices: 0.38 us -> 109 us
  Pallas kernels: 0 us -> 99.5 us
  matrix products: 74.2 us -> 0 us
  blocking collectives: 52.2 us -> 0 us
  other arithmetic: 33.5 us -> 0 us
  between operations: 24.5 us -> 9.19 us
    psum x2 -> x0, waiting for transfers between devices: 222 us -> none  [the longest x1 176 us: shards(): dmap = lax.psum(dmap_part, 'gene')]
    reduce_scatter x1 -> x0, waiting for transfers between devices: 128 us -> none  [shards(): lax.psum_scatter(jnp.dot(rows, dpred, precision=HIGH, preferred_element_t...]
    ppermute x0 -> x67, starting transfers between devices: none -> 109 us  [the longest x19 66.8 us: send(): got[t] = lax.ppermute(buffer, 'gene', PAIR)]
    pallas_call x0 -> x81, Pallas kernels: none -> 99.5 us  [the longest x11 29.3 us: final_pieces(): pl.pallas_call(functools.partial(final_kernel, place, n), in_specs=[SMEM,...]
    all_gather x1 -> x0, waiting for transfers between devices: 99.2 us -> none  [shards(): lax.all_gather(expression, 'blk', axis=0, tiled=True)]
    dot_general x8 -> x0, matrix products: 74.2 us -> none  [the longest x1 29.2 us: shards(): lax.dot_general(lax.all_gather(expression, 'blk', axis=0, tiled=True), dp...]
    ppermute x0 -> x67, waiting for transfers between devices: none -> 59.6 us  [the longest x6 29.9 us: across(): return lax.ppermute(x, 'gene', [(i, i ^ m) for i in range(n_gene)])]
    psum x2 -> x0, blocking collectives: 52.2 us -> none  [the longest x1 40.5 us: shards(): totals = lax.psum(partials, ('blk', 'gene'))]
  transfers between devices with their start and end apart: 4 -> 67, of which waited for: 4 -> 21; matrix products, arithmetic and copies ran while one was open for 10% -> 1% of each run, Pallas kernels for 0% -> 31%
where the time goes in v2:
time: 289 us; the launch traced here: 288 us
  starting transfers between devices  109 us (38%)
  Pallas kernels  99.5 us (34%)
  waiting for transfers between devices  59.6 us (21%)
  local copies, waits for them, and re-layouts  11 us (4%)
  between operations  9.19 us (3%)
    ppermute x19, starting transfers between devices, send(): got[t] = lax.ppermute(buffer, 'gene', PAIR)  66.8 us
    ppermute x6, waiting for transfers between devices, across(): return lax.ppermute(x, 'gene', [(i, i ^ m) for i in range(n_gene)])  29.9 us
    pallas_call x11, Pallas kernels, final_pieces(): pl.pallas_call(functools.partial(final_kernel, place, n), in_specs=[SMEM,...  29.3 us
    ppermute x26, waiting for transfers between devices, swap(): return lax.ppermute(x, 'blk', [(i, i ^ m) for i in range(n_blk)])  22.5 us
    ppermute x26, starting transfers between devices, swap(): return lax.ppermute(x, 'blk', [(i, i ^ m) for i in range(n_blk)])  20.6 us
    pallas_call x4, Pallas kernels, ratio_part(): pl.pallas_call(functools.partial(ratio_kernel, spots, lo, hi, block, floa...  12.6 us
    pallas_call x7, Pallas kernels, dmap_blocks(): pl.pallas_call(functools.partial(dmap_kernel, rows, step, len(ds)), in_sp...  12.3 us
    ppermute x16, starting transfers between devices, shards(): mid[t] = lax.ppermute(part[t], 'gene', MIDDLE)  12 us
  transfers between devices with their start and end apart: 67, of which 21 were waited for; matrix products, arithmetic and copies ran while one was open for 1% of the time, Pallas kernels for 31%

profile of v2, /device:TPU:0, one launch (start us, length us, event | category | flops | bytes accessed | tf_op | source)
XLA Modules:
  0.0 287.8 jit_solution(6939811373172720502)
XLA Ops:
  19.5 7.5 %softmax.1 = (f32[1,128]{1,0:T(1,128)S(1)}, f32[24,512]{1,0:T(8,128)S(1)}, f32[11264,128]{1,0:T(8,128)}) custom-call(f32[11264,128]{1,0:T(8,128)S(1)} %copy-done.7), custom_call_target="tpu_custom_call" | custom-call | flops 1 | bytes 1 | tf_op jit(solution)/shard_map/softmax/pallas_call | solution.py:137
  40.9 5.1 %collective-permute-done.5.refs_0_.refs_2_.refs_4_ = f32[1408,128]{1,0:T(8,128)S(1)} collective-permute-done((f32[1408,128]{1,0:T(8,128)S(1)}, f32[1408,128]{1,0:T(8,128)S(1)}, u32[]{:S(2)}, u32[]{:S(2)}) %collective-permute-start.5) | collective-permute-done | bytes 720928 | tf_op jit(solution)/shard_map/ppermute | solution.py:562
  47.4 4.4 %collective-permute-done.4.refs_0_.refs_1_ = f32[1408,128]{1,0:T(8,128)S(1)} collective-permute-done((f32[1408,128]{1,0:T(8,128)S(1)}, f32[1408,128]{1,0:T(8,128)S(1)}, u32[]{:S(2)}, u32[]{:S(2)}) %collective-permute-start.4) | collective-permute-done | bytes 720928 | tf_op jit(solution)/shard_map/ppermute | solution.py:559
  55.9 5.1 %collective-permute-done.10.refs_0_.refs_6_.refs_4_ = f32[1408,128]{1,0:T(8,128)S(1)} collective-permute-done((f32[1408,128]{1,0:T(8,128)S(1)}, f32[1408,128]{1,0:T(8,128)S(1)}, u32[]{:S(2)}, u32[]{:S(2)}) %collective-permute-start.10) | collective-permute-done | bytes 720928 | tf_op jit(solution)/shard_map/ppermute | solution.py:562
  63.9 8.4 %collective-permute-done.11.refs_3_ = f32[152,512]{1,0:T(8,128)S(1)} collective-permute-done((f32[152,512]{1,0:T(8,128)S(1)}, f32[152,512]{1,0:T(8,128)S(1)}, u32[]{:S(2)}, u32[]{:S(2)}) %collective-permute-start.11) | collective-permute-done | bytes 311328 | tf_op jit(solution)/shard_map/ppermute | solution.py:559
  101.6 3.0 %ratio.4 = (f32[11264,128]{1,0:T(8,128)}, f32[11264,128]{1,0:T(8,128)}, f32[8,128]{1,0:T(8,128)S(1)}, f32[8,128]{1,0:T(8,128)}) custom-call(f32[24,512]{1,0:T(8,128)S(1)} %get-tuple-element.370.refs_0_, f32[22,512]{1,0:T(8,128)S(1)} %reshape.28.refs_1_, f32[1,128]{1,0:T(1,128)S(1)} %get-tuple-element.283.refs_5_.refs_9_.refs_2_, ...), custom_call_target="tpu_custom_call", output_to_operand_aliasing={{0}: (3, {})} | custom-call | flops 1 | bytes 1 | tf_op jit(solution)/shard_map/ratio/pallas_call | solution.py:419
  110.0 3.5 %ratio.5 = (f32[11264,128]{1,0:T(8,128)}, f32[11264,128]{1,0:T(8,128)}, f32[8,128]{1,0:T(8,128)S(1)}, f32[8,128]{1,0:T(8,128)}) custom-call(f32[24,512]{1,0:T(8,128)S(1)} %get-tuple-element.370.refs_0_, f32[22,512]{1,0:T(8,128)S(1)} %reshape.28.refs_1_, ...), custom_call_target="tpu_custom_call", output_to_operand_aliasing={{0}: (3, {}), {1}: (4, {})} | custom-call | flops 1 | bytes 1 | tf_op jit(solution)/shard_map/ratio/pallas_call | solution.py:419
  120.6 3.9 %collective-permute-start.24 = (f32[704,128]{1,0:T(8,128)S(1)}, f32[704,128]{1,0:T(8,128)S(1)}, u32[]{:S(2)}, u32[]{:S(2)}) collective-permute-start(f32[704,128]{1,0:T(8,128)S(1)} %copy-done.28), channel_id=1, source_target_pairs={{0,1},{1,0},{2,3},{3,2},{4,5},{5,4},{6,7},{7,6},{8,9},{9,8},{10,11... | collective-permute-start | bytes 1081352 | tf_op jit(solution)/shard_map/ppermute | solution.py:710
  127.9 3.4 %ratio.6 = (f32[11264,128]{1,0:T(8,128)}, f32[11264,128]{1,0:T(8,128)}, f32[8,128]{1,0:T(8,128)S(1)}, f32[8,128]{1,0:T(8,128)}) custom-call(f32[24,512]{1,0:T(8,128)S(1)} %get-tuple-element.370.refs_0_, f32[22,512]{1,0:T(8,128)S(1)} %reshape.28.refs_1_, ...), custom_call_target="tpu_custom_call", output_to_operand_aliasing={{0}: (3, {}), {1}: (4, {})} | custom-call | flops 1 | bytes 1 | tf_op jit(solution)/shard_map/ratio/pallas_call | solution.py:419
  134.5 4.2 %collective-permute-start.27 = (f32[704,128]{1,0:T(8,128)S(1)}, f32[704,128]{1,0:T(8,128)S(1)}, u32[]{:S(2)}, u32[]{:S(2)}) collective-permute-start(f32[704,128]{1,0:T(8,128)S(1)} %get-tuple-element.367), channel_id=1, source_target_pairs={{0,1},{1,0},{2,3},{3,2},{4,5},{5,4},{6,7},{7,6},{8,9},{9,8},{10,11... | collective-permute-start | bytes 1081352 | tf_op jit(solution)/shard_map/ppermute | solution.py:710
  143.2 3.4 %collective-permute-start.32 = (f32[704,128]{1,0:T(8,128)S(1)}, f32[704,128]{1,0:T(8,128)S(1)}, u32[]{:S(2)}, u32[]{:S(2)}) collective-permute-start(f32[704,128]{1,0:T(8,128)S(1)} %get-tuple-element.383), channel_id=1, source_target_pairs={{0,1},{1,0},{2,3},{3,2},{4,5},{5,4},{6,7},{7,6},{8,9},{9,8},{10,11... | collective-permute-start | bytes 1081352 | tf_op jit(solution)/shard_map/ppermute | solution.py:710
  150.7 5.1 %collective-permute-start.36 = (f32[704,128]{1,0:T(8,128)S(1)}, f32[704,128]{1,0:T(8,128)S(1)}, u32[]{:S(2)}, u32[]{:S(2)}) collective-permute-start(f32[704,128]{1,0:T(8,128)S(1)} %get-tuple-element.403), channel_id=1, source_target_pairs={{0,1},{1,0},{2,3},{3,2},{4,5},{5,4},{6,7},{7,6},{8,9},{9,8},{10,11... | collective-permute-start | bytes 1081352 | tf_op jit(solution)/shard_map/ppermute | solution.py:710
  163.8 3.7 %collective-permute-start.38 = (f32[704,128]{1,0:T(8,128)S(1)}, f32[704,128]{1,0:T(8,128)S(1)}, u32[]{:S(2)}, u32[]{:S(2)}) collective-permute-start(f32[704,128]{1,0:T(8,128)S(1)} %get-tuple-element.406), channel_id=1, source_target_pairs={{0,1},{1,0},{2,3},{3,2},{4,5},{5,4},{6,7},{7,6},{8,9},{9,8},{10,11... | collective-permute-start | bytes 1081352 | tf_op jit(solution)/shard_map/ppermute | solution.py:710
  170.4 2.9 final.12
  174.6 7.0 %collective-permute-done.35.b_ref = f32[8,128]{1,0:T(8,128)S(1)} collective-permute-done((f32[8,128]{1,0:T(8,128)S(1)}, f32[8,128]{1,0:T(8,128)S(1)}, u32[]{:S(2)}, u32[]{:S(2)}) %collective-permute-start.35) | collective-permute-done | bytes 4128 | tf_op jit(solution)/shard_map/ppermute | solution.py:562
  193.4 3.6 %collective-permute-start.49 = (f32[704,128]{1,0:T(8,128)S(1)}, f32[704,128]{1,0:T(8,128)S(1)}, u32[]{:S(2)}, u32[]{:S(2)}) collective-permute-start(f32[704,128]{1,0:T(8,128)S(1)} %get-tuple-element.454), channel_id=1, source_target_pairs={{0,1},{1,0},{2,3},{3,2},{4,5},{5,4},{6,7},{7,6},{8,9},{9,8},{10,11... | collective-permute-start | bytes 1081352 | tf_op jit(solution)/shard_map/ppermute | solution.py:710
  198.5 8.8 %collective-permute-done.40.b_ref = f32[8,128]{1,0:T(8,128)S(1)} collective-permute-done((f32[8,128]{1,0:T(8,128)S(1)}, f32[8,128]{1,0:T(8,128)S(1)}, u32[]{:S(2)}, u32[]{:S(2)}) %collective-permute-start.40) | collective-permute-done | bytes 4128 | tf_op jit(solution)/shard_map/ppermute | solution.py:562
  208.2 3.9 %collective-permute-start.52 = (f32[704,128]{1,0:T(8,128)S(1)}, f32[704,128]{1,0:T(8,128)S(1)}, u32[]{:S(2)}, u32[]{:S(2)}) collective-permute-start(f32[704,128]{1,0:T(8,128)S(1)} %get-tuple-element.472), channel_id=1, source_target_pairs={{0,1},{1,0},{2,3},{3,2},{4,5},{5,4},{6,7},{7,6},{8,9},{9,8},{10,11... | collective-permute-start | bytes 1081352 | tf_op jit(solution)/shard_map/ppermute | solution.py:710
  216.5 3.3 %collective-permute-start.54 = (f32[704,128]{1,0:T(8,128)S(1)}, f32[704,128]{1,0:T(8,128)S(1)}, u32[]{:S(2)}, u32[]{:S(2)}) collective-permute-start(f32[704,128]{1,0:T(8,128)S(1)} %get-tuple-element.479), channel_id=1, source_target_pairs={{0,1},{1,0},{2,3},{3,2},{4,5},{5,4},{6,7},{7,6},{8,9},{9,8},{10,11... | collective-permute-start | bytes 1081352 | tf_op jit(solution)/shard_map/ppermute | solution.py:710
  225.2 2.9 final.17
  229.9 5.5 %collective-permute-start.59 = (f32[704,128]{1,0:T(8,128)S(1)}, f32[704,128]{1,0:T(8,128)S(1)}, u32[]{:S(2)}, u32[]{:S(2)}) collective-permute-start(f32[704,128]{1,0:T(8,128)S(1)} %get-tuple-element.502), channel_id=1, source_target_pairs={{0,1},{1,0},{2,3},{3,2},{4,5},{5,4},{6,7},{7,6},{8,9},{9,8},{10,11... | collective-permute-start | bytes 1081352 | tf_op jit(solution)/shard_map/ppermute | solution.py:710
  247.2 8.0 %collective-permute-start.66 = (f32[704,128]{1,0:T(8,128)S(1)}, f32[704,128]{1,0:T(8,128)S(1)}, u32[]{:S(2)}, u32[]{:S(2)}) collective-permute-start(f32[704,128]{1,0:T(8,128)S(1)} %add.126.refs_3_), channel_id=1, source_target_pairs={{0,1},{1,0},{2,3},{3,2},{4,5},{5,4},{6,7},{7,6},{8,9},{9,8},{10,11... | collective-permute-start | bytes 1081352 | tf_op jit(solution)/shard_map/ppermute | solution.py:710
  255.3 10.2 %collective-permute-start.62 = (f32[704,128]{1,0:T(8,128)S(1)}, f32[704,128]{1,0:T(8,128)S(1)}, u32[]{:S(2)}, u32[]{:S(2)}) collective-permute-start(f32[704,128]{1,0:T(8,128)S(1)} %add.130.refs_1_), channel_id=1, source_target_pairs={{0,1},{1,0},{2,3},{3,2},{4,5},{5,4},{6,7},{7,6},{8,9},{9,8},{10,11... | collective-permute-start | bytes 1081352 | tf_op jit(solution)/shard_map/ppermute | solution.py:710
  274.4 5.0 %egrad.5 = f32[1408,512]{1,0:T(8,128)} custom-call(s32[26]{0:T(128)S(1)} %stack.107.at_ref, f32[2816,128]{1,0:T(8,128)S(1)} %copy-done.9, f32[1408,128]{1,0:T(8,128)S(1)} %copy-done.23, f32[1408,128]{1,0:T(8,128)S(1)} %copy-done.25, f32[1408,128]{1,0:T(8,128)S(1)} %copy-done.15, f32[1408,128]{1,0:T(8,128)S(1)} %copy-done.13, ...), custom_call_target="tpu_custom_call" | custom-call | flops 1 | bytes 1 | tf_op jit(solution)/shard_map/egrad/pallas_call | solution.py:358
  (263 shorter events, 157.0 us)
Async XLA Ops:
  0.6 29.5 %collective-permute-start.3 = (f32[1408,512]{1,0:T(8,128)}, f32[1408,512]{1,0:T(8,128)}, u32[]{:S(2)}, u32[]{:S(2)}) collective-permute-start(f32[1408,512]{1,0:T(8,128)} %x_ref), channel_id=1, source_target_pairs={{0,4},{4,0},{8,12},{12,8},{16,20},{20,16},{24,28},{28,24},{1,5},{5... | collective-permute-start | bytes 8650760 | tf_op jit(solution)/shard_map/ppermute | solution.py:559
  17.9 20.1 %collective-permute-start.6 = (f32[1408,128]{1,0:T(8,128)S(1)}, f32[1408,128]{1,0:T(8,128)S(1)}, u32[]{:S(2)}, u32[]{:S(2)}) collective-permute-start(f32[1408,128]{1,0:T(8,128)S(1)} %get-tuple-element.297), channel_id=1, source_target_pairs={{0,24},{4,28},{8,16},{12,20},{16,8},{20,12},{24,0},{28,4},{1,25},{... | collective-permute-start | bytes 2162696 | tf_op jit(solution)/shard_map/ppermute | solution.py:559
  27.0 19.0 %collective-permute-start.5 = (f32[1408,128]{1,0:T(8,128)S(1)}, f32[1408,128]{1,0:T(8,128)S(1)}, u32[]{:S(2)}, u32[]{:S(2)}) collective-permute-start(f32[1408,128]{1,0:T(8,128)S(1)} %join.1), channel_id=1, source_target_pairs={{0,1},{1,0},{2,3},{3,2},{4,5},{5,4},{6,7},{7,6},{8,9},{9,8},{10,11... | collective-permute-start | bytes 2162696 | tf_op jit(solution)/shard_map/ppermute | solution.py:562
  28.7 23.2 %collective-permute-start.4 = (f32[1408,128]{1,0:T(8,128)S(1)}, f32[1408,128]{1,0:T(8,128)S(1)}, u32[]{:S(2)}, u32[]{:S(2)}) collective-permute-start(f32[1408,128]{1,0:T(8,128)S(1)} %get-tuple-element.292), channel_id=1, source_target_pairs={{0,8},{4,12},{8,0},{12,4},{16,24},{20,28},{24,16},{28,20},{1,9},{5... | collective-permute-start | bytes 2162696 | tf_op jit(solution)/shard_map/ppermute | solution.py:559
  30.2 23.7 %collective-permute-start.8 = (f32[1408,128]{1,0:T(8,128)S(1)}, f32[1408,128]{1,0:T(8,128)S(1)}, u32[]{:S(2)}, u32[]{:S(2)}) collective-permute-start(f32[1408,128]{1,0:T(8,128)S(1)} %get-tuple-element.306), channel_id=1, source_target_pairs={{0,16},{4,20},{8,24},{12,28},{16,0},{20,4},{24,8},{28,12},{1,17},{... | collective-permute-start | bytes 2162696 | tf_op jit(solution)/shard_map/ppermute | solution.py:559
  38.0 23.0 %collective-permute-start.10 = (f32[1408,128]{1,0:T(8,128)S(1)}, f32[1408,128]{1,0:T(8,128)S(1)}, u32[]{:S(2)}, u32[]{:S(2)}) collective-permute-start(f32[1408,128]{1,0:T(8,128)S(1)} %collective-permute-done.6.refs_0_.refs_5_.refs_3_), channel_id=1, source_target_pairs={{0,1},{1,0},{2,3},{3,2},{4,5},{5,4},{6,7},{7,6},{8,9},{9,8},{10,11... | collective-permute-start | bytes 2162696 | tf_op jit(solution)/shard_map/ppermute | solution.py:562
  87.6 17.0 %collective-permute-start.22 = (f32[704,128]{1,0:T(8,128)}, f32[704,128]{1,0:T(8,128)}, u32[]{:S(2)}, u32[]{:S(2)}) collective-permute-start(f32[704,128]{1,0:T(8,128)} %dmap.7.a_ref), channel_id=1, source_target_pairs={{0,1},{1,0},{2,3},{3,2},{4,5},{5,4},{6,7},{7,6},{8,9},{9,8},{10,11... | collective-permute-start | bytes 1081352 | tf_op jit(solution)/shard_map/ppermute | solution.py:710
  96.3 17.2 %collective-permute-start.21 = (f32[704,128]{1,0:T(8,128)}, f32[704,128]{1,0:T(8,128)}, u32[]{:S(2)}, u32[]{:S(2)}) collective-permute-start(f32[704,128]{1,0:T(8,128)} %dmap.8.a_ref), channel_id=1, source_target_pairs={{0,1},{1,0},{2,3},{3,2},{4,5},{5,4},{6,7},{7,6},{8,9},{9,8},{10,11... | collective-permute-start | bytes 1081352 | tf_op jit(solution)/shard_map/ppermute | solution.py:710
  120.1 30.6 %collective-permute-start.34 = (f32[2112,128]{1,0:T(8,128)S(1)}, f32[2112,128]{1,0:T(8,128)S(1)}, u32[]{:S(2)}, u32[]{:S(2)}) collective-permute-start(f32[2112,128]{1,0:T(8,128)S(1)} %get-tuple-element.357), channel_id=1, source_target_pairs={{0,8},{4,12},{8,0},{12,4},{16,24},{20,28},{24,16},{28,20},{1,9},{5... | collective-permute-start | bytes 3244040 | tf_op jit(solution)/shard_map/ppermute | solution.py:559
  125.2 35.2 %collective-permute-start.31 = (f32[2112,128]{1,0:T(8,128)S(1)}, f32[2112,128]{1,0:T(8,128)S(1)}, u32[]{:S(2)}, u32[]{:S(2)}) collective-permute-start(f32[2112,128]{1,0:T(8,128)S(1)} %get-tuple-element.382), channel_id=1, source_target_pairs={{0,16},{4,20},{8,24},{12,28},{16,0},{20,4},{24,8},{28,12},{1,17},{... | collective-permute-start | bytes 3244040 | tf_op jit(solution)/shard_map/ppermute | solution.py:559
  125.8 15.6 %collective-permute-start.29 = (f32[704,128]{1,0:T(8,128)S(1)}, f32[704,128]{1,0:T(8,128)S(1)}, u32[]{:S(2)}, u32[]{:S(2)}) collective-permute-start(f32[704,128]{1,0:T(8,128)S(1)} %get-tuple-element.368), channel_id=1, source_target_pairs={{0,1},{1,0},{2,3},{3,2},{4,5},{5,4},{6,7},{7,6},{8,9},{9,8},{10,11... | collective-permute-start | bytes 1081352 | tf_op jit(solution)/shard_map/ppermute | solution.py:710
  143.2 15.5 %collective-permute-start.32 = (f32[704,128]{1,0:T(8,128)S(1)}, f32[704,128]{1,0:T(8,128)S(1)}, u32[]{:S(2)}, u32[]{:S(2)}) collective-permute-start(f32[704,128]{1,0:T(8,128)S(1)} %get-tuple-element.383), channel_id=1, source_target_pairs={{0,1},{1,0},{2,3},{3,2},{4,5},{5,4},{6,7},{7,6},{8,9},{9,8},{10,11... | collective-permute-start | bytes 1081352 | tf_op jit(solution)/shard_map/ppermute | solution.py:710
  150.7 16.8 %collective-permute-start.36 = (f32[704,128]{1,0:T(8,128)S(1)}, f32[704,128]{1,0:T(8,128)S(1)}, u32[]{:S(2)}, u32[]{:S(2)}) collective-permute-start(f32[704,128]{1,0:T(8,128)S(1)} %get-tuple-element.403), channel_id=1, source_target_pairs={{0,1},{1,0},{2,3},{3,2},{4,5},{5,4},{6,7},{7,6},{8,9},{9,8},{10,11... | collective-permute-start | bytes 1081352 | tf_op jit(solution)/shard_map/ppermute | solution.py:710
  163.0 45.1 %collective-permute-start.48 = (f32[2816,128]{1,0:T(8,128)S(1)}, f32[2816,128]{1,0:T(8,128)S(1)}, u32[]{:S(2)}, u32[]{:S(2)}) collective-permute-start(f32[2816,128]{1,0:T(8,128)S(1)} %dmap.13), channel_id=1, source_target_pairs={{0,24},{4,28},{8,16},{12,20},{16,8},{20,12},{24,0},{28,4},{1,25},{... | collective-permute-start | bytes 4325384 | tf_op jit(solution)/shard_map/ppermute | solution.py:559
  168.4 18.1 %collective-permute-start.41 = (f32[704,128]{1,0:T(8,128)S(1)}, f32[704,128]{1,0:T(8,128)S(1)}, u32[]{:S(2)}, u32[]{:S(2)}) collective-permute-start(f32[704,128]{1,0:T(8,128)S(1)} %get-tuple-element.426), channel_id=1, source_target_pairs={{0,1},{1,0},{2,3},{3,2},{4,5},{5,4},{6,7},{7,6},{8,9},{9,8},{10,11... | collective-permute-start | bytes 1081352 | tf_op jit(solution)/shard_map/ppermute | solution.py:710
  187.3 20.0 %collective-permute-start.46 = (f32[704,128]{1,0:T(8,128)S(1)}, f32[704,128]{1,0:T(8,128)S(1)}, u32[]{:S(2)}, u32[]{:S(2)}) collective-permute-start(f32[704,128]{1,0:T(8,128)S(1)} %get-tuple-element.451), channel_id=1, source_target_pairs={{0,1},{1,0},{2,3},{3,2},{4,5},{5,4},{6,7},{7,6},{8,9},{9,8},{10,11... | collective-permute-start | bytes 1081352 | tf_op jit(solution)/shard_map/ppermute | solution.py:710
  192.6 15.5 %collective-permute-start.50 = (f32[704,128]{1,0:T(8,128)S(1)}, f32[704,128]{1,0:T(8,128)S(1)}, u32[]{:S(2)}, u32[]{:S(2)}) collective-permute-start(f32[704,128]{1,0:T(8,128)S(1)} %add.117.s_ref), channel_id=1, source_target_pairs={{1,2},{2,1},{5,6},{6,5},{9,10},{10,9},{13,14},{14,13},{17,18},{18,... | collective-permute-start | bytes 1081352 | tf_op jit(solution)/shard_map/ppermute | solution.py:787
  193.4 21.1 %collective-permute-start.49 = (f32[704,128]{1,0:T(8,128)S(1)}, f32[704,128]{1,0:T(8,128)S(1)}, u32[]{:S(2)}, u32[]{:S(2)}) collective-permute-start(f32[704,128]{1,0:T(8,128)S(1)} %get-tuple-element.454), channel_id=1, source_target_pairs={{0,1},{1,0},{2,3},{3,2},{4,5},{5,4},{6,7},{7,6},{8,9},{9,8},{10,11... | collective-permute-start | bytes 1081352 | tf_op jit(solution)/shard_map/ppermute | solution.py:710
  208.2 14.1 %collective-permute-start.52 = (f32[704,128]{1,0:T(8,128)S(1)}, f32[704,128]{1,0:T(8,128)S(1)}, u32[]{:S(2)}, u32[]{:S(2)}) collective-permute-start(f32[704,128]{1,0:T(8,128)S(1)} %get-tuple-element.472), channel_id=1, source_target_pairs={{0,1},{1,0},{2,3},{3,2},{4,5},{5,4},{6,7},{7,6},{8,9},{9,8},{10,11... | collective-permute-start | bytes 1081352 | tf_op jit(solution)/shard_map/ppermute | solution.py:710
  240.1 34.2 %collective-permute-start.64 = (f32[704,512]{1,0:T(8,128)S(1)}, f32[704,512]{1,0:T(8,128)S(1)}, u32[]{:S(2)}, u32[]{:S(2)}) collective-permute-start(f32[704,512]{1,0:T(8,128)S(1)} %egrad.3), channel_id=1, source_target_pairs={{0,4},{4,0},{8,12},{12,8},{16,20},{20,16},{24,28},{28,24},{1,5},{5... | collective-permute-start | bytes 4325384 | tf_op jit(solution)/shard_map/ppermute | solution.py:559
  246.4 28.0 %collective-permute-start.65 = (f32[704,512]{1,0:T(8,128)S(1)}, f32[704,512]{1,0:T(8,128)S(1)}, u32[]{:S(2)}, u32[]{:S(2)}) collective-permute-start(f32[704,512]{1,0:T(8,128)S(1)} %egrad.4), channel_id=1, source_target_pairs={{0,4},{4,0},{8,12},{12,8},{16,20},{20,16},{24,28},{28,24},{1,5},{5... | collective-permute-start | bytes 4325384 | tf_op jit(solution)/shard_map/ppermute | solution.py:559
  247.2 24.4 %collective-permute-start.66 = (f32[704,128]{1,0:T(8,128)S(1)}, f32[704,128]{1,0:T(8,128)S(1)}, u32[]{:S(2)}, u32[]{:S(2)}) collective-permute-start(f32[704,128]{1,0:T(8,128)S(1)} %add.126.refs_3_), channel_id=1, source_target_pairs={{0,1},{1,0},{2,3},{3,2},{4,5},{5,4},{6,7},{7,6},{8,9},{9,8},{10,11... | collective-permute-start | bytes 1081352 | tf_op jit(solution)/shard_map/ppermute | solution.py:710
  255.1 24.3 %collective-permute-start.63 = (f32[704,128]{1,0:T(8,128)S(1)}, f32[704,128]{1,0:T(8,128)S(1)}, u32[]{:S(2)}, u32[]{:S(2)}) collective-permute-start(f32[704,128]{1,0:T(8,128)S(1)} %add.128.refs_1_), channel_id=1, source_target_pairs={{0,1},{1,0},{2,3},{3,2},{4,5},{5,4},{6,7},{7,6},{8,9},{9,8},{10,11... | collective-permute-start | bytes 1081352 | tf_op jit(solution)/shard_map/ppermute | solution.py:710
  255.3 26.7 %collective-permute-start.62 = (f32[704,128]{1,0:T(8,128)S(1)}, f32[704,128]{1,0:T(8,128)S(1)}, u32[]{:S(2)}, u32[]{:S(2)}) collective-permute-start(f32[704,128]{1,0:T(8,128)S(1)} %add.130.refs_1_), channel_id=1, source_target_pairs={{0,1},{1,0},{2,3},{3,2},{4,5},{5,4},{6,7},{7,6},{8,9},{9,8},{10,11... | collective-permute-start | bytes 1081352 | tf_op jit(solution)/shard_map/ppermute | solution.py:710
  (76 other events, 776.5 us)

commit v3 on v2

--- a/solution.py
+++ b/solution.py
@@ -102,45 +102,51 @@
     )(at, logits)
 
 
-def softmax_kernel(spots, scale, l_ref, inv_ref, cell_ref, o_ref, buffer, sem):
+def by_cell_rows(ref, count, step):
+    genes = ref.shape[1]
+    return jnp.concatenate([ref[:count, :], ref[count : 2 * count, : step - genes]], axis=1)
+
+
+def softmax_kernel(spots, scale, step, l_ref, inv_ref, cell_ref, o_ref, buffer, sem):
     cells, width = l_ref.shape
     genes = cell_ref.shape[1]
-    n_q = cells // genes
+    count = cells // step
 
     def column(k, total):
-        e = jnp.exp(l_ref[at_rows(k, genes), :])
-        return total + jnp.sum(e.reshape(genes // 8, 8, width), axis=0)
-
-    total = lax.fori_loop(0, n_q, column, jnp.zeros((8, width), F32))
+        e = jnp.exp(l_ref[at_rows(k, step), :])
+        return total + jnp.sum(e.reshape(step // 8, 8, width), axis=0)
+
+    total = lax.fori_loop(0, count, column, jnp.zeros((8, width), F32))
     inv = 1.0 / jnp.sum(total, axis=0, keepdims=True)
     inv_ref[...] = inv
     ones = jnp.ones((16, width), BF16)
 
     def row(k, square):
-        e = jnp.exp(l_ref[at_rows(k, genes), :])
+        e = jnp.exp(l_ref[at_rows(k, step), :])
         share = e * inv
-        buffer[at_rows(k, genes), :] = e * scale
-        pltpu.make_async_copy(buffer.at[at_rows(k, genes)], o_ref.at[at_rows(k, genes)], sem).start()
+        buffer[at_rows(k, step), :] = e * scale
+        pltpu.make_async_copy(buffer.at[at_rows(k, step)], o_ref.at[at_rows(k, step)], sem).start()
         high, low = split(share)
         sums = [lax.dot_general(ones, x, (((1,), (1,)), ((), ())), preferred_element_type=F32) for x in (high, low)]
-        cell_ref[pl.ds(k, 1), :] = (sums[0] + sums[1])[0:1, :] * (1.0 / spots)
-        return square + jnp.sum((share * share).reshape(genes // 8, 8, width), axis=0)
-
-    square = lax.fori_loop(0, n_q, row, jnp.zeros((8, width), F32))
-    cell_ref[n_q:, :] = jnp.full((cell_ref.shape[0] - n_q, genes), jnp.sum(square), F32)
+        sums = (sums[0] + sums[1])[0:1, :] * (1.0 / spots)
+        cell_ref[pl.ds(k, 1), :] = sums[:, :genes]
+        cell_ref[pl.ds(count + k, 1), : step - genes] = sums[:, genes:]
+        return square + jnp.sum((share * share).reshape(step // 8, 8, width), axis=0)
+
+    square = lax.fori_loop(0, count, row, jnp.zeros((8, width), F32))
+    cell_ref[count:, step - genes :] = jnp.full((count, 2 * genes - step), jnp.sum(square), F32)
     pltpu.make_async_copy(buffer, o_ref, sem).wait()
 
 
-def softmax_sums(spots, genes, logits):
+def softmax_sums(spots, genes, step, logits):
     cells, width = logits.shape
-    n_cells = -(-(cells // genes + 1) // 8) * 8
-    return pl.pallas_call(
-        functools.partial(softmax_kernel, spots, float(cells)),
+    return pl.pallas_call(
+        functools.partial(softmax_kernel, spots, float(cells), step),
         in_specs=[VMEM],
         out_specs=(VMEM, VMEM, HBM),
         out_shape=(
             jax.ShapeDtypeStruct((1, width), F32),
-            jax.ShapeDtypeStruct((n_cells, genes), F32),
+            jax.ShapeDtypeStruct((2 * cells // step, genes), F32),
             pltpu.HBM((cells, width), F32),
         ),
         scratch_shapes=[pltpu.VMEM((cells, width), F32), pltpu.SemaphoreType.DMA],
@@ -260,7 +266,7 @@
     )(*parts, by_cell, inv, spatial, ids, mask, counts)
 
 
-def dpred_kernel(spots, share_blk, share_gene, *refs):
+def dpred_kernel(spots, share_gene, *refs):
     wides, spot, refs = refs[:2], refs[2][...] + refs[3][...], refs[4:]
     pred_ref, spatial_ref, ids_ref, mask_ref, counts_ref, inv_ref, d_ref, tot_ref = refs
     weights = weights_of(mask_ref, counts_ref)
@@ -286,17 +292,17 @@
     own = exact(jnp.ones((8, genes), F32), pred * dpred, ((1,), (1,))) * inv
     d_ref[LANES:, :] = wide([own] * (genes // LANES))
     rows = lax.broadcasted_iota(jnp.int32, (8, LANES), 0)
-    tot = jnp.where(rows == 0, jnp.sum(weights * a * inv_g) * share_blk, 0.0)
-    tot = jnp.where(rows == 1, jnp.sum(e * inv_s) * share_gene, tot)
-    tot = jnp.where(rows == 2, jnp.sum(f) * share_gene, tot)
-    tot_ref[...] = jnp.where(rows == 3, wsum, tot)
-
-
-def dpred_scaled(spots, share_blk, share_gene, *args):
+    tot = jnp.where(rows == 0, jnp.sum(weights * a * inv_g), 0.0)
+    tot = jnp.where(rows == 1, jnp.sum(e * inv_s), tot)
+    tot = jnp.where(rows == 2, jnp.sum(f), tot)
+    tot_ref[...] = jnp.where(rows == 3, wsum * share_gene, tot)
+
+
+def dpred_scaled(spots, share_gene, *args):
     spatial = args[5]
     width, genes = spatial.shape
     return pl.pallas_call(
-        functools.partial(dpred_kernel, spots, share_blk, share_gene),
+        functools.partial(dpred_kernel, spots, share_gene),
         out_shape=(
             jax.ShapeDtypeStruct((width + 8, genes), F32),
             jax.ShapeDtypeStruct((8, width), F32),
@@ -308,7 +314,7 @@
 
 
 def dmap_kernel(rows, step, n, *refs):
-    xs, ds, outs = refs[:4], refs[4 : 4 + n], refs[4 + n :]
+    xs, ds, outs = refs[:4], refs[4 : 4 + n], refs[-n:]
     parts = [split(d[:LANES, :]) for d in ds]
     d = tuple(jnp.concatenate([part[i] for part in parts], axis=0) for i in range(2))
     own = jnp.concatenate([d[LANES : LANES + 1, :LANES] for d in ds], axis=1)
@@ -317,20 +323,23 @@
         value = three((xs[2 * x][here, :], xs[2 * x + 1][here, :]), d, ((1,), (1,))) - own
         for i, out in enumerate(outs):
             out[at_rows(k, step), :] = value[:, i * LANES : (i + 1) * LANES]
-
-
-def dmap_blocks(rows, step, ds, xs):
+    if len(refs) > 4 + 2 * n:
+        for out in outs:
+            out[len(rows) * step :, :] = refs[4 + n][...]
+
+
+def dmap_blocks(rows, step, ds, xs, tail=()):
     genes = ds[0].shape[1]
     width = ds[0].shape[0] - 8
     return pl.pallas_call(
         functools.partial(dmap_kernel, rows, step, len(ds)),
-        in_specs=[VMEM] * (4 + len(ds)),
+        in_specs=[VMEM] * (4 + len(ds) + len(tail)),
         out_specs=(VMEM,) * len(ds),
-        out_shape=(jax.ShapeDtypeStruct((len(rows) * step, width), F32),) * len(ds),
+        out_shape=(jax.ShapeDtypeStruct((len(rows) * step + 8 * len(tail), width), F32),) * len(ds),
         name="dmap",
         compiler_params=room(16),
         cost_estimate=cost(0, 0),
-    )(*xs, *ds)
+    )(*xs, *ds, *tail)
 
 
 def egrad_kernel(scale, ks, step, wheres, n_add, at_ref, *refs):
@@ -366,72 +375,51 @@
     )(at, *ls, *ds, *adds)
 
 
-def ratio_kernel(spots, lo, hi, block, scale, *refs):
-    more = lo > 0
-    cell_ref, density_ref, inv_ref, a_ref = refs[:4]
-    b_ref, given_ref = refs[4:6] if more else (None, None)
-    _, o_ref, sum_ref, kl_ref, a, b, sems = refs[-7:]
+def ratio_kernel(spots, scale, cell_ref, density_ref, inv_ref, a_ref, _, ratio_ref, sum_ref, kl_ref, a, sems):
     inv = inv_ref[...]
-    width = a_ref.shape[1]
-    n_q, genes = density_ref.shape
-    step = block * genes
+    count, step = density_ref.shape
 
     def load(k):
-        return pltpu.make_async_copy(a_ref.at[at_rows(lo + k, step)], a.at[at_rows(k, step)], sems.at[k])
-
-    def store(k):
-        return pltpu.make_async_copy(b.at[at_rows(k, step)], o_ref.at[at_rows(lo + k, step)], sems.at[hi - lo + k])
-
-    for k in range(hi - lo):
+        return pltpu.make_async_copy(a_ref.at[at_rows(k, step)], a.at[at_rows(k, step)], sems.at[k])
+
+    for k in range(count):
         load(k).start()
     density = density_ref[...]
     target = density / jnp.sum(density)
-    q = cell_ref[:n_q, :]
+    q = by_cell_rows(cell_ref, count, step)
     ratios = target / q / spots
+    ratio_ref[...] = ratios
     kl_ref[...] = jnp.full(kl_ref.shape, jnp.sum(target * (jnp.log(target) - jnp.log(q))))
-    rows = lax.broadcasted_iota(jnp.int32, (16, genes), 0)
-    ones = (lax.broadcasted_iota(jnp.int32, (16, LANES), 0) < 3).astype(BF16)
-    total = jnp.zeros((8, width), F32)
-    for k in range(hi - lo):
+    rows = lax.broadcasted_iota(jnp.int32, (16, step), 0)
+    total = jnp.zeros((1, LANES), F32)
+    for k in range(count):
         load(k).wait()
-        for i in range(block):
-            ratio = ratios[(lo + k) * block + i : (lo + k) * block + i + 1, :]
-            high = ratio.astype(BF16).astype(F32)
-            mid = (ratio - high).astype(BF16).astype(F32)
-            terms = jnp.where(rows == 0, high, jnp.where(rows == 1, mid, jnp.where(rows == 2, ratio - high - mid, 0.0)))
-            column = lax.dot_general(terms.astype(BF16), ones, (((0,), (0,)), ((), ())), preferred_element_type=F32)
-            here = at_rows(k * block + i, genes)
-            product = a[here, :] * column
-            total = total + jnp.sum(product.reshape(genes // 8, 8, width), axis=0)
-            b[here, :] = -product * inv
-        store(k).start()
-    total = jnp.sum(total, axis=0, keepdims=True) * (inv * inv * (1.0 / scale))
-    sum_ref[...] = jnp.broadcast_to(total, sum_ref.shape) + (given_ref[...] if more else 0.0)
-    for k in range(hi - lo):
-        store(k).wait()
-
-
-def ratio_part(spots, lo, hi, block, by_cell, density, inv, a, b=None, given=None):
+        high, low = split(ratios[k : k + 1, :])
+        lhs = jnp.where(rows == 0, high.astype(F32), jnp.where(rows == 1, low.astype(F32), 0.0)).astype(BF16)
+        for part in split(a[at_rows(k, step), :]):
+            sums = lax.dot_general(lhs, part, (((1,), (0,)), ((), ())), preferred_element_type=F32)
+            total = total + (sums[0:1, :] + sums[1:2, :])
+    sum_ref[...] = jnp.broadcast_to(total * (inv * inv * (1.0 / scale)), sum_ref.shape)
+
+
+def ratio_part(spots, by_cell, density, inv, a):
     cells, width = a.shape
-    genes = density.shape[1]
-    size = (hi - lo) * block * genes
-    more = () if b is None else (b, given)
-    return pl.pallas_call(
-        functools.partial(ratio_kernel, spots, lo, hi, block, float(cells)),
-        in_specs=[VMEM, VMEM, VMEM, HBM] + [HBM, VMEM][: len(more)],
-        out_specs=(HBM, HBM, VMEM, VMEM),
+    return pl.pallas_call(
+        functools.partial(ratio_kernel, spots, float(cells)),
+        in_specs=[VMEM, VMEM, VMEM, HBM],
+        out_specs=(HBM, VMEM, VMEM, VMEM),
         out_shape=(
             pltpu.HBM((cells, width), F32),
-            pltpu.HBM((cells, width), F32),
+            jax.ShapeDtypeStruct(density.shape, F32),
             jax.ShapeDtypeStruct((8, width), F32),
             jax.ShapeDtypeStruct((8, width), F32),
         ),
-        scratch_shapes=[pltpu.VMEM((size, width), F32)] * 2 + [pltpu.SemaphoreType.DMA((2 * (hi - lo),))],
-        input_output_aliases={3: 0, 4: 1} if more else {3: 0},
+        scratch_shapes=[pltpu.VMEM((cells, width), F32), pltpu.SemaphoreType.DMA((density.shape[0],))],
+        input_output_aliases={3: 0},
         name="ratio",
-        compiler_params=room(2 * (size * width * 4 // 2**20 + 1) + 6),
-        cost_estimate=cost(0, 0),
-    )(by_cell, density, inv, a, *more)
+        compiler_params=room(big(a) + 8),
+        cost_estimate=cost(0, 0),
+    )(by_cell, density, inv, a)
 
 
 def join_kernel(a_ref, b_ref, o_ref):
@@ -453,19 +441,23 @@
 
 
 def add_kernel(first, a_ref, b_ref, o_ref):
-    o_ref[...] = a_ref[pl.ds(first, o_ref.shape[0]), :] + b_ref[...]
-
-
-def add(first, a, b):
+    o_ref[...] = a_ref[pl.ds(first, o_ref.shape[0]), :] + b_ref[: o_ref.shape[0], :]
+
+
+def add(first, rows, a, b):
     return pl.pallas_call(
         functools.partial(add_kernel, first),
         in_specs=[VMEM, VMEM],
         out_specs=VMEM,
-        out_shape=jax.ShapeDtypeStruct(b.shape, F32),
+        out_shape=jax.ShapeDtypeStruct((rows, b.shape[1]), F32),
         name="add",
         compiler_params=room(8),
         cost_estimate=cost(0, 0),
     )(a, b)
+
+
+def plus(a, b):
+    return add(0, a.shape[0], a, b)
 
 
 def add_all_kernel(*refs):
@@ -487,15 +479,17 @@
     )(*arrays)
 
 
-def next_kernel(first, at_ref, s_ref, y_ref, b_ref, t_ref, o_ref):
+def next_kernel(first, step, end_ref, s_ref, y_ref, b_ref, t_ref, o_ref):
     total = s_ref[...] + y_ref[...]
     t_ref[...] = total
-    o_ref[...] = jnp.where(at_ref[0] == 1, b_ref[pl.ds(first, o_ref.shape[0]), :], total)
-
-
-def next_piece(first, end, s, y, b):
-    return pl.pallas_call(
-        functools.partial(next_kernel, first),
+    o_ref[:step, :] = jnp.where(end_ref[0] == 1, b_ref[pl.ds(first, step), :], total[:step, :])
+    if total.shape[0] > step:
+        o_ref[step:, :] = total[step:, :]
+
+
+def next_piece(first, step, end, s, y, b):
+    return pl.pallas_call(
+        functools.partial(next_kernel, first, step),
         in_specs=[SMEM, VMEM, VMEM, VMEM],
         out_specs=(VMEM, VMEM),
         out_shape=(jax.ShapeDtypeStruct(s.shape, F32), jax.ShapeDtypeStruct(s.shape, F32)),
@@ -506,42 +500,75 @@
 
 
 def final_kernel(place, n, end_ref, at_ref, *refs):
-    rxs, ss, (sum_ref, a_ref, g_ref, _, o_ref, a, b, sems) = refs[:n], refs[n : 2 * n], refs[2 * n :]
+    rx_ref, s_ref, (ratio_ref, sum_ref, inv_ref, a_ref, _, _, o_ref, a, b, sems) = refs[0], refs[1], refs[2:]
     step = a.shape[0] // n
     here = at_rows(at_ref[place], step, n)
-    loads = [
-        pltpu.make_async_copy(a_ref.at[here], a, sems.at[0]),
-        pltpu.make_async_copy(g_ref.at[here], b, sems.at[1]),
-    ]
-    for load in loads:
-        load.start()
-    for load in loads:
-        load.wait()
+    load = pltpu.make_async_copy(a_ref.at[here], a, sems.at[n])
+    load.start()
+    rows = lax.broadcasted_iota(jnp.int32, (16, step), 0)
+    ones = (lax.broadcasted_iota(jnp.int32, (16, LANES), 0) < 3).astype(BF16)
     stores = []
     for k in range(n):
-        there, rows = at_rows(at_ref[place] + k, step), at_rows(k, step)
-        whole = jnp.where(end_ref[0] == 1, rxs[k][...], ss[k][...])
-        b[rows, :] = a[rows, :] * (whole + sum_ref[0:1, :]) + b[rows, :]
-        stores.append(pltpu.make_async_copy(b.at[rows], o_ref.at[there], sems.at[2 + k]))
+        at, here = at_ref[place] + k, at_rows(k, step)
+        ratio = ratio_ref[pl.ds(at, 1), :]
+        high = ratio.astype(BF16).astype(F32)
+        mid = (ratio - high).astype(BF16).astype(F32)
+        terms = jnp.where(rows == 0, high, jnp.where(rows == 1, mid, jnp.where(rows == 2, ratio - high - mid, 0.0)))
+        column = lax.dot_general(terms.astype(BF16), ones, (((0,), (0,)), ((), ())), preferred_element_type=F32)
+        whole = jnp.where(end_ref[0] == 1, rx_ref[here, :], s_ref[here, :])
+        value = whole + (sum_ref[0:1, :] - column * inv_ref[...])
+        if k == 0:
+            load.wait()
+        b[here, :] = a[here, :] * value
+        stores.append(pltpu.make_async_copy(b.at[here], o_ref.at[at_rows(at, step)], sems.at[k]))
         stores[-1].start()
     for store in stores:
         store.wait()
 
 
-def final_pieces(place, end, at, rxs, ss, ratio_sum, a, grad):
-    step, width = ss[0].shape
-    n = len(ss)
+def final_piece(step, n, place, end, at, rx, s, ratio, ratio_sum, inv, a, grad):
+    width = s.shape[1]
     return pl.pallas_call(
         functools.partial(final_kernel, place, n),
-        in_specs=[SMEM, SMEM] + [VMEM] * (2 * n + 1) + [HBM, HBM],
+        in_specs=[SMEM, SMEM] + [VMEM] * 5 + [HBM, HBM],
         out_specs=(HBM, HBM),
         out_shape=(pltpu.HBM(a.shape, F32), pltpu.HBM(grad.shape, F32)),
-        scratch_shapes=[pltpu.VMEM((n * step, width), F32)] * 2 + [pltpu.SemaphoreType.DMA((2 + n,))],
-        input_output_aliases={3 + 2 * n: 0, 4 + 2 * n: 1},
+        scratch_shapes=[pltpu.VMEM((n * step, width), F32)] * 2 + [pltpu.SemaphoreType.DMA((1 + n,))],
+        input_output_aliases={7: 0, 8: 1},
         name="final",
-        compiler_params=room(8),
-        cost_estimate=cost(0, 0),
-    )(end, at, *rxs, *ss, ratio_sum, a, grad)
+        compiler_params=room(10),
+        cost_estimate=cost(0, 0),
+    )(end, at, rx, s, ratio, ratio_sum, inv, a, grad)
+
+
+def blank(shape):
+    return pl.pallas_call(lambda o_ref: None, out_specs=HBM, out_shape=pltpu.HBM(shape, F32), name="blank")()
+
+
+def scalars_kernel(n, cells, spots, step, end_ref, *refs):
+    sums = [refs[k][-8:, :] for k in range(n)]
+    rx_ref, s_ref, q_ref, kl_ref, loss_ref, map_ref, pred_ref = refs[n:]
+    while len(sums) > 1:
+        sums = [a + b for a, b in zip(sums[::2], sums[1::2], strict=True)]
+    by_gene = jnp.where(end_ref[0] == 1, rx_ref[step:, :], s_ref[step:, :])
+    cosine, fitted, wsum, scos = by_gene[0:1, :], sums[0][2:3, :], by_gene[3:4, :], sums[0][1:2, :]
+    loss = -cosine / wsum - scos / spots + kl_ref[0:1, :]
+    rms_map = jnp.sqrt(q_ref[q_ref.shape[0] - 1 :, q_ref.shape[1] - LANES :] / (cells * spots))
+    rms_pred = jnp.sqrt(fitted / (spots * GENES))
+    for ref, value in zip((loss_ref, map_ref, pred_ref), (loss, rms_map, rms_pred), strict=True):
+        ref[0, 0] = jnp.max(value)
+
+
+def scalar_results(n, cells, spots, step, end, *args):
+    return pl.pallas_call(
+        functools.partial(scalars_kernel, n, cells, spots, step),
+        in_specs=[SMEM] + [VMEM] * len(args),
+        out_specs=(SMEM,) * 3,
+        out_shape=(jax.ShapeDtypeStruct((1, 1), F32),) * 3,
+        name="scalars",
+        compiler_params=room(24),
+        cost_estimate=cost(0, 0),
+    )(end, *args)
 
 
 def shards(logits, expression, spatial, density, gene_mask, gene_counts, slide_ids):
@@ -593,22 +620,25 @@
         return order(lambda l: cut_blocks(layout, half, at, l), (logits,))
 
     if n_blk == 8 and n_gene == 4:
-        near3, near5 = cuts(mine(3), mine(5))
+        near3, near5 = order(
+            lambda l: [lax.dynamic_slice_in_dim(l, (me ^ r) * rows + side * half, half, 0) for r in (3, 5)], (logits,)
+        )
         sent[3], sent[5] = swap(near3, 2), swap(near5, 4)
         own_x = order(lambda x: parts_of(x, half), (expression,))
         both, near2, near4, stay = cuts(mine(6) + mine(7), whole(2), whole(4), whole(0) + whole(1))
         passed[3] = across(order(join, (sent[3], sent[5])), 1)
         sent[6], sent[2], sent[4] = swap(order.here(both), 6), swap(order.here(near2), 2), swap(order.here(near4), 4)
-        inv, by_cell, scale = order(functools.partial(softmax_sums, spots, genes), (logits,))
+        inv, by_cell, scale = order(functools.partial(softmax_sums, spots, genes, half), (logits,))
         other_x = order(lambda x: parts_of(x, half), (other,))
-        by_cell = order(functools.partial(add, 0), (by_cell, swap(by_cell, 1)))
         (acc0,) = add_pred(((0, 0, 0, 0, 0, 0, 2), (0, 0, 0, 2, 1, 0, 2)), 1, (stay,))
         acc2, acc4 = add_pred(((0, 0, 0, 0, 1, [0], 1), (1, 0, 1, 0, 1, [0], 1)), 2, (sent[3], sent[5]))
+        cell_moved = swap(order.here(by_cell), 1)
         passed[6] = across(order.here(sent[6]), 1)
         (acc6,) = add_pred(((0, 0, 0, 0, 0, [0], 1), (0, 0, 0, 1, 1, [0], 1)), 1, (sent[6],))
         acc2, acc4 = add_pred(
             ((0, 1, 0, 0, 1, [1], 1), (1, 2, 0, 1, 1, [1], 1)), 2, (passed[3],), (acc2, acc4)
         )
+        by_cell = order(plus, (by_cell, cell_moved))
         (acc2,) = add_pred(((0, 1, 0, 0, 0, 0, 2),), 1, (sent[2],), (acc2,), (by_cell,))
         moved = {2: swap(acc2, 2)}
         (acc4,) = add_pred(((0, 1, 0, 0, 0, 0, 2),), 1, (sent[4],), (acc4,), (by_cell,))
@@ -624,8 +654,8 @@
             7: ((sent[6], passed[6]), (1, 1)),
         }
     else:
-        inv, by_cell, scale = order(functools.partial(softmax_sums, spots, genes), (logits,))
-        by_cell = order(functools.partial(add, 0), (by_cell, swap(by_cell, 1)))
+        inv, by_cell, scale = order(functools.partial(softmax_sums, spots, genes, half), (logits,))
+        by_cell = order(plus, (by_cell, swap(by_cell, 1)))
         own_x = order(lambda x: parts_of(x, half), (expression,))
         other_x = order(lambda x: parts_of(x, half), (other,))
         (stay,) = cuts(whole(0) + whole(1))
@@ -644,52 +674,44 @@
     pred, wide, spot, by_cell = order(
         functools.partial(pred_sums, len(parts)), parts, (by_cell, inv, spatial, *constants)
     )
-    density = density.reshape(n_q, genes)
-    blocks = n_q // 2
-    state = {"scale": scale}
-
-    def kl_part(lo, hi):
-        more = (state["grad"], state["ratio_sum"]) if lo else ()
-        state["scale"], state["grad"], state["ratio_sum"], state["kl"] = order(
-            functools.partial(ratio_part, spots, lo, hi, 2), (by_cell,), (density, inv, state["scale"], *more)
-        )
+    density = density.reshape(cells // half, half)
+    state = {"scale": scale, "grad": blank((cells, width))}
 
     spot_moved = across(spot, 1)
     m = 1
     while 2 * m < n_blk:
-        wide = order(functools.partial(add, 0), (wide, swap(wide, m)))
+        wide = order(plus, (wide, swap(wide, m)))
         m *= 2
         if m == 2:
             spot = order(add_all, (spot, spot_moved))
             spot_moved = across(spot, 2)
     wide_moved = swap(wide, m)
     grad, tot = order(
-        functools.partial(dpred_scaled, spots, 1.0 / n_blk, 1.0 / n_gene),
+        functools.partial(dpred_scaled, spots, 1.0 / n_gene),
         (wide, wide_moved, spot, spot_moved),
         (pred, spatial, *constants, inv),
     )
-    grads = {0: grad}
+    grads, back, tails = {0: grad}, {}, {}
     for m in far:
         grads[m] = swap(grad, m)
-    back = {}
-
-    def dmap(ms, rows, wait=()):
+
+    def dmap(ms, steps, wait=(), tail=()):
         outs = order(
-            lambda *a: dmap_blocks(rows, half, a[: len(ms)], a[len(ms) :]),
+            lambda *a: dmap_blocks(steps, half, a[: len(ms)], a[len(ms) : len(ms) + 4], a[len(ms) + 4 :]),
             [grads[m] for m in ms],
-            (*own_x, *other_x),
+            (*own_x, *other_x, *tail),
             wait,
         )
         for m, d in zip(ms, outs, strict=True):
             d = swap(d, m) if m else d
-            for k, (odd, first) in enumerate(rows):
-                back[m + odd, first] = (d, k * half)
-
-    if n_blk == 8:
-        places = [(0, 0), (0, 1), (1, 0), (1, 1), (2, 0), (4, 0), (2, 1), (4, 1)]
-        places += [(r, k) for r in (3, 5, 6, 7) for k in range(2)]
-    else:
-        places = [(r, k) for m in [0, *far] for r in (m, m + 1) for k in range(2)]
+            for k, (odd, first) in enumerate(steps):
+                if first == 0:
+                    back[m + odd] = (d, k * half)
+            if tail:
+                tails[m] = d
+
+    own_rows, other_rows = ((0, 0), (0, 1)), ((1, 0), (1, 1))
+    places = [0, 1, 2, 4, 3, 5, 6, 7] if n_blk == 8 else [r for m in [0, *far] for r in (m, m + 1)]
     count, lag = len(places), 3
     part, total_of, mid, got = {}, {}, {}, {}
     end = jnp.reshape((plane == 0) | (plane == n_gene - 1), (1,)).astype(jnp.int32)
@@ -700,22 +722,20 @@
         if t < count:
             block, first = back[places[t]]
         if t < lag:
-            buffer = block if block.shape[0] == half else order(lambda b: b[first : first + half], (block,))
+            buffer = block if block.shape[0] <= rows + 8 else block[first : first + rows]
         elif t < count:
             total_of[t - lag], buffer = order(
-                lambda s, y, b: next_piece(first, end, s, y, b), (part[t - lag], mid[t - lag], block)
+                lambda s, y, b: next_piece(first, rows, end, s, y, b), (part[t - lag], mid[t - lag], block)
             )
         else:
-            buffer = total_of[t - lag] = order(functools.partial(add, 0), (part[t - lag], mid[t - lag]))
+            buffer = total_of[t - lag] = order(plus, (part[t - lag], mid[t - lag]))
         got[t] = lax.ppermute(buffer, "gene", PAIR)
 
-    def finish(*ts):
-        r, k = places[ts[0]]
-        n = len(ts)
+    def finish(t):
         state["scale"], state["grad"] = order(
-            lambda *a: final_pieces(2 + 2 * r + k, end, at, a[:n], a[n : 2 * n], *a[2 * n :]),
-            (*[got[t + lag] for t in ts], *[total_of[t] for t in ts]),
-            (state["ratio_sum"], state["scale"], state["grad"]),
+            functools.partial(final_piece, half, 2, 2 + 2 * places[t], end, at),
+            (got[t + lag], total_of[t]),
+            (state["ratio"], state["ratio_sum"], inv, state["scale"], state["grad"]),
         )
 
     def expr_part(odd, ks, adds=()):
@@ -729,69 +749,49 @@
             (*ls, *[grads[m] for m in far]),
         )
 
-    all_rows = ((0, 0), (0, 1), (1, 0), (1, 1))
-
     def extra(t):
         if t == 0:
-            dmap((0,), ((1, 0),))
-            dmap((0,), ((1, 1),))
+            tails[0] = order(plus, (tot, tot_moved))
             if n_blk == 8:
-                dmap((2, 4), ((0, 0),))
+                dmap((2, 4), own_rows)
             else:
                 for m in far:
-                    dmap((m,), all_rows)
+                    dmap((m,), own_rows + other_rows, (), (tails[0],))
+            state["scale"], state["ratio"], state["ratio_sum"], state["kl"] = order(
+                functools.partial(ratio_part, spots), (by_cell,), (density, inv, state["scale"])
+            )
         if n_blk == 8:
-            if t == 2:
-                dmap((2, 4), ((0, 1), (1, 0), (1, 1)), (back[2, 0][0], back[4, 0][0]))
-            if t == 6:
-                dmap((6,), all_rows, (back[3, 0][0], back[5, 0][0]))
-        if 0 <= t < 4:
-            kl_part(blocks * t // 4, blocks * (t + 1) // 4)
-        for step, (move, m) in enumerate(stages):
-            if t == first_stage + 2 * step + 2:
-                state["tot"] = order(functools.partial(add, 0), (state.get("tot", tot), state["moving"]))
-        for step, (move, m) in enumerate(stages):
-            if t == first_stage + 2 * step:
-                state["moving"] = move(order.here(state.get("tot", tot)), m)
-        if t in (15, 16):
-            state["swapped", t] = swap(expr_part(1, (t - 15,)), 1)
-        if t == 18:
-            state["expr"] = expr_part(0, (0, 1), (state["swapped", 15], state["swapped", 16]))
-
-    stages, m = [(across, 1), (across, 2)], 1
-    while m < n_blk:
-        stages.append((swap, m))
-        m *= 2
-    first_stage = 16 - 2 * len(stages)
-
-    def joins(t):
-        return t + 1 < count and places[t][0] == places[t + 1][0] and places[t][1] == 0
-
-    ready = []
-    dmap((0,), ((0, 0),))
+            if t == 1:
+                dmap((2, 4), other_rows, (back[2][0], back[4][0]), (tails[0],))
+            if t == 3:
+                dmap((6,), own_rows + other_rows, (back[3][0], back[5][0]), (tails[0],))
+        if t in (count - 2, count - 1):
+            state["swapped", t - count] = swap(expr_part(1, (t - count + 2,)), 1)
+        if t == count:
+            state["scalars"] = order(
+                functools.partial(scalar_results, n_blk // 2, cells, spots, rows, end),
+                (*[tails[m] for m in range(0, n_blk, 2)], got[lag], total_of[0], by_cell),
+                (state["kl"],),
+            )
+        if t == count + 1:
+            state["expr"] = expr_part(0, (0, 1), (state["swapped", -2], state["swapped", -1]))
+
+    dmap((0,), own_rows, (), (tot,))
     send(0)
-    dmap((0,), ((0, 1),))
+    dmap((0,), other_rows)
+    tot_moved = swap(order.here(tot), 1)
     for t in range(count + lag):
         send(t + 1)
         extra(t)
-        done = t - lag
-        if done > 0:
-            ready.append(done - 1)
-        while ready and (len(ready) > 1 or places[ready[0]][1] == 0 and not joins(ready[0])):
-            n = 2 if joins(ready[0]) else 1
-            finish(*ready[:n])
-            del ready[:n]
+        if t > lag:
+            finish(t - lag - 1)
         if t < count:
             block, first = back[places[t]]
-            part[t] = order(functools.partial(add, first), (block, got[t]))
+            size = block.shape[0] if t == 0 else rows
+            part[t] = order(functools.partial(add, first, size), (block, got[t]))
             mid[t] = lax.ppermute(part[t], "gene", MIDDLE)
-    for t in (*ready, count - 1):
-        finish(t)
-
-    sums = state["tot"]
-    loss = -sums[0, 0] / tot[3, 0] - sums[1, 0] / spots + state["kl"][0, 0]
-    rms_map = jnp.sqrt(by_cell[n_q, 0] / (cells * spots))
-    rms_pred = jnp.sqrt(sums[2, 0] / (spots * GENES))
+    finish(count - 1)
+    loss, rms_map, rms_pred = (x[0, 0] for x in state["scalars"])
     return (loss, state["grad"], state["expr"], rms_map, rms_pred)
 
 

time: 289 us -> 275 us (0.952)
  starting transfers between devices: 109 us -> 99 us
  between operations: 9.19 us -> 1.59 us
  local copies, waits for them, and re-layouts: 11 us -> 17.3 us
    ppermute x6 -> x4, waiting for transfers between devices: 29.9 us -> 3.96 us  [across(): return lax.ppermute(x, 'gene', [(i, i ^ m) for i in range(n_gene)])]
    ppermute x19 -> x11, waiting for transfers between devices: 7.09 us -> 20.2 us  [send(): got[t] = lax.ppermute(buffer, 'gene', PAIR)]
    ppermute x26 -> x24, waiting for transfers between devices: 22.5 us -> 34.9 us  [swap(): return lax.ppermute(x, 'blk', [(i, i ^ m) for i in range(n_blk)])]
    pallas_call x30 -> x18, Pallas kernels: 54.6 us -> 44.8 us  [the longest x8 23.1 us: final_piece(): pl.pallas_call(functools.partial(final_kernel, place, n), in_specs=[SMEM,...]
    ppermute x19 -> x11, starting transfers between devices: 66.8 us -> 59.3 us  [send(): got[t] = lax.ppermute(buffer, 'gene', PAIR)]
    unnamed x66 -> x100, local copies, waits for them, and re-layouts: 8.01 us -> 15.1 us
    pallas_call x27 -> x15, Pallas kernels: 5.79 us -> 10.5 us  [add(): pl.pallas_call(functools.partial(add_kernel, first), in_specs=[VMEM, VMEM...]
    ppermute x16 -> x8, starting transfers between devices: 12 us -> 7.84 us  [shards(): mid[t] = lax.ppermute(part[t], 'gene', MIDDLE)]
  transfers between devices with their start and end apart: 67 -> 47, of which waited for: 21 -> 17; matrix products, arithmetic and copies ran while one was open for 1% -> 1% of each run, Pallas kernels for 31% -> 33%
where the time goes in v3:
time: 275 us; the launch traced here: 274 us
  starting transfers between devices  99 us (36%)
  Pallas kernels  96.7 us (35%)
  waiting for transfers between devices  59.1 us (21%)
  local copies, waits for them, and re-layouts  17.3 us (6%)
    ppermute x11, starting transfers between devices, send(): got[t] = lax.ppermute(buffer, 'gene', PAIR)  59.3 us
    ppermute x24, waiting for transfers between devices, swap(): return lax.ppermute(x, 'blk', [(i, i ^ m) for i in range(n_blk)])  34.9 us
    ppermute x24, starting transfers between devices, swap(): return lax.ppermute(x, 'blk', [(i, i ^ m) for i in range(n_blk)])  24.6 us
    pallas_call x8, Pallas kernels, final_piece(): pl.pallas_call(functools.partial(final_kernel, place, n), in_specs=[SMEM,...  23.1 us
    ppermute x11, waiting for transfers between devices, send(): got[t] = lax.ppermute(buffer, 'gene', PAIR)  20.2 us
    unnamed x100, local copies, waits for them, and re-layouts  15.1 us
    pallas_call x5, Pallas kernels, dmap_blocks(): pl.pallas_call(functools.partial(dmap_kernel, rows, step, len(ds)), in_sp...  13.7 us
    pallas_call x7, Pallas kernels, pred_sums_of(): pl.pallas_call(functools.partial(pred_kernel, jobs, n_acc, step, len(tail...  10.7 us
  transfers between devices with their start and end apart: 47, of which 17 were waited for; matrix products, arithmetic and copies ran while one was open for 1% of the time, Pallas kernels for 33%

profile of v3, /device:TPU:0, one launch (start us, length us, event | category | flops | bytes accessed | tf_op | source)
XLA Modules:
  0.0 273.7 jit_solution(17160610717869484432)
XLA Ops:
  22.2 6.8 %softmax.1 = (f32[1,128]{1,0:T(1,128)S(1)}, f32[32,512]{1,0:T(8,128)S(1)}, f32[11264,128]{1,0:T(8,128)}) custom-call(f32[11264,128]{1,0:T(8,128)S(1)} %copy-done.7), custom_call_target="tpu_custom_call" | custom-call | flops 1 | bytes 1 | tf_op jit(solution)/shard_map/softmax/pallas_call | solution.py:143
  42.0 9.4 %collective-permute-done.3.refs_0_.refs_1_ = f32[1408,128]{1,0:T(8,128)S(1)} collective-permute-done((f32[1408,128]{1,0:T(8,128)S(1)}, f32[1408,128]{1,0:T(8,128)S(1)}, u32[]{:S(2)}, u32[]{:S(2)}) %collective-permute-start.3) | collective-permute-done | bytes 720928 | tf_op jit(solution)/shard_map/ppermute | solution.py:586
  59.4 3.7 %collective-permute-done.7.refs_1_ = f32[160,512]{1,0:T(8,128)S(1)} collective-permute-done((f32[160,512]{1,0:T(8,128)S(1)}, f32[160,512]{1,0:T(8,128)S(1)}, u32[]{:S(2)}, u32[]{:S(2)}) %collective-permute-start.7) | collective-permute-done | bytes 327712 | tf_op jit(solution)/shard_map/ppermute | solution.py:586
  63.1 7.1 %collective-permute-done.9.refs_2_ = f32[160,512]{1,0:T(8,128)S(1)} collective-permute-done((f32[160,512]{1,0:T(8,128)S(1)}, f32[160,512]{1,0:T(8,128)S(1)}, u32[]{:S(2)}, u32[]{:S(2)}) %collective-permute-start.9) | collective-permute-done | bytes 327712 | tf_op jit(solution)/shard_map/ppermute | solution.py:586
  101.5 4.2 %ratio.1 = (f32[11264,128]{1,0:T(8,128)}, f32[16,704]{1,0:T(8,128)S(1)}, f32[8,128]{1,0:T(8,128)S(1)}, f32[8,128]{1,0:T(8,128)S(1)}) custom-call(f32[32,512]{1,0:T(8,128)S(1)} %copy-done.42, f32[16,704]{1,0:T(8,128)S(1)} %reshape.16.density_ref, f32[1,128]{1,0:T(1,128)S(1)} %get-tuple-element.185.refs_5_.refs_9_.inv_ref.refs_4_, ...), custom_call_target="tpu_custom_call", output_to_operand_aliasing={{0}: (3, {})} | custom-call | flops 1 | bytes 1 | tf_op jit(solution)/shard_map/ratio/pallas_call | solution.py:407
  108.6 5.6 %collective-permute-done.21.a_ref = f32[1408,128]{1,0:T(8,128)} collective-permute-done((f32[1408,128]{1,0:T(8,128)}, f32[1408,128]{1,0:T(8,128)}, u32[]{:S(2)}, u32[]{:S(2)}) %collective-permute-start.21) | collective-permute-done | bytes 720928 | tf_op jit(solution)/shard_map/ppermute | solution.py:586
  130.6 5.2 %collective-permute-done.28.b_ref = f32[1408,128]{1,0:T(8,128)} collective-permute-done((f32[1408,128]{1,0:T(8,128)}, f32[1408,128]{1,0:T(8,128)}, u32[]{:S(2)}, u32[]{:S(2)}) %collective-permute-start.28) | collective-permute-done | bytes 720928 | tf_op jit(solution)/shard_map/ppermute | solution.py:732
  140.6 4.5 %dmap.9 = f32[2824,128]{1,0:T(8,128)} custom-call(bf16[1408,512]{1,0:T(8,128)(2,1)S(1)} %get-tuple-element.178.refs_1_.refs_2_.refs_0_, bf16[1408,512]{1,0:T(8,128)(2,1)S(1)} %get-tuple-element.189.refs_2_.refs_3_.refs_1_, bf16[1408,512]{1,0:T(8,128)(2,1)S(1)} %copy-done.2, bf16[1408,512]{1,0:T(8,128)(2,1)S(1)} %copy-done.5, ...), custom_call_target="tpu_custom_call" | custom-call | flops 1 | bytes 1 | tf_op jit(solution)/shard_map/dmap/pallas_call | solution.py:334
  147.8 6.9 %collective-permute-start.33 = (f32[1408,128]{1,0:T(8,128)}, f32[1408,128]{1,0:T(8,128)}, u32[]{:S(2)}, u32[]{:S(2)}) collective-permute-start(f32[1408,128]{1,0:T(8,128)} %get-tuple-element.270), channel_id=1, source_target_pairs={{0,1},{1,0},{2,3},{3,2},{4,5},{5,4},{6,7},{7,6},{8,9},{9,8},{10,11... | collective-permute-start | bytes 2162696 | tf_op jit(solution)/shard_map/ppermute | solution.py:732
  162.3 12.9 %collective-permute-start.36 = (f32[1408,128]{1,0:T(8,128)}, f32[1408,128]{1,0:T(8,128)}, u32[]{:S(2)}, u32[]{:S(2)}) collective-permute-start(f32[1408,128]{1,0:T(8,128)} %get-tuple-element.286), channel_id=1, source_target_pairs={{0,1},{1,0},{2,3},{3,2},{4,5},{5,4},{6,7},{7,6},{8,9},{9,8},{10,11... | collective-permute-start | bytes 2162696 | tf_op jit(solution)/shard_map/ppermute | solution.py:732
  177.4 2.7 final.8
  183.8 5.5 %collective-permute-start.35 = (f32[1408,128]{1,0:T(8,128)S(1)}, f32[1408,128]{1,0:T(8,128)S(1)}, u32[]{:S(2)}, u32[]{:S(2)}) collective-permute-start(f32[1408,128]{1,0:T(8,128)S(1)} %get-tuple-element.285), channel_id=1, source_target_pairs={{0,1},{1,0},{2,3},{3,2},{4,5},{5,4},{6,7},{7,6},{8,9},{9,8},{10,11... | collective-permute-start | bytes 2162696 | tf_op jit(solution)/shard_map/ppermute | solution.py:732
  189.3 3.4 %final.9 = (f32[11264,128]{1,0:T(8,128)}, f32[11264,128]{1,0:T(8,128)}) custom-call(s32[1]{0:T(128)} %bitcast.end_ref, s32[26]{0:T(128)S(1)} %stack.107.at_ref, f32[1408,128]{1,0:T(8,128)} %collective-permute-done.33.b_ref.refs_0_, f32[1408,128]{1,0:T(8,128)S(1)} %copy-done.38, ...), custom_call_target="tpu_custom_call", output_to_operand_aliasing={{0}: (7, {}), {1}: (8, {})} | custom-call | flops 1 | bytes 1 | tf_op jit(solution)/shard_map/final/pallas_call | solution.py:531
  195.4 7.9 %collective-permute-start.39 = (f32[1408,128]{1,0:T(8,128)S(1)}, f32[1408,128]{1,0:T(8,128)S(1)}, u32[]{:S(2)}, u32[]{:S(2)}) collective-permute-start(f32[1408,128]{1,0:T(8,128)S(1)} %get-tuple-element.305), channel_id=1, source_target_pairs={{0,1},{1,0},{2,3},{3,2},{4,5},{5,4},{6,7},{7,6},{8,9},{9,8},{10,11... | collective-permute-start | bytes 2162696 | tf_op jit(solution)/shard_map/ppermute | solution.py:732
  205.9 3.3 %final.10 = (f32[11264,128]{1,0:T(8,128)}, f32[11264,128]{1,0:T(8,128)}) custom-call(s32[1]{0:T(128)} %bitcast.end_ref, s32[26]{0:T(128)S(1)} %stack.107.at_ref, f32[1408,128]{1,0:T(8,128)} %collective-permute-done.36.b_ref.refs_0_, f32[1408,128]{1,0:T(8,128)S(1)} %copy-done.40, ...), custom_call_target="tpu_custom_call", output_to_operand_aliasing={{0}: (7, {}), {1}: (8, {})} | custom-call | flops 1 | bytes 1 | tf_op jit(solution)/shard_map/final/pallas_call | solution.py:531
  213.0 2.7 final.11
  216.8 6.6 %collective-permute-start.44 = (f32[1408,128]{1,0:T(8,128)S(1)}, f32[1408,128]{1,0:T(8,128)S(1)}, u32[]{:S(2)}, u32[]{:S(2)}) collective-permute-start(f32[1408,128]{1,0:T(8,128)S(1)} %add.111.refs_1_), channel_id=1, source_target_pairs={{0,1},{1,0},{2,3},{3,2},{4,5},{5,4},{6,7},{7,6},{8,9},{9,8},{10,11... | collective-permute-start | bytes 2162696 | tf_op jit(solution)/shard_map/ppermute | solution.py:732
  223.5 6.8 %collective-permute-start.43 = (f32[1408,128]{1,0:T(8,128)S(1)}, f32[1408,128]{1,0:T(8,128)S(1)}, u32[]{:S(2)}, u32[]{:S(2)}) collective-permute-start(f32[1408,128]{1,0:T(8,128)S(1)} %add.113.refs_1_), channel_id=1, source_target_pairs={{0,1},{1,0},{2,3},{3,2},{4,5},{5,4},{6,7},{7,6},{8,9},{9,8},{10,11... | collective-permute-start | bytes 2162696 | tf_op jit(solution)/shard_map/ppermute | solution.py:732
  232.3 2.7 final.12
  235.1 10.2 %collective-permute-start.42 = (f32[1408,128]{1,0:T(8,128)S(1)}, f32[1408,128]{1,0:T(8,128)S(1)}, u32[]{:S(2)}, u32[]{:S(2)}) collective-permute-start(f32[1408,128]{1,0:T(8,128)S(1)} %add.114.refs_1_), channel_id=1, source_target_pairs={{0,1},{1,0},{2,3},{3,2},{4,5},{5,4},{6,7},{7,6},{8,9},{9,8},{10,11... | collective-permute-start | bytes 2162696 | tf_op jit(solution)/shard_map/ppermute | solution.py:732
  245.3 5.0 %egrad.5 = f32[1408,512]{1,0:T(8,128)} custom-call(s32[26]{0:T(128)S(1)} %stack.107.at_ref, f32[2816,128]{1,0:T(8,128)S(1)} %copy-done.9, f32[1408,128]{1,0:T(8,128)S(1)} %copy-done.30, f32[1408,128]{1,0:T(8,128)S(1)} %copy-done.32, f32[1408,128]{1,0:T(8,128)S(1)} %copy-done.15, f32[1408,128]{1,0:T(8,128)S(1)} %copy-done.13, ...), custom_call_target="tpu_custom_call" | custom-call | flops 1 | bytes 1 | tf_op jit(solution)/shard_map/egrad/pallas_call | solution.py:367
  253.0 2.7 %collective-permute-done.43.refs_0_ = f32[1408,128]{1,0:T(8,128)S(1)} collective-permute-done((f32[1408,128]{1,0:T(8,128)S(1)}, f32[1408,128]{1,0:T(8,128)S(1)}, u32[]{:S(2)}, u32[]{:S(2)}) %collective-permute-start.43) | collective-permute-done | bytes 720928 | tf_op jit(solution)/shard_map/ppermute | solution.py:732
  258.5 12.3 %collective-permute-done.42.refs_0_ = f32[1408,128]{1,0:T(8,128)S(1)} collective-permute-done((f32[1408,128]{1,0:T(8,128)S(1)}, f32[1408,128]{1,0:T(8,128)S(1)}, u32[]{:S(2)}, u32[]{:S(2)}) %collective-permute-start.42) | collective-permute-done | bytes 720928 | tf_op jit(solution)/shard_map/ppermute | solution.py:732
  270.8 2.7 final.15
  (227 shorter events, 131.2 us)
Async XLA Ops:
  0.6 28.9 %collective-permute-start = (f32[1408,512]{1,0:T(8,128)}, f32[1408,512]{1,0:T(8,128)}, u32[]{:S(2)}, u32[]{:S(2)}) collective-permute-start(f32[1408,512]{1,0:T(8,128)} %x_ref), channel_id=1, source_target_pairs={{0,4},{4,0},{8,12},{12,8},{16,20},{20,16},{24,28},{28,24},{1,5},{5... | collective-permute-start | bytes 8650760 | tf_op jit(solution)/shard_map/ppermute | solution.py:586
  17.5 20.1 %collective-permute-start.5 = (f32[1408,128]{1,0:T(8,128)S(1)}, f32[1408,128]{1,0:T(8,128)S(1)}, u32[]{:S(2)}, u32[]{:S(2)}) collective-permute-start(f32[1408,128]{1,0:T(8,128)S(1)} %get-tuple-element.197), channel_id=1, source_target_pairs={{0,24},{4,28},{8,16},{12,20},{16,8},{20,12},{24,0},{28,4},{1,25},{... | collective-permute-start | bytes 2162696 | tf_op jit(solution)/shard_map/ppermute | solution.py:586
  19.1 21.5 %collective-permute-start.4 = (f32[1408,128]{1,0:T(8,128)S(1)}, f32[1408,128]{1,0:T(8,128)S(1)}, u32[]{:S(2)}, u32[]{:S(2)}) collective-permute-start(f32[1408,128]{1,0:T(8,128)S(1)} %join.1), channel_id=1, source_target_pairs={{0,1},{1,0},{2,3},{3,2},{4,5},{5,4},{6,7},{7,6},{8,9},{9,8},{10,11... | collective-permute-start | bytes 2162696 | tf_op jit(solution)/shard_map/ppermute | solution.py:589
  20.7 30.8 %collective-permute-start.3 = (f32[1408,128]{1,0:T(8,128)S(1)}, f32[1408,128]{1,0:T(8,128)S(1)}, u32[]{:S(2)}, u32[]{:S(2)}) collective-permute-start(f32[1408,128]{1,0:T(8,128)S(1)} %get-tuple-element.192), channel_id=1, source_target_pairs={{0,8},{4,12},{8,0},{12,4},{16,24},{20,28},{24,16},{28,20},{1,9},{5... | collective-permute-start | bytes 2162696 | tf_op jit(solution)/shard_map/ppermute | solution.py:586
  29.0 24.7 %collective-permute-start.8 = (f32[1408,128]{1,0:T(8,128)S(1)}, f32[1408,128]{1,0:T(8,128)S(1)}, u32[]{:S(2)}, u32[]{:S(2)}) collective-permute-start(f32[1408,128]{1,0:T(8,128)S(1)} %get-tuple-element.210), channel_id=1, source_target_pairs={{0,16},{4,20},{8,24},{12,28},{16,0},{20,4},{24,8},{28,12},{1,17},{... | collective-permute-start | bytes 2162696 | tf_op jit(solution)/shard_map/ppermute | solution.py:586
  37.6 18.1 %collective-permute-start.10 = (f32[1408,128]{1,0:T(8,128)S(1)}, f32[1408,128]{1,0:T(8,128)S(1)}, u32[]{:S(2)}, u32[]{:S(2)}) collective-permute-start(f32[1408,128]{1,0:T(8,128)S(1)} %collective-permute-done.5.refs_0_.refs_5_.refs_3_), channel_id=1, source_target_pairs={{0,1},{1,0},{2,3},{3,2},{4,5},{5,4},{6,7},{7,6},{8,9},{9,8},{10,11... | collective-permute-start | bytes 2162696 | tf_op jit(solution)/shard_map/ppermute | solution.py:589
  85.8 20.5 %collective-permute-start.20 = (f32[1416,128]{1,0:T(8,128)}, f32[1416,128]{1,0:T(8,128)}, u32[]{:S(2)}, u32[]{:S(2)}) collective-permute-start(f32[1416,128]{1,0:T(8,128)} %dmap.5.a_ref), channel_id=1, source_target_pairs={{0,1},{1,0},{2,3},{3,2},{4,5},{5,4},{6,7},{7,6},{8,9},{9,8},{10,11... | collective-permute-start | bytes 2174984 | tf_op jit(solution)/shard_map/ppermute | solution.py:732
  98.4 16.6 %collective-permute-start.22 = (f32[1408,128]{1,0:T(8,128)}, f32[1408,128]{1,0:T(8,128)}, u32[]{:S(2)}, u32[]{:S(2)}) collective-permute-start(f32[1408,128]{1,0:T(8,128)} %get-tuple-element.249), channel_id=1, source_target_pairs={{0,16},{4,20},{8,24},{12,28},{16,0},{20,4},{24,8},{28,12},{1,17},{... | collective-permute-start | bytes 2162696 | tf_op jit(solution)/shard_map/ppermute | solution.py:586
  99.9 19.8 %collective-permute-start.26 = (f32[1408,128]{1,0:T(8,128)}, f32[1408,128]{1,0:T(8,128)}, u32[]{:S(2)}, u32[]{:S(2)}) collective-permute-start(f32[1408,128]{1,0:T(8,128)} %dmap.6.a_ref), channel_id=1, source_target_pairs={{0,1},{1,0},{2,3},{3,2},{4,5},{5,4},{6,7},{7,6},{8,9},{9,8},{10,11... | collective-permute-start | bytes 2162696 | tf_op jit(solution)/shard_map/ppermute | solution.py:732
  117.4 19.8 %collective-permute-start.23 = (f32[1416,128]{1,0:T(8,128)}, f32[1416,128]{1,0:T(8,128)}, u32[]{:S(2)}, u32[]{:S(2)}) collective-permute-start(f32[1416,128]{1,0:T(8,128)} %get-tuple-element.252), channel_id=1, source_target_pairs={{0,8},{4,12},{8,0},{12,4},{16,24},{20,28},{24,16},{28,20},{1,9},{5... | collective-permute-start | bytes 2174984 | tf_op jit(solution)/shard_map/ppermute | solution.py:586
  118.4 22.2 %collective-permute-start.24 = (f32[1416,128]{1,0:T(8,128)}, f32[1416,128]{1,0:T(8,128)}, u32[]{:S(2)}, u32[]{:S(2)}) collective-permute-start(f32[1416,128]{1,0:T(8,128)} %get-tuple-element.253), channel_id=1, source_target_pairs={{0,16},{4,20},{8,24},{12,28},{16,0},{20,4},{24,8},{28,12},{1,17},{... | collective-permute-start | bytes 2174984 | tf_op jit(solution)/shard_map/ppermute | solution.py:586
  135.8 19.0 %collective-permute-start.31 = (f32[1416,128]{1,0:T(8,128)S(1)}, f32[1416,128]{1,0:T(8,128)S(1)}, u32[]{:S(2)}, u32[]{:S(2)}) collective-permute-start(f32[1416,128]{1,0:T(8,128)S(1)} %get-tuple-element.267), channel_id=1, source_target_pairs={{0,1},{1,0},{2,3},{3,2},{4,5},{5,4},{6,7},{7,6},{8,9},{9,8},{10,11... | collective-permute-start | bytes 2174984 | tf_op jit(solution)/shard_map/ppermute | solution.py:732
  145.0 37.3 %collective-permute-start.30 = (f32[2824,128]{1,0:T(8,128)}, f32[2824,128]{1,0:T(8,128)S(1)}, u32[]{:S(2)}, u32[]{:S(2)}) collective-permute-start(f32[2824,128]{1,0:T(8,128)} %dmap.9), channel_id=1, source_target_pairs={{0,24},{4,28},{8,16},{12,20},{16,8},{20,12},{24,0},{28,4},{1,25},{... | collective-permute-start | bytes 4337672 | tf_op jit(solution)/shard_map/ppermute | solution.py:586
  147.8 32.3 %collective-permute-start.33 = (f32[1408,128]{1,0:T(8,128)}, f32[1408,128]{1,0:T(8,128)}, u32[]{:S(2)}, u32[]{:S(2)}) collective-permute-start(f32[1408,128]{1,0:T(8,128)} %get-tuple-element.270), channel_id=1, source_target_pairs={{0,1},{1,0},{2,3},{3,2},{4,5},{5,4},{6,7},{7,6},{8,9},{9,8},{10,11... | collective-permute-start | bytes 2162696 | tf_op jit(solution)/shard_map/ppermute | solution.py:732
  157.7 24.6 %collective-permute-start.32 = (f32[1408,128]{1,0:T(8,128)}, f32[1408,128]{1,0:T(8,128)}, u32[]{:S(2)}, u32[]{:S(2)}) collective-permute-start(f32[1408,128]{1,0:T(8,128)} %add.107.s_ref), channel_id=1, source_target_pairs={{1,2},{2,1},{5,6},{6,5},{9,10},{10,9},{13,14},{14,13},{17,18},{18,... | collective-permute-start | bytes 2162696 | tf_op jit(solution)/shard_map/ppermute | solution.py:792
  162.3 30.5 %collective-permute-start.36 = (f32[1408,128]{1,0:T(8,128)}, f32[1408,128]{1,0:T(8,128)}, u32[]{:S(2)}, u32[]{:S(2)}) collective-permute-start(f32[1408,128]{1,0:T(8,128)} %get-tuple-element.286), channel_id=1, source_target_pairs={{0,1},{1,0},{2,3},{3,2},{4,5},{5,4},{6,7},{7,6},{8,9},{9,8},{10,11... | collective-permute-start | bytes 2162696 | tf_op jit(solution)/shard_map/ppermute | solution.py:732
  183.8 25.3 %collective-permute-start.35 = (f32[1408,128]{1,0:T(8,128)S(1)}, f32[1408,128]{1,0:T(8,128)S(1)}, u32[]{:S(2)}, u32[]{:S(2)}) collective-permute-start(f32[1408,128]{1,0:T(8,128)S(1)} %get-tuple-element.285), channel_id=1, source_target_pairs={{0,1},{1,0},{2,3},{3,2},{4,5},{5,4},{6,7},{7,6},{8,9},{9,8},{10,11... | collective-permute-start | bytes 2162696 | tf_op jit(solution)/shard_map/ppermute | solution.py:732
  195.4 20.4 %collective-permute-start.39 = (f32[1408,128]{1,0:T(8,128)S(1)}, f32[1408,128]{1,0:T(8,128)S(1)}, u32[]{:S(2)}, u32[]{:S(2)}) collective-permute-start(f32[1408,128]{1,0:T(8,128)S(1)} %get-tuple-element.305), channel_id=1, source_target_pairs={{0,1},{1,0},{2,3},{3,2},{4,5},{5,4},{6,7},{7,6},{8,9},{9,8},{10,11... | collective-permute-start | bytes 2162696 | tf_op jit(solution)/shard_map/ppermute | solution.py:732
  205.8 39.5 %collective-permute-start.45 = (f32[704,512]{1,0:T(8,128)S(1)}, f32[704,512]{1,0:T(8,128)S(1)}, u32[]{:S(2)}, u32[]{:S(2)}) collective-permute-start(f32[704,512]{1,0:T(8,128)S(1)} %egrad.3), channel_id=1, source_target_pairs={{0,4},{4,0},{8,12},{12,8},{16,20},{20,16},{24,28},{28,24},{1,5},{5... | collective-permute-start | bytes 4325384 | tf_op jit(solution)/shard_map/ppermute | solution.py:586
  212.5 32.8 %collective-permute-start.46 = (f32[704,512]{1,0:T(8,128)S(1)}, f32[704,512]{1,0:T(8,128)S(1)}, u32[]{:S(2)}, u32[]{:S(2)}) collective-permute-start(f32[704,512]{1,0:T(8,128)S(1)} %egrad.4), channel_id=1, source_target_pairs={{0,4},{4,0},{8,12},{12,8},{16,20},{20,16},{24,28},{28,24},{1,5},{5... | collective-permute-start | bytes 4325384 | tf_op jit(solution)/shard_map/ppermute | solution.py:586
  215.9 19.1 %collective-permute-start.41 = (f32[1408,128]{1,0:T(8,128)S(1)}, f32[1408,128]{1,0:T(8,128)S(1)}, u32[]{:S(2)}, u32[]{:S(2)}) collective-permute-start(f32[1408,128]{1,0:T(8,128)S(1)} %add.112.a_ref), channel_id=1, source_target_pairs={{1,2},{2,1},{5,6},{6,5},{9,10},{10,9},{13,14},{14,13},{17,18},{18,... | collective-permute-start | bytes 2162696 | tf_op jit(solution)/shard_map/ppermute | solution.py:792
  216.8 33.5 %collective-permute-start.44 = (f32[1408,128]{1,0:T(8,128)S(1)}, f32[1408,128]{1,0:T(8,128)S(1)}, u32[]{:S(2)}, u32[]{:S(2)}) collective-permute-start(f32[1408,128]{1,0:T(8,128)S(1)} %add.111.refs_1_), channel_id=1, source_target_pairs={{0,1},{1,0},{2,3},{3,2},{4,5},{5,4},{6,7},{7,6},{8,9},{9,8},{10,11... | collective-permute-start | bytes 2162696 | tf_op jit(solution)/shard_map/ppermute | solution.py:732
  223.5 32.3 %collective-permute-start.43 = (f32[1408,128]{1,0:T(8,128)S(1)}, f32[1408,128]{1,0:T(8,128)S(1)}, u32[]{:S(2)}, u32[]{:S(2)}) collective-permute-start(f32[1408,128]{1,0:T(8,128)S(1)} %add.113.refs_1_), channel_id=1, source_target_pairs={{0,1},{1,0},{2,3},{3,2},{4,5},{5,4},{6,7},{7,6},{8,9},{9,8},{10,11... | collective-permute-start | bytes 2162696 | tf_op jit(solution)/shard_map/ppermute | solution.py:732
  235.1 35.7 %collective-permute-start.42 = (f32[1408,128]{1,0:T(8,128)S(1)}, f32[1408,128]{1,0:T(8,128)S(1)}, u32[]{:S(2)}, u32[]{:S(2)}) collective-permute-start(f32[1408,128]{1,0:T(8,128)S(1)} %add.114.refs_1_), channel_id=1, source_target_pairs={{0,1},{1,0},{2,3},{3,2},{4,5},{5,4},{6,7},{7,6},{8,9},{9,8},{10,11... | collective-permute-start | bytes 2162696 | tf_op jit(solution)/shard_map/ppermute | solution.py:732
  (73 other events, 856.6 us)

commit v4 on v3

--- a/solution.py
+++ b/solution.py
@@ -313,29 +313,31 @@
     )(*args)
 
 
-def dmap_kernel(rows, step, n, *refs):
+def dmap_kernel(ranges, n, *refs):
     xs, ds, outs = refs[:4], refs[4 : 4 + n], refs[-n:]
     parts = [split(d[:LANES, :]) for d in ds]
     d = tuple(jnp.concatenate([part[i] for part in parts], axis=0) for i in range(2))
     own = jnp.concatenate([d[LANES : LANES + 1, :LANES] for d in ds], axis=1)
-    for k, (x, first) in enumerate(rows):
-        here = at_rows(first, step)
+    at = 0
+    for x, first, count in ranges:
+        here = pl.ds(first, count)
         value = three((xs[2 * x][here, :], xs[2 * x + 1][here, :]), d, ((1,), (1,))) - own
         for i, out in enumerate(outs):
-            out[at_rows(k, step), :] = value[:, i * LANES : (i + 1) * LANES]
+            out[at : at + count, :] = value[:, i * LANES : (i + 1) * LANES]
+        at += count
     if len(refs) > 4 + 2 * n:
         for out in outs:
-            out[len(rows) * step :, :] = refs[4 + n][...]
-
-
-def dmap_blocks(rows, step, ds, xs, tail=()):
-    genes = ds[0].shape[1]
+            out[at:, :] = refs[4 + n][...]
+
+
+def dmap_blocks(ranges, ds, xs, tail=()):
     width = ds[0].shape[0] - 8
-    return pl.pallas_call(
-        functools.partial(dmap_kernel, rows, step, len(ds)),
+    rows = sum(count for _, _, count in ranges) + 8 * len(tail)
+    return pl.pallas_call(
+        functools.partial(dmap_kernel, ranges, len(ds)),
         in_specs=[VMEM] * (4 + len(ds) + len(tail)),
         out_specs=(VMEM,) * len(ds),
-        out_shape=(jax.ShapeDtypeStruct((len(rows) * step + 8 * len(tail), width), F32),) * len(ds),
+        out_shape=(jax.ShapeDtypeStruct((rows, width), F32),) * len(ds),
         name="dmap",
         compiler_params=room(16),
         cost_estimate=cost(0, 0),
@@ -440,24 +442,20 @@
     )(a, b)
 
 
-def add_kernel(first, a_ref, b_ref, o_ref):
-    o_ref[...] = a_ref[pl.ds(first, o_ref.shape[0]), :] + b_ref[: o_ref.shape[0], :]
-
-
-def add(first, rows, a, b):
-    return pl.pallas_call(
-        functools.partial(add_kernel, first),
+def add_kernel(a_ref, b_ref, o_ref):
+    o_ref[...] = a_ref[...] + b_ref[: o_ref.shape[0], :]
+
+
+def plus(a, b):
+    return pl.pallas_call(
+        add_kernel,
         in_specs=[VMEM, VMEM],
         out_specs=VMEM,
-        out_shape=jax.ShapeDtypeStruct((rows, b.shape[1]), F32),
+        out_shape=jax.ShapeDtypeStruct(a.shape, F32),
         name="add",
         compiler_params=room(8),
         cost_estimate=cost(0, 0),
     )(a, b)
-
-
-def plus(a, b):
-    return add(0, a.shape[0], a, b)
 
 
 def add_all_kernel(*refs):
@@ -479,31 +477,43 @@
     )(*arrays)
 
 
-def next_kernel(first, step, end_ref, s_ref, y_ref, b_ref, t_ref, o_ref):
+def next_kernel(cuts, end_ref, s_ref, y_ref, *refs):
+    blocks, (t_ref, o_ref, c_ref) = refs[:-3], refs[-3:]
     total = s_ref[...] + y_ref[...]
     t_ref[...] = total
-    o_ref[:step, :] = jnp.where(end_ref[0] == 1, b_ref[pl.ds(first, step), :], total[:step, :])
-    if total.shape[0] > step:
-        o_ref[step:, :] = total[step:, :]
-
-
-def next_piece(first, step, end, s, y, b):
-    return pl.pallas_call(
-        functools.partial(next_kernel, first, step),
-        in_specs=[SMEM, VMEM, VMEM, VMEM],
-        out_specs=(VMEM, VMEM),
-        out_shape=(jax.ShapeDtypeStruct(s.shape, F32), jax.ShapeDtypeStruct(s.shape, F32)),
+    at = 0
+    for block, (first, count) in zip(blocks, cuts, strict=True):
+        c_ref[at : at + count, :] = block[first : first + count, :]
+        at += count
+    own = c_ref[...]
+    both = min(at, total.shape[0])
+    o_ref[:both, :] = jnp.where(end_ref[0] == 1, own[:both, :], total[:both, :])
+    if o_ref.shape[0] > both:
+        o_ref[both:, :] = (own if at > both else total)[both:, :]
+
+
+def next_piece(cuts, end, s, y, *blocks):
+    size, width = sum(count for _, count in cuts), s.shape[1]
+    return pl.pallas_call(
+        functools.partial(next_kernel, cuts),
+        in_specs=[SMEM] + [VMEM] * (2 + len(blocks)),
+        out_specs=(VMEM, VMEM, VMEM),
+        out_shape=(
+            jax.ShapeDtypeStruct(s.shape, F32),
+            jax.ShapeDtypeStruct((max(size, s.shape[0]), width), F32),
+            jax.ShapeDtypeStruct((size, width), F32),
+        ),
         name="next",
-        compiler_params=room(8),
-        cost_estimate=cost(0, 0),
-    )(end, s, y, b)
-
-
-def final_kernel(place, n, end_ref, at_ref, *refs):
-    rx_ref, s_ref, (ratio_ref, sum_ref, inv_ref, a_ref, _, _, o_ref, a, b, sems) = refs[0], refs[1], refs[2:]
-    step = a.shape[0] // n
-    here = at_rows(at_ref[place], step, n)
-    load = pltpu.make_async_copy(a_ref.at[here], a, sems.at[n])
+        compiler_params=room(10),
+        cost_estimate=cost(0, 0),
+    )(end, s, y, *blocks)
+
+
+def final_kernel(place, cuts, step, end_ref, at_ref, *refs):
+    n, m = len(cuts), 1 + max(k for half in cuts for k, _, _ in half)
+    rxs, ss = refs[:m], refs[m : 2 * m]
+    ratio_ref, sum_ref, inv_ref, a_ref, _, _, o_ref, a, b, sems = refs[2 * m :]
+    load = pltpu.make_async_copy(a_ref.at[at_rows(at_ref[place], step, n)], a, sems.at[n])
     load.start()
     rows = lax.broadcasted_iota(jnp.int32, (16, step), 0)
     ones = (lax.broadcasted_iota(jnp.int32, (16, LANES), 0) < 3).astype(BF16)
@@ -515,7 +525,13 @@
         mid = (ratio - high).astype(BF16).astype(F32)
         terms = jnp.where(rows == 0, high, jnp.where(rows == 1, mid, jnp.where(rows == 2, ratio - high - mid, 0.0)))
         column = lax.dot_general(terms.astype(BF16), ones, (((0,), (0,)), ((), ())), preferred_element_type=F32)
-        whole = jnp.where(end_ref[0] == 1, rx_ref[here, :], s_ref[here, :])
+        whole = jnp.concatenate(
+            [
+                jnp.where(end_ref[0] == 1, rxs[i][first : first + count, :], ss[i][first : first + count, :])
+                for i, first, count in cuts[k]
+            ],
+            axis=0,
+        )
         value = whole + (sum_ref[0:1, :] - column * inv_ref[...])
         if k == 0:
             load.wait()
@@ -526,19 +542,20 @@
         store.wait()
 
 
-def final_piece(step, n, place, end, at, rx, s, ratio, ratio_sum, inv, a, grad):
-    width = s.shape[1]
-    return pl.pallas_call(
-        functools.partial(final_kernel, place, n),
-        in_specs=[SMEM, SMEM] + [VMEM] * 5 + [HBM, HBM],
+def final_block(step, cuts, place, end, at, rxs, ss, ratio, ratio_sum, inv, a, grad):
+    width = a.shape[1]
+    n, m = len(cuts), len(ss)
+    return pl.pallas_call(
+        functools.partial(final_kernel, place, cuts, step),
+        in_specs=[SMEM, SMEM] + [VMEM] * (2 * m + 3) + [HBM, HBM],
         out_specs=(HBM, HBM),
         out_shape=(pltpu.HBM(a.shape, F32), pltpu.HBM(grad.shape, F32)),
         scratch_shapes=[pltpu.VMEM((n * step, width), F32)] * 2 + [pltpu.SemaphoreType.DMA((1 + n,))],
-        input_output_aliases={7: 0, 8: 1},
+        input_output_aliases={5 + 2 * m: 0, 6 + 2 * m: 1},
         name="final",
-        compiler_params=room(10),
-        cost_estimate=cost(0, 0),
-    )(end, at, rx, s, ratio, ratio_sum, inv, a, grad)
+        compiler_params=room(12),
+        cost_estimate=cost(0, 0),
+    )(end, at, *rxs, *ss, ratio, ratio_sum, inv, a, grad)
 
 
 def blank(shape):
@@ -550,7 +567,7 @@
     rx_ref, s_ref, q_ref, kl_ref, loss_ref, map_ref, pred_ref = refs[n:]
     while len(sums) > 1:
         sums = [a + b for a, b in zip(sums[::2], sums[1::2], strict=True)]
-    by_gene = jnp.where(end_ref[0] == 1, rx_ref[step:, :], s_ref[step:, :])
+    by_gene = jnp.where(end_ref[0] == 1, rx_ref[step : step + 8, :], s_ref[step : step + 8, :])
     cosine, fitted, wsum, scos = by_gene[0:1, :], sums[0][2:3, :], by_gene[3:4, :], sums[0][1:2, :]
     loss = -cosine / wsum - scos / spots + kl_ref[0:1, :]
     rms_map = jnp.sqrt(q_ref[q_ref.shape[0] - 1 :, q_ref.shape[1] - LANES :] / (cells * spots))
@@ -692,51 +709,70 @@
         (pred, spatial, *constants, inv),
     )
     grads, back, tails = {0: grad}, {}, {}
-    for m in far:
-        grads[m] = swap(grad, m)
-
-    def dmap(ms, steps, wait=(), tail=()):
+
+    def dmap(ms, ranges, wait=(), tail=()):
         outs = order(
-            lambda *a: dmap_blocks(steps, half, a[: len(ms)], a[len(ms) : len(ms) + 4], a[len(ms) + 4 :]),
+            lambda *a: dmap_blocks(ranges, a[: len(ms)], a[len(ms) : len(ms) + 4], a[len(ms) + 4 :]),
             [grads[m] for m in ms],
             (*own_x, *other_x, *tail),
             wait,
         )
-        for m, d in zip(ms, outs, strict=True):
-            d = swap(d, m) if m else d
-            for k, (odd, first) in enumerate(steps):
-                if first == 0:
-                    back[m + odd] = (d, k * half)
-            if tail:
-                tails[m] = d
-
-    own_rows, other_rows = ((0, 0), (0, 1)), ((1, 0), (1, 1))
-    places = [0, 1, 2, 4, 3, 5, 6, 7] if n_blk == 8 else [r for m in [0, *far] for r in (m, m + 1)]
-    count, lag = len(places), 3
-    part, total_of, mid, got = {}, {}, {}, {}
+        if tail and ms != (0,):
+            tails.update({m: swap(d, m) for m, d in zip(ms, outs, strict=True)})
+            return [tails[m] for m in ms]
+        return [swap(d, m) if m else d for m, d in zip(ms, outs, strict=True)]
+
+    def block_rows(odd):
+        return ((odd, 0, half), (odd, half, half))
+
+    blocks = [0, 1, 2, 4, 3, 5, 6, 7] if n_blk == 8 else [r for m in [0, *far] for r in (m, m + 1)]
+    long = 3 * half // 2
+    sizes = [long, long, half] + [long] * ((cells - 2 * rows) // long)
+    starts = [sum(sizes[:t]) for t in range(len(sizes))]
+    count, lag = len(sizes), 3
+    assert starts[3] == 2 * rows and sum(sizes) == cells
+
+    def overlap(first, size, cuts_at, cuts_size):
+        found = []
+        for k, (a, n) in enumerate(zip(cuts_at, cuts_size, strict=True)):
+            low, high = max(first, a), min(first + size, a + n)
+            if low < high:
+                found.append((k, low - a, high - low))
+        return found
+
+    block_starts, block_sizes = [rows * k for k in range(len(blocks))], [rows] * len(blocks)
+    part, total_of, mid, got, own = {}, {}, {}, {}, {}
     end = jnp.reshape((plane == 0) | (plane == n_gene - 1), (1,)).astype(jnp.int32)
 
     def send(t):
         if t >= count + lag:
             return
-        if t < count:
-            block, first = back[places[t]]
         if t < lag:
-            buffer = block if block.shape[0] <= rows + 8 else block[first : first + rows]
+            ranges = overlap(starts[t], sizes[t], (0, rows), (rows, rows))
+            own[t] = buffer = dmap((0,), tuple(ranges), (), (tot,) if t == 0 else ())[0]
         elif t < count:
-            total_of[t - lag], buffer = order(
-                lambda s, y, b: next_piece(first, rows, end, s, y, b), (part[t - lag], mid[t - lag], block)
+            found = overlap(starts[t], sizes[t], block_starts, block_sizes)
+            cuts = tuple((back[blocks[k]][1] + first, n) for k, first, n in found)
+            total_of[t - lag], buffer, own[t] = order(
+                lambda s, y, *b: next_piece(cuts, end, s, y, *b),
+                (part[t - lag], mid[t - lag], *[back[blocks[k]][0] for k, _, _ in found]),
             )
         else:
             buffer = total_of[t - lag] = order(plus, (part[t - lag], mid[t - lag]))
         got[t] = lax.ppermute(buffer, "gene", PAIR)
 
-    def finish(t):
+    def finish(k):
+        halves = [overlap(block_starts[k] + half * h, half, starts, sizes) for h in range(2)]
+        ts = sorted({t for found in halves for t, _, _ in found})
+        cuts = tuple(tuple((ts.index(t), first, n) for t, first, n in found) for found in halves)
+        m = len(ts)
         state["scale"], state["grad"] = order(
-            functools.partial(final_piece, half, 2, 2 + 2 * places[t], end, at),
-            (got[t + lag], total_of[t]),
+            lambda *a: final_block(half, cuts, 2 + 2 * blocks[k], end, at, a[:m], a[m : 2 * m], *a[2 * m :]),
+            (*[got[t + lag] for t in ts], *[total_of[t] for t in ts]),
             (state["ratio"], state["ratio_sum"], inv, state["scale"], state["grad"]),
         )
+
+    last_piece = [max(t for t, _, _ in overlap(a, rows, starts, sizes)) for a in block_starts]
 
     def expr_part(odd, ks, adds=()):
         ms = [0, *far]
@@ -749,48 +785,84 @@
             (*ls, *[grads[m] for m in far]),
         )
 
-    def extra(t):
-        if t == 0:
+    def first_dmap():
+        if n_blk == 8:
+            for r, d in zip((2, 4), dmap((2, 4), block_rows(0)), strict=True):
+                back[r] = (d, 0)
+        else:
             tails[0] = order(plus, (tot, tot_moved))
-            if n_blk == 8:
-                dmap((2, 4), own_rows)
-            else:
-                for m in far:
-                    dmap((m,), own_rows + other_rows, (), (tails[0],))
-            state["scale"], state["ratio"], state["ratio_sum"], state["kl"] = order(
-                functools.partial(ratio_part, spots), (by_cell,), (density, inv, state["scale"])
-            )
+            for m in far:
+                (d,) = dmap((m,), block_rows(0) + block_rows(1), (), (tails[0],))
+                back[m], back[m + 1] = (d, 0), (d, rows)
+
+    def second_dmap():
         if n_blk == 8:
-            if t == 1:
-                dmap((2, 4), other_rows, (back[2][0], back[4][0]), (tails[0],))
-            if t == 3:
-                dmap((6,), own_rows + other_rows, (back[3][0], back[5][0]), (tails[0],))
-        if t in (count - 2, count - 1):
-            state["swapped", t - count] = swap(expr_part(1, (t - count + 2,)), 1)
-        if t == count:
-            state["scalars"] = order(
-                functools.partial(scalar_results, n_blk // 2, cells, spots, rows, end),
-                (*[tails[m] for m in range(0, n_blk, 2)], got[lag], total_of[0], by_cell),
-                (state["kl"],),
-            )
-        if t == count + 1:
-            state["expr"] = expr_part(0, (0, 1), (state["swapped", -2], state["swapped", -1]))
-
-    dmap((0,), own_rows, (), (tot,))
+            tails[0] = order(plus, (tot, tot_moved))
+            for r, d in zip((3, 5), dmap((2, 4), block_rows(1), (back[2][0], back[4][0]), (tails[0],)), strict=True):
+                back[r] = (d, 0)
+
+    def third_dmap():
+        if n_blk == 8:
+            back[6] = (dmap((6,), block_rows(0), (back[3][0], back[5][0]))[0], 0)
+
+    def fourth_dmap():
+        if n_blk == 8:
+            back[7] = (dmap((6,), block_rows(1), (), (tails[0],))[0], 0)
+
+    def kl():
+        state["scale"], state["ratio"], state["ratio_sum"], state["kl"] = order(
+            functools.partial(ratio_part, spots), (by_cell,), (density, inv, state["scale"])
+        )
+
+    def egrad(k):
+        state["swapped", k] = swap(expr_part(1, (k,)), 1)
+
+    def scalars():
+        state["scalars"] = order(
+            functools.partial(scalar_results, n_blk // 2, cells, spots, long, end),
+            (*[tails[m] for m in range(0, n_blk, 2)], got[lag], total_of[0], by_cell),
+            (state["kl"],),
+        )
+
+    def expr():
+        state["expr"] = expr_part(0, (0, 1), (state["swapped", 0], state["swapped", 1]))
+
+    late = count - 11
+    plan = {
+        (0, "between"): [first_dmap],
+        (1, "after"): [kl],
+        (2, "between"): [second_dmap],
+        (4, "between"): [third_dmap],
+        (5, "between"): [fourth_dmap],
+        (late + 7, "between"): [functools.partial(egrad, 0)],
+        (late + 8, "between"): [functools.partial(egrad, 1)],
+        (late + 11, "between"): [scalars],
+        (late + 12, "between"): [expr],
+    }
+    for k in range(len(blocks)):
+        t = last_piece[k] + lag + 1
+        if t < count + lag:
+            plan.setdefault((t, "after"), []).append(functools.partial(finish, k))
+
+    def extra(t, place):
+        for step in plan.get((t, place), ()):
+            step()
+
     send(0)
-    dmap((0,), other_rows)
+    for m in far:
+        grads[m] = swap(order.here(grad), m)
     tot_moved = swap(order.here(tot), 1)
     for t in range(count + lag):
+        extra(t, "before")
         send(t + 1)
-        extra(t)
-        if t > lag:
-            finish(t - lag - 1)
+        extra(t, "between")
         if t < count:
-            block, first = back[places[t]]
-            size = block.shape[0] if t == 0 else rows
-            part[t] = order(functools.partial(add, first, size), (block, got[t]))
+            part[t] = order(plus, (own[t], got[t]))
             mid[t] = lax.ppermute(part[t], "gene", MIDDLE)
-    finish(count - 1)
+        extra(t, "after")
+    for k in range(len(blocks)):
+        if last_piece[k] + lag + 1 >= count + lag:
+            finish(k)
     loss, rms_map, rms_pred = (x[0, 0] for x in state["scalars"])
     return (loss, state["grad"], state["expr"], rms_map, rms_pred)
 

time: 275 us -> 263 us (0.956)
  starting transfers between devices: 99 us -> 85.6 us
  waiting for transfers between devices: 59.1 us -> 67.2 us
  Pallas kernels: 96.7 us -> 91.1 us
    ppermute x11 -> x14, starting transfers between devices: 59.3 us -> 42.5 us  [send(): got[t] = lax.ppermute(buffer, 'gene', PAIR)]
    ppermute x24 -> x25, waiting for transfers between devices: 34.9 us -> 42.1 us  [swap(): return lax.ppermute(x, 'blk', [(i, i ^ m) for i in range(n_blk)])]
    pallas_call x33 -> x41, Pallas kernels: 54.9 us -> 51.1 us  [the longest x8 23.2 us: final_block(): pl.pallas_call(functools.partial(final_kernel, place, cuts, step), in_spe...]
    ppermute x8 -> x11, starting transfers between devices: 7.84 us -> 10.3 us  [shards(): mid[t] = lax.ppermute(part[t], 'gene', MIDDLE)]
    unnamed x100 -> x116, local copies, waits for them, and re-layouts: 15.1 us -> 13.2 us
    ppermute x11 -> x14, waiting for transfers between devices: 20.2 us -> 21.2 us  [send(): got[t] = lax.ppermute(buffer, 'gene', PAIR)]
    ppermute x24 -> x25, starting transfers between devices: 24.6 us -> 25.4 us  [swap(): return lax.ppermute(x, 'blk', [(i, i ^ m) for i in range(n_blk)])]
  transfers between devices with their start and end apart: 47 -> 54, of which waited for: 17 -> 19; matrix products, arithmetic and copies ran while one was open for 1% -> 1% of each run, Pallas kernels for 33% -> 33%
where the time goes in v4:
time: 263 us; the launch traced here: 261 us
  Pallas kernels  91.1 us (35%)
  starting transfers between devices  85.6 us (33%)
  waiting for transfers between devices  67.2 us (26%)
  local copies, waits for them, and re-layouts  15.4 us (6%)
    ppermute x14, starting transfers between devices, send(): got[t] = lax.ppermute(buffer, 'gene', PAIR)  42.5 us
    ppermute x25, waiting for transfers between devices, swap(): return lax.ppermute(x, 'blk', [(i, i ^ m) for i in range(n_blk)])  42.1 us
    ppermute x25, starting transfers between devices, swap(): return lax.ppermute(x, 'blk', [(i, i ^ m) for i in range(n_blk)])  25.4 us
    pallas_call x8, Pallas kernels, final_block(): pl.pallas_call(functools.partial(final_kernel, place, cuts, step), in_spe...  23.2 us
    ppermute x14, waiting for transfers between devices, send(): got[t] = lax.ppermute(buffer, 'gene', PAIR)  21.2 us
    unnamed x116, local copies, waits for them, and re-layouts  13.2 us
    pallas_call x7, Pallas kernels, pred_sums_of(): pl.pallas_call(functools.partial(pred_kernel, jobs, n_acc, step, len(tail...  10.7 us
    pallas_call x7, Pallas kernels, dmap_blocks(): pl.pallas_call(functools.partial(dmap_kernel, ranges, len(ds)), in_specs=...  10.7 us
  transfers between devices with their start and end apart: 54, of which 19 were waited for; matrix products, arithmetic and copies ran while one was open for 1% of the time, Pallas kernels for 33%

profile of v4, /device:TPU:0, one launch (start us, length us, event | category | flops | bytes accessed | tf_op | source)
XLA Modules:
  0.0 261.2 jit_solution(12731509733967181439)
XLA Ops:
  22.2 6.9 %softmax.1 = (f32[1,128]{1,0:T(1,128)S(1)}, f32[32,512]{1,0:T(8,128)S(1)}, f32[11264,128]{1,0:T(8,128)}) custom-call(f32[11264,128]{1,0:T(8,128)S(1)} %copy-done.7), custom_call_target="tpu_custom_call" | custom-call | flops 1 | bytes 1 | tf_op jit(solution)/shard_map/softmax/pallas_call | solution.py:143
  42.0 9.4 %collective-permute-done.3.refs_0_.refs_1_ = f32[1408,128]{1,0:T(8,128)S(1)} collective-permute-done((f32[1408,128]{1,0:T(8,128)S(1)}, f32[1408,128]{1,0:T(8,128)S(1)}, u32[]{:S(2)}, u32[]{:S(2)}) %collective-permute-start.3) | collective-permute-done | bytes 720928 | tf_op jit(solution)/shard_map/ppermute | solution.py:603
  59.4 10.8 %collective-permute-done.9.refs_2_ = f32[160,512]{1,0:T(8,128)S(1)} collective-permute-done((f32[160,512]{1,0:T(8,128)S(1)}, f32[160,512]{1,0:T(8,128)S(1)}, u32[]{:S(2)}, u32[]{:S(2)}) %collective-permute-start.9) | collective-permute-done | bytes 327712 | tf_op jit(solution)/shard_map/ppermute | solution.py:603
  103.9 3.9 %collective-permute-done.23.b_ref = f32[1056,128]{1,0:T(8,128)S(1)} collective-permute-done((f32[1056,128]{1,0:T(8,128)S(1)}, f32[1056,128]{1,0:T(8,128)S(1)}, u32[]{:S(2)}, u32[]{:S(2)}) %collective-permute-start.23) | collective-permute-done | bytes 540704 | tf_op jit(solution)/shard_map/ppermute | solution.py:762
  110.2 3.7 %collective-permute-start.30 = (f32[704,128]{1,0:T(8,128)}, f32[704,128]{1,0:T(8,128)}, u32[]{:S(2)}, u32[]{:S(2)}) collective-permute-start(f32[704,128]{1,0:T(8,128)} %dmap.10.a_ref), channel_id=1, source_target_pairs={{0,1},{1,0},{2,3},{3,2},{4,5},{5,4},{6,7},{7,6},{8,9},{9,8},{10,11... | collective-permute-start | bytes 1081352 | tf_op jit(solution)/shard_map/ppermute | solution.py:762
  114.9 4.2 %ratio.1 = (f32[11264,128]{1,0:T(8,128)}, f32[16,704]{1,0:T(8,128)S(1)}, f32[8,128]{1,0:T(8,128)S(1)}, f32[8,128]{1,0:T(8,128)S(1)}) custom-call(f32[32,512]{1,0:T(8,128)S(1)} %copy-done.50, f32[16,704]{1,0:T(8,128)S(1)} %reshape.16.density_ref, f32[1,128]{1,0:T(1,128)S(1)} %get-tuple-element.236.refs_5_.refs_9_.inv_ref.refs_6_, ...), custom_call_target="tpu_custom_call", output_to_operand_aliasing={{0}: (3, {})} | custom-call | flops 1 | bytes 1 | tf_op jit(solution)/shard_map/ratio/pallas_call | solution.py:409
  134.7 8.6 %collective-permute-done.25.refs_1_.refs_0_ = f32[1416,128]{1,0:T(8,128)S(1)} collective-permute-done((f32[1416,128]{1,0:T(8,128)S(1)}, f32[1416,128]{1,0:T(8,128)S(1)}, u32[]{:S(2)}, u32[]{:S(2)}) %collective-permute-start.25) | collective-permute-done | bytes 725024 | tf_op jit(solution)/shard_map/ppermute | solution.py:603
  147.2 2.9 %collective-permute-start.37 = (f32[1056,128]{1,0:T(8,128)}, f32[1056,128]{1,0:T(8,128)}, u32[]{:S(2)}, u32[]{:S(2)}) collective-permute-start(f32[1056,128]{1,0:T(8,128)} %get-tuple-element.341), channel_id=1, source_target_pairs={{0,1},{1,0},{2,3},{3,2},{4,5},{5,4},{6,7},{7,6},{8,9},{9,8},{10,11... | collective-permute-start | bytes 1622024 | tf_op jit(solution)/shard_map/ppermute | solution.py:762
  159.3 2.9 %collective-permute-start.35 = (f32[1056,128]{1,0:T(8,128)}, f32[1056,128]{1,0:T(8,128)}, u32[]{:S(2)}, u32[]{:S(2)}) collective-permute-start(f32[1056,128]{1,0:T(8,128)} %get-tuple-element.339), channel_id=1, source_target_pairs={{0,1},{1,0},{2,3},{3,2},{4,5},{5,4},{6,7},{7,6},{8,9},{9,8},{10,11... | collective-permute-start | bytes 1622024 | tf_op jit(solution)/shard_map/ppermute | solution.py:762
  168.1 2.7 %final.8 = (f32[11264,128]{1,0:T(8,128)}, f32[11264,128]{1,0:T(8,128)}) custom-call(s32[1]{0:T(128)} %bitcast.end_ref, s32[26]{0:T(128)S(1)} %stack.107.at_ref, f32[1064,128]{1,0:T(8,128)S(1)} %copy-done.28, f32[1056,128]{1,0:T(8,128)S(1)} %copy-done.30, f32[1064,128]{1,0:T(8,128)S(1)} %copy-done.37, ...), custom_call_target="tpu_custom_call", output_to_operand_aliasing={{0}: (9, {}), {1}: (10, {})} | custom-call | flops 1 | bytes 1 | tf_op jit(solution)/shard_map/final/pallas_call | solution.py:548
  172.2 2.9 %collective-permute-start.40 = (f32[1056,128]{1,0:T(8,128)S(1)}, f32[1056,128]{1,0:T(8,128)S(1)}, u32[]{:S(2)}, u32[]{:S(2)}) collective-permute-start(f32[1056,128]{1,0:T(8,128)S(1)} %get-tuple-element.358), channel_id=1, source_target_pairs={{0,1},{1,0},{2,3},{3,2},{4,5},{5,4},{6,7},{7,6},{8,9},{9,8},{10,11... | collective-permute-start | bytes 1622024 | tf_op jit(solution)/shard_map/ppermute | solution.py:762
  178.5 3.6 %final.9 = (f32[11264,128]{1,0:T(8,128)}, f32[11264,128]{1,0:T(8,128)}) custom-call(s32[1]{0:T(128)} %bitcast.end_ref, s32[26]{0:T(128)S(1)} %stack.107.at_ref, f32[1056,128]{1,0:T(8,128)S(1)} %copy-done.30, f32[1056,128]{1,0:T(8,128)} %collective-permute-done.37.b_ref.refs_1_, ...), custom_call_target="tpu_custom_call", output_to_operand_aliasing={{0}: (9, {}), {1}: (10, {})} | custom-call | flops 1 | bytes 1 | tf_op jit(solution)/shard_map/final/pallas_call | solution.py:548
  189.1 3.1 %collective-permute-done.34.refs_1_.refs_0_.refs_3_ = f32[1416,128]{1,0:T(8,128)S(1)} collective-permute-done((f32[1416,128]{1,0:T(8,128)S(1)}, f32[1416,128]{1,0:T(8,128)S(1)}, u32[]{:S(2)}, u32[]{:S(2)}) %collective-permute-start.34) | collective-permute-done | bytes 725024 | tf_op jit(solution)/shard_map/ppermute | solution.py:603
  193.4 3.9 %collective-permute-start.42 = (f32[1056,128]{1,0:T(8,128)S(1)}, f32[1056,128]{1,0:T(8,128)S(1)}, u32[]{:S(2)}, u32[]{:S(2)}) collective-permute-start(f32[1056,128]{1,0:T(8,128)S(1)} %get-tuple-element.378), channel_id=1, source_target_pairs={{0,1},{1,0},{2,3},{3,2},{4,5},{5,4},{6,7},{7,6},{8,9},{9,8},{10,11... | collective-permute-start | bytes 1622024 | tf_op jit(solution)/shard_map/ppermute | solution.py:762
  200.4 3.2 %final.10 = (f32[11264,128]{1,0:T(8,128)}, f32[11264,128]{1,0:T(8,128)}) custom-call(s32[1]{0:T(128)} %bitcast.end_ref, s32[26]{0:T(128)S(1)} %stack.107.at_ref, f32[1056,128]{1,0:T(8,128)} %collective-permute-done.35.b_ref.refs_0_, f32[1056,128]{1,0:T(8,128)S(1)} %collective-permute-done.40.b_ref.refs_1_.refs_0_, ...), custom_call_target="tpu_custom_call", output_to_operand_aliasing={{0}: (9, {}), {1}: (10, {})} | custom-call | flops 1 | bytes 1 | tf_op jit(solution)/shard_map/final/pallas_call | solution.py:548
  203.9 4.2 %collective-permute-start.46 = (f32[1056,128]{1,0:T(8,128)S(1)}, f32[1056,128]{1,0:T(8,128)S(1)}, u32[]{:S(2)}, u32[]{:S(2)}) collective-permute-start(f32[1056,128]{1,0:T(8,128)S(1)} %get-tuple-element.398), channel_id=1, source_target_pairs={{0,1},{1,0},{2,3},{3,2},{4,5},{5,4},{6,7},{7,6},{8,9},{9,8},{10,11... | collective-permute-start | bytes 1622024 | tf_op jit(solution)/shard_map/ppermute | solution.py:762
  211.9 2.7 %final.11 = (f32[11264,128]{1,0:T(8,128)}, f32[11264,128]{1,0:T(8,128)}) custom-call(s32[1]{0:T(128)} %bitcast.end_ref, s32[26]{0:T(128)S(1)} %stack.107.at_ref, f32[1056,128]{1,0:T(8,128)S(1)} %collective-permute-done.40.b_ref.refs_1_.refs_0_, ...), custom_call_target="tpu_custom_call", output_to_operand_aliasing={{0}: (9, {}), {1}: (10, {})} | custom-call | flops 1 | bytes 1 | tf_op jit(solution)/shard_map/final/pallas_call | solution.py:548
  214.7 5.9 %collective-permute-done.46.b_ref.refs_0_ = f32[1056,128]{1,0:T(8,128)S(1)} collective-permute-done((f32[1056,128]{1,0:T(8,128)S(1)}, f32[1056,128]{1,0:T(8,128)S(1)}, u32[]{:S(2)}, u32[]{:S(2)}) %collective-permute-start.46) | collective-permute-done | bytes 540704 | tf_op jit(solution)/shard_map/ppermute | solution.py:762
  221.6 3.8 %collective-permute-start.51 = (f32[1056,128]{1,0:T(8,128)S(1)}, f32[1056,128]{1,0:T(8,128)S(1)}, u32[]{:S(2)}, u32[]{:S(2)}) collective-permute-start(f32[1056,128]{1,0:T(8,128)S(1)} %add.117.refs_3_.refs_2_), channel_id=1, source_target_pairs={{0,1},{1,0},{2,3},{3,2},{4,5},{5,4},{6,7},{7,6},{8,9},{9,8},{10,11... | collective-permute-start | bytes 1622024 | tf_op jit(solution)/shard_map/ppermute | solution.py:762
  231.7 9.1 %collective-permute-start.50 = (f32[1056,128]{1,0:T(8,128)S(1)}, f32[1056,128]{1,0:T(8,128)S(1)}, u32[]{:S(2)}, u32[]{:S(2)}) collective-permute-start(f32[1056,128]{1,0:T(8,128)S(1)} %add.120.refs_3_), channel_id=1, source_target_pairs={{0,1},{1,0},{2,3},{3,2},{4,5},{5,4},{6,7},{7,6},{8,9},{9,8},{10,11... | collective-permute-start | bytes 1622024 | tf_op jit(solution)/shard_map/ppermute | solution.py:762
  240.8 4.6 %egrad.5 = f32[1408,512]{1,0:T(8,128)} custom-call(s32[26]{0:T(128)S(1)} %stack.107.at_ref, f32[2816,128]{1,0:T(8,128)S(1)} %copy-done.9, f32[1408,128]{1,0:T(8,128)S(1)} %copy-done.32, f32[1408,128]{1,0:T(8,128)S(1)} %copy-done.34, f32[1408,128]{1,0:T(8,128)S(1)} %copy-done.15, f32[1408,128]{1,0:T(8,128)S(1)} %copy-done.13, ...), custom_call_target="tpu_custom_call" | custom-call | flops 1 | bytes 1 | tf_op jit(solution)/shard_map/egrad/pallas_call | solution.py:369
  245.4 2.7 %final.13 = (f32[11264,128]{1,0:T(8,128)}, f32[11264,128]{1,0:T(8,128)}) custom-call(s32[1]{0:T(128)} %bitcast.end_ref, s32[26]{0:T(128)S(1)} %stack.107.at_ref, f32[1056,128]{1,0:T(8,128)S(1)} %collective-permute-done.46.b_ref.refs_0_, f32[1056,128]{1,0:T(8,128)S(1)} %collective-permute-done.51.refs_1_.refs_0_, ...), custom_call_target="tpu_custom_call", output_to_operand_aliasing={{0}: (9, {}), {1}: (10, {})} | custom-call | flops 1 | bytes 1 | tf_op jit(solution)/shard_map/final/pallas_call | solution.py:548
  250.2 2.7 %final.14 = (f32[11264,128]{1,0:T(8,128)}, f32[11264,128]{1,0:T(8,128)}) custom-call(s32[1]{0:T(128)} %bitcast.end_ref, s32[26]{0:T(128)S(1)} %stack.107.at_ref, f32[1056,128]{1,0:T(8,128)S(1)} %collective-permute-done.51.refs_1_.refs_0_, f32[1056,128]{1,0:T(8,128)S(1)} %collective-permute-done.48.refs_1_.refs_0_, ...), custom_call_target="tpu_custom_call", output_to_operand_aliasing={{0}: (9, {}), {1}: (10, {})} | custom-call | flops 1 | bytes 1 | tf_op jit(solution)/shard_map/final/pallas_call | solution.py:548
  252.9 5.4 %collective-permute-done.50.refs_1_ = f32[1056,128]{1,0:T(8,128)S(1)} collective-permute-done((f32[1056,128]{1,0:T(8,128)S(1)}, f32[1056,128]{1,0:T(8,128)S(1)}, u32[]{:S(2)}, u32[]{:S(2)}) %collective-permute-start.50) | collective-permute-done | bytes 540704 | tf_op jit(solution)/shard_map/ppermute | solution.py:762
  (265 shorter events, 145.5 us)
Async XLA Ops:
  0.6 29.0 %collective-permute-start = (f32[1408,512]{1,0:T(8,128)}, f32[1408,512]{1,0:T(8,128)}, u32[]{:S(2)}, u32[]{:S(2)}) collective-permute-start(f32[1408,512]{1,0:T(8,128)} %x_ref), channel_id=1, source_target_pairs={{0,4},{4,0},{8,12},{12,8},{16,20},{20,16},{24,28},{28,24},{1,5},{5... | collective-permute-start | bytes 8650760 | tf_op jit(solution)/shard_map/ppermute | solution.py:603
  17.5 20.1 %collective-permute-start.5 = (f32[1408,128]{1,0:T(8,128)S(1)}, f32[1408,128]{1,0:T(8,128)S(1)}, u32[]{:S(2)}, u32[]{:S(2)}) collective-permute-start(f32[1408,128]{1,0:T(8,128)S(1)} %get-tuple-element.248), channel_id=1, source_target_pairs={{0,24},{4,28},{8,16},{12,20},{16,8},{20,12},{24,0},{28,4},{1,25},{... | collective-permute-start | bytes 2162696 | tf_op jit(solution)/shard_map/ppermute | solution.py:603
  19.1 21.5 %collective-permute-start.4 = (f32[1408,128]{1,0:T(8,128)S(1)}, f32[1408,128]{1,0:T(8,128)S(1)}, u32[]{:S(2)}, u32[]{:S(2)}) collective-permute-start(f32[1408,128]{1,0:T(8,128)S(1)} %join.1), channel_id=1, source_target_pairs={{0,1},{1,0},{2,3},{3,2},{4,5},{5,4},{6,7},{7,6},{8,9},{9,8},{10,11... | collective-permute-start | bytes 2162696 | tf_op jit(solution)/shard_map/ppermute | solution.py:606
  20.7 30.8 %collective-permute-start.3 = (f32[1408,128]{1,0:T(8,128)S(1)}, f32[1408,128]{1,0:T(8,128)S(1)}, u32[]{:S(2)}, u32[]{:S(2)}) collective-permute-start(f32[1408,128]{1,0:T(8,128)S(1)} %get-tuple-element.243), channel_id=1, source_target_pairs={{0,8},{4,12},{8,0},{12,4},{16,24},{20,28},{24,16},{28,20},{1,9},{5... | collective-permute-start | bytes 2162696 | tf_op jit(solution)/shard_map/ppermute | solution.py:603
  29.0 24.6 %collective-permute-start.8 = (f32[1408,128]{1,0:T(8,128)S(1)}, f32[1408,128]{1,0:T(8,128)S(1)}, u32[]{:S(2)}, u32[]{:S(2)}) collective-permute-start(f32[1408,128]{1,0:T(8,128)S(1)} %get-tuple-element.261), channel_id=1, source_target_pairs={{0,16},{4,20},{8,24},{12,28},{16,0},{20,4},{24,8},{28,12},{1,17},{... | collective-permute-start | bytes 2162696 | tf_op jit(solution)/shard_map/ppermute | solution.py:603
  37.6 18.1 %collective-permute-start.10 = (f32[1408,128]{1,0:T(8,128)S(1)}, f32[1408,128]{1,0:T(8,128)S(1)}, u32[]{:S(2)}, u32[]{:S(2)}) collective-permute-start(f32[1408,128]{1,0:T(8,128)S(1)} %collective-permute-done.5.refs_0_.refs_5_.refs_3_), channel_id=1, source_target_pairs={{0,1},{1,0},{2,3},{3,2},{4,5},{5,4},{6,7},{7,6},{8,9},{9,8},{10,11... | collective-permute-start | bytes 2162696 | tf_op jit(solution)/shard_map/ppermute | solution.py:606
  89.8 18.1 %collective-permute-start.23 = (f32[1056,128]{1,0:T(8,128)S(1)}, f32[1056,128]{1,0:T(8,128)S(1)}, u32[]{:S(2)}, u32[]{:S(2)}) collective-permute-start(f32[1056,128]{1,0:T(8,128)S(1)} %dmap.8.a_ref), channel_id=1, source_target_pairs={{0,1},{1,0},{2,3},{3,2},{4,5},{5,4},{6,7},{7,6},{8,9},{9,8},{10,11... | collective-permute-start | bytes 1622024 | tf_op jit(solution)/shard_map/ppermute | solution.py:762
  96.6 22.6 %collective-permute-start.22 = (f32[1408,128]{1,0:T(8,128)}, f32[1408,128]{1,0:T(8,128)}, u32[]{:S(2)}, u32[]{:S(2)}) collective-permute-start(f32[1408,128]{1,0:T(8,128)} %get-tuple-element.291), channel_id=1, source_target_pairs={{0,8},{4,12},{8,0},{12,4},{16,24},{20,28},{24,16},{28,20},{1,9},{5... | collective-permute-start | bytes 2162696 | tf_op jit(solution)/shard_map/ppermute | solution.py:603
  97.3 25.4 %collective-permute-start.24 = (f32[1408,128]{1,0:T(8,128)}, f32[1408,128]{1,0:T(8,128)}, u32[]{:S(2)}, u32[]{:S(2)}) collective-permute-start(f32[1408,128]{1,0:T(8,128)} %get-tuple-element.307), channel_id=1, source_target_pairs={{0,16},{4,20},{8,24},{12,28},{16,0},{20,4},{24,8},{28,12},{1,17},{... | collective-permute-start | bytes 2162696 | tf_op jit(solution)/shard_map/ppermute | solution.py:603
  100.9 18.2 %collective-permute-start.21 = (f32[1064,128]{1,0:T(8,128)}, f32[1064,128]{1,0:T(8,128)}, u32[]{:S(2)}, u32[]{:S(2)}) collective-permute-start(f32[1064,128]{1,0:T(8,128)} %add.106.s_ref), channel_id=1, source_target_pairs={{1,2},{2,1},{5,6},{6,5},{9,10},{10,9},{13,14},{14,13},{17,18},{18,... | collective-permute-start | bytes 1634312 | tf_op jit(solution)/shard_map/ppermute | solution.py:861
  108.7 19.1 %collective-permute-start.29 = (f32[1056,128]{1,0:T(8,128)}, f32[1056,128]{1,0:T(8,128)}, u32[]{:S(2)}, u32[]{:S(2)}) collective-permute-start(f32[1056,128]{1,0:T(8,128)} %add.107.s_ref), channel_id=1, source_target_pairs={{1,2},{2,1},{5,6},{6,5},{9,10},{10,9},{13,14},{14,13},{17,18},{18,... | collective-permute-start | bytes 1622024 | tf_op jit(solution)/shard_map/ppermute | solution.py:861
  124.1 19.1 %collective-permute-start.25 = (f32[1416,128]{1,0:T(8,128)S(1)}, f32[1416,128]{1,0:T(8,128)S(1)}, u32[]{:S(2)}, u32[]{:S(2)}) collective-permute-start(f32[1416,128]{1,0:T(8,128)S(1)} %get-tuple-element.310), channel_id=1, source_target_pairs={{0,8},{4,12},{8,0},{12,4},{16,24},{20,28},{24,16},{28,20},{1,9},{5... | collective-permute-start | bytes 2174984 | tf_op jit(solution)/shard_map/ppermute | solution.py:603
  125.8 24.3 %collective-permute-start.26 = (f32[1416,128]{1,0:T(8,128)S(1)}, f32[1416,128]{1,0:T(8,128)S(1)}, u32[]{:S(2)}, u32[]{:S(2)}) collective-permute-start(f32[1416,128]{1,0:T(8,128)S(1)} %get-tuple-element.311), channel_id=1, source_target_pairs={{0,16},{4,20},{8,24},{12,28},{16,0},{20,4},{24,8},{28,12},{1,17},{... | collective-permute-start | bytes 2174984 | tf_op jit(solution)/shard_map/ppermute | solution.py:603
  129.6 23.6 %collective-permute-start.32 = (f32[1056,128]{1,0:T(8,128)S(1)}, f32[1056,128]{1,0:T(8,128)S(1)}, u32[]{:S(2)}, u32[]{:S(2)}) collective-permute-start(f32[1056,128]{1,0:T(8,128)S(1)} %get-tuple-element.324), channel_id=1, source_target_pairs={{0,1},{1,0},{2,3},{3,2},{4,5},{5,4},{6,7},{7,6},{8,9},{9,8},{10,11... | collective-permute-start | bytes 1622024 | tf_op jit(solution)/shard_map/ppermute | solution.py:762
  132.4 17.8 %collective-permute-start.27 = (f32[136,512]{1,0:T(8,128)S(1)}, f32[136,512]{1,0:T(8,128)S(1)}, u32[]{:S(2)}, u32[]{:S(2)}) collective-permute-start(f32[136,512]{1,0:T(8,128)S(1)} %get-tuple-element.428.refs_4_.refs_7_.refs_5_), channel_id=1, source_target_pairs={{0,24},{4,28},{8,16},{12,20},{16,8},{20,12},{24,0},{28,4},{1,25},{... | collective-permute-start | bytes 835592 | tf_op jit(solution)/shard_map/ppermute | solution.py:603
  134.0 22.7 %collective-permute-start.31 = (f32[1056,128]{1,0:T(8,128)S(1)}, f32[1056,128]{1,0:T(8,128)S(1)}, u32[]{:S(2)}, u32[]{:S(2)}) collective-permute-start(f32[1056,128]{1,0:T(8,128)S(1)} %add.110.s_ref), channel_id=1, source_target_pairs={{1,2},{2,1},{5,6},{6,5},{9,10},{10,9},{13,14},{14,13},{17,18},{18,... | collective-permute-start | bytes 1622024 | tf_op jit(solution)/shard_map/ppermute | solution.py:861
  147.2 19.0 %collective-permute-start.37 = (f32[1056,128]{1,0:T(8,128)}, f32[1056,128]{1,0:T(8,128)}, u32[]{:S(2)}, u32[]{:S(2)}) collective-permute-start(f32[1056,128]{1,0:T(8,128)} %get-tuple-element.341), channel_id=1, source_target_pairs={{0,1},{1,0},{2,3},{3,2},{4,5},{5,4},{6,7},{7,6},{8,9},{9,8},{10,11... | collective-permute-start | bytes 1622024 | tf_op jit(solution)/shard_map/ppermute | solution.py:762
  155.7 26.5 %collective-permute-start.39 = (f32[1408,128]{1,0:T(8,128)}, f32[1408,128]{1,0:T(8,128)}, u32[]{:S(2)}, u32[]{:S(2)}) collective-permute-start(f32[1408,128]{1,0:T(8,128)} %dmap.12), channel_id=1, source_target_pairs={{0,24},{4,28},{8,16},{12,20},{16,8},{20,12},{24,0},{28,4},{1,25},{... | collective-permute-start | bytes 2162696 | tf_op jit(solution)/shard_map/ppermute | solution.py:603
  193.4 17.7 %collective-permute-start.42 = (f32[1056,128]{1,0:T(8,128)S(1)}, f32[1056,128]{1,0:T(8,128)S(1)}, u32[]{:S(2)}, u32[]{:S(2)}) collective-permute-start(f32[1056,128]{1,0:T(8,128)S(1)} %get-tuple-element.378), channel_id=1, source_target_pairs={{0,1},{1,0},{2,3},{3,2},{4,5},{5,4},{6,7},{7,6},{8,9},{9,8},{10,11... | collective-permute-start | bytes 1622024 | tf_op jit(solution)/shard_map/ppermute | solution.py:762
  208.0 32.8 %collective-permute-start.52 = (f32[704,512]{1,0:T(8,128)S(1)}, f32[704,512]{1,0:T(8,128)S(1)}, u32[]{:S(2)}, u32[]{:S(2)}) collective-permute-start(f32[704,512]{1,0:T(8,128)S(1)} %egrad.3), channel_id=1, source_target_pairs={{0,4},{4,0},{8,12},{12,8},{16,20},{20,16},{24,28},{28,24},{1,5},{5... | collective-permute-start | bytes 4325384 | tf_op jit(solution)/shard_map/ppermute | solution.py:603
  208.0 32.8 %collective-permute-start.53 = (f32[704,512]{1,0:T(8,128)S(1)}, f32[704,512]{1,0:T(8,128)S(1)}, u32[]{:S(2)}, u32[]{:S(2)}) collective-permute-start(f32[704,512]{1,0:T(8,128)S(1)} %egrad.4), channel_id=1, source_target_pairs={{0,4},{4,0},{8,12},{12,8},{16,20},{20,16},{24,28},{28,24},{1,5},{5... | collective-permute-start | bytes 4325384 | tf_op jit(solution)/shard_map/ppermute | solution.py:603
  221.6 23.8 %collective-permute-start.51 = (f32[1056,128]{1,0:T(8,128)S(1)}, f32[1056,128]{1,0:T(8,128)S(1)}, u32[]{:S(2)}, u32[]{:S(2)}) collective-permute-start(f32[1056,128]{1,0:T(8,128)S(1)} %add.117.refs_3_.refs_2_), channel_id=1, source_target_pairs={{0,1},{1,0},{2,3},{3,2},{4,5},{5,4},{6,7},{7,6},{8,9},{9,8},{10,11... | collective-permute-start | bytes 1622024 | tf_op jit(solution)/shard_map/ppermute | solution.py:762
  228.2 22.0 %collective-permute-start.48 = (f32[1056,128]{1,0:T(8,128)S(1)}, f32[1056,128]{1,0:T(8,128)S(1)}, u32[]{:S(2)}, u32[]{:S(2)}) collective-permute-start(f32[1056,128]{1,0:T(8,128)S(1)} %add.119.refs_3_.refs_2_), channel_id=1, source_target_pairs={{0,1},{1,0},{2,3},{3,2},{4,5},{5,4},{6,7},{7,6},{8,9},{9,8},{10,11... | collective-permute-start | bytes 1622024 | tf_op jit(solution)/shard_map/ppermute | solution.py:762
  231.7 26.6 %collective-permute-start.50 = (f32[1056,128]{1,0:T(8,128)S(1)}, f32[1056,128]{1,0:T(8,128)S(1)}, u32[]{:S(2)}, u32[]{:S(2)}) collective-permute-start(f32[1056,128]{1,0:T(8,128)S(1)} %add.120.refs_3_), channel_id=1, source_target_pairs={{0,1},{1,0},{2,3},{3,2},{4,5},{5,4},{6,7},{7,6},{8,9},{9,8},{10,11... | collective-permute-start | bytes 1622024 | tf_op jit(solution)/shard_map/ppermute | solution.py:762
  (88 other events, 942.0 us)

commit v5 on v4

--- a/solution.py
+++ b/solution.py
@@ -726,8 +726,10 @@
         return ((odd, 0, half), (odd, half, half))
 
     blocks = [0, 1, 2, 4, 3, 5, 6, 7] if n_blk == 8 else [r for m in [0, *far] for r in (m, m + 1)]
-    long = 3 * half // 2
-    sizes = [long, long, half] + [long] * ((cells - 2 * rows) // long)
+    long = 848
+    short = 2 * rows // 3 // 16 * 16
+    sizes = [2 * rows - 2 * short, short, short] + [long] * ((cells - 2 * rows) // long)
+    sizes += [n for n in [cells - sum(sizes)] if n]
     starts = [sum(sizes[:t]) for t in range(len(sizes))]
     count, lag = len(sizes), 3
     assert starts[3] == 2 * rows and sum(sizes) == cells
@@ -819,7 +821,7 @@
 
     def scalars():
         state["scalars"] = order(
-            functools.partial(scalar_results, n_blk // 2, cells, spots, long, end),
+            functools.partial(scalar_results, n_blk // 2, cells, spots, sizes[0], end),
             (*[tails[m] for m in range(0, n_blk, 2)], got[lag], total_of[0], by_cell),
             (state["kl"],),
         )
@@ -827,22 +829,20 @@
     def expr():
         state["expr"] = expr_part(0, (0, 1), (state["swapped", 0], state["swapped", 1]))
 
-    late = count - 11
     plan = {
         (0, "between"): [first_dmap],
         (1, "after"): [kl],
         (2, "between"): [second_dmap],
-        (4, "between"): [third_dmap],
-        (5, "between"): [fourth_dmap],
-        (late + 7, "between"): [functools.partial(egrad, 0)],
-        (late + 8, "between"): [functools.partial(egrad, 1)],
-        (late + 11, "between"): [scalars],
-        (late + 12, "between"): [expr],
+        (5, "between"): [third_dmap],
+        (7, "between"): [fourth_dmap, functools.partial(egrad, 0)],
+        (8, "between"): [functools.partial(egrad, 1)],
+        (count, "between"): [scalars],
+        (count + 1, "between"): [expr],
     }
     for k in range(len(blocks)):
         t = last_piece[k] + lag + 1
         if t < count + lag:
-            plan.setdefault((t, "after"), []).append(functools.partial(finish, k))
+            plan.setdefault((t, "between"), []).append(functools.partial(finish, k))
 
     def extra(t, place):
         for step in plan.get((t, place), ()):

time: 263 us -> 261 us (level)
  waiting for transfers between devices: 67.2 us -> 50.7 us
  starting transfers between devices: 85.6 us -> 98.4 us
    ppermute x25, waiting for transfers between devices: 42.1 us -> 29.4 us  [swap(): return lax.ppermute(x, 'blk', [(i, i ^ m) for i in range(n_blk)])]
    ppermute x14 -> x16, starting transfers between devices: 42.5 us -> 53.4 us  [send(): got[t] = lax.ppermute(buffer, 'gene', PAIR)]
    ppermute x14 -> x16, waiting for transfers between devices: 21.2 us -> 17.3 us  [send(): got[t] = lax.ppermute(buffer, 'gene', PAIR)]
    pallas_call x8 -> x10, Pallas kernels: 10.6 us -> 12.4 us  [next_piece(): pl.pallas_call(functools.partial(next_kernel, cuts), in_specs=[SMEM] + [V...]
    ppermute x11 -> x13, starting transfers between devices: 10.3 us -> 11.7 us  [shards(): mid[t] = lax.ppermute(part[t], 'gene', MIDDLE)]
    unnamed x116 -> x124, local copies, waits for them, and re-layouts: 13.2 us -> 13.7 us
    pallas_call x18 -> x20, Pallas kernels: 6.64 us -> 6.58 us  [plus(): pl.pallas_call(add_kernel, in_specs=[VMEM, VMEM], out_specs=VMEM, out_sha...]
  transfers between devices with their start and end apart: 54 -> 58, of which waited for: 19 -> 18; matrix products, arithmetic and copies ran while one was open for 1% -> 1% of each run, Pallas kernels for 33% -> 33%
where the time goes in v5:
time: 261 us; the launch traced here: 260 us
  starting transfers between devices  98.4 us (38%)
  Pallas kernels  92.9 us (36%)
  waiting for transfers between devices  50.7 us (19%)
  local copies, waits for them, and re-layouts  15.9 us (6%)
    ppermute x16, starting transfers between devices, send(): got[t] = lax.ppermute(buffer, 'gene', PAIR)  53.4 us
    ppermute x25, waiting for transfers between devices, swap(): return lax.ppermute(x, 'blk', [(i, i ^ m) for i in range(n_blk)])  29.4 us
    ppermute x25, starting transfers between devices, swap(): return lax.ppermute(x, 'blk', [(i, i ^ m) for i in range(n_blk)])  26 us
    pallas_call x8, Pallas kernels, final_block(): pl.pallas_call(functools.partial(final_kernel, place, cuts, step), in_spe...  23.2 us
    ppermute x16, waiting for transfers between devices, send(): got[t] = lax.ppermute(buffer, 'gene', PAIR)  17.3 us
    unnamed x124, local copies, waits for them, and re-layouts  13.7 us
    pallas_call x10, Pallas kernels, next_piece(): pl.pallas_call(functools.partial(next_kernel, cuts), in_specs=[SMEM] + [V...  12.4 us
    ppermute x13, starting transfers between devices, shards(): mid[t] = lax.ppermute(part[t], 'gene', MIDDLE)  11.7 us
  transfers between devices with their start and end apart: 58, of which 18 were waited for; matrix products, arithmetic and copies ran while one was open for 1% of the time, Pallas kernels for 33%

profile of v5, /device:TPU:0, one launch (start us, length us, event | category | flops | bytes accessed | tf_op | source)
XLA Modules:
  0.0 259.8 jit_solution(16489666650045237849)
XLA Ops:
  10.1 2.6 %copy-done.6 = f32[11264,128]{1,0:T(8,128)S(1)} copy-done((f32[11264,128]{1,0:T(8,128)S(1)}, f32[11264,128]{1,0:T(8,128)}, u32[]{:S(2)}) %copy-start.6) | copy-done | bytes 5767192
  22.7 6.9 %softmax.1 = (f32[1,128]{1,0:T(1,128)S(1)}, f32[32,512]{1,0:T(8,128)S(1)}, f32[11264,128]{1,0:T(8,128)}) custom-call(f32[11264,128]{1,0:T(8,128)S(1)} %copy-done.7), custom_call_target="tpu_custom_call" | custom-call | flops 1 | bytes 1 | tf_op jit(solution)/shard_map/softmax/pallas_call | solution.py:143
  42.1 8.6 %collective-permute-done.3.refs_0_.refs_1_ = f32[1408,128]{1,0:T(8,128)S(1)} collective-permute-done((f32[1408,128]{1,0:T(8,128)S(1)}, f32[1408,128]{1,0:T(8,128)S(1)}, u32[]{:S(2)}, u32[]{:S(2)}) %collective-permute-start.3) | collective-permute-done | bytes 720928 | tf_op jit(solution)/shard_map/ppermute | solution.py:603
  58.6 11.6 %collective-permute-done.9.refs_2_ = f32[160,512]{1,0:T(8,128)S(1)} collective-permute-done((f32[160,512]{1,0:T(8,128)S(1)}, f32[160,512]{1,0:T(8,128)S(1)}, u32[]{:S(2)}, u32[]{:S(2)}) %collective-permute-start.9) | collective-permute-done | bytes 327712 | tf_op jit(solution)/shard_map/ppermute | solution.py:603
  78.0 2.6 collective-permute-start.16
  103.8 3.8 %collective-permute-start.28 = (f32[928,128]{1,0:T(8,128)}, f32[928,128]{1,0:T(8,128)}, u32[]{:S(2)}, u32[]{:S(2)}) collective-permute-start(f32[928,128]{1,0:T(8,128)} %dmap.10.a_ref), channel_id=1, source_target_pairs={{0,1},{1,0},{2,3},{3,2},{4,5},{5,4},{6,7},{7,6},{8,9},{9,8},{10,11... | collective-permute-start | bytes 1425416 | tf_op jit(solution)/shard_map/ppermute | solution.py:764
  113.3 4.2 %ratio.1 = (f32[11264,128]{1,0:T(8,128)}, f32[16,704]{1,0:T(8,128)S(1)}, f32[8,128]{1,0:T(8,128)S(1)}, f32[8,128]{1,0:T(8,128)S(1)}) custom-call(f32[32,512]{1,0:T(8,128)S(1)} %copy-done.54, f32[16,704]{1,0:T(8,128)S(1)} %reshape.16.density_ref, ...), custom_call_target="tpu_custom_call", output_to_operand_aliasing={{0}: (3, {})} | custom-call | flops 1 | bytes 1 | tf_op jit(solution)/shard_map/ratio/pallas_call | solution.py:409
  119.9 3.6 %collective-permute-start.30 = (f32[968,128]{1,0:T(8,128)S(1)}, f32[968,128]{1,0:T(8,128)S(1)}, u32[]{:S(2)}, u32[]{:S(2)}) collective-permute-start(f32[968,128]{1,0:T(8,128)S(1)} %get-tuple-element.338), channel_id=1, source_target_pairs={{0,1},{1,0},{2,3},{3,2},{4,5},{5,4},{6,7},{7,6},{8,9},{9,8},{10,11... | collective-permute-start | bytes 1486856 | tf_op jit(solution)/shard_map/ppermute | solution.py:764
  139.4 4.9 %collective-permute-done.33.b_ref.refs_1_.refs_0_ = f32[928,128]{1,0:T(8,128)S(1)} collective-permute-done((f32[928,128]{1,0:T(8,128)S(1)}, f32[928,128]{1,0:T(8,128)S(1)}, u32[]{:S(2)}, u32[]{:S(2)}) %collective-permute-start.33) | collective-permute-done | bytes 475168 | tf_op jit(solution)/shard_map/ppermute | solution.py:764
  144.3 4.0 %collective-permute-start.32 = (f32[928,128]{1,0:T(8,128)}, f32[928,128]{1,0:T(8,128)}, u32[]{:S(2)}, u32[]{:S(2)}) collective-permute-start(f32[928,128]{1,0:T(8,128)} %get-tuple-element.350), channel_id=1, source_target_pairs={{0,1},{1,0},{2,3},{3,2},{4,5},{5,4},{6,7},{7,6},{8,9},{9,8},{10,11... | collective-permute-start | bytes 1425416 | tf_op jit(solution)/shard_map/ppermute | solution.py:764
  165.3 3.0 %final.8 = (f32[11264,128]{1,0:T(8,128)}, f32[11264,128]{1,0:T(8,128)}) custom-call(s32[1]{0:T(128)} %bitcast.end_ref, s32[26]{0:T(128)S(1)} %stack.107.at_ref, f32[968,128]{1,0:T(8,128)S(1)} %copy-done.28, f32[928,128]{1,0:T(8,128)S(1)} %copy-done.31, f32[968,128]{1,0:T(8,128)S(1)} %copy-done.39, ...), custom_call_target="tpu_custom_call", output_to_operand_aliasing={{0}: (9, {}), {1}: (10, {})} | custom-call | flops 1 | bytes 1 | tf_op jit(solution)/shard_map/final/pallas_call | solution.py:548
  173.9 3.4 %final.9 = (f32[11264,128]{1,0:T(8,128)}, f32[11264,128]{1,0:T(8,128)}) custom-call(s32[1]{0:T(128)} %bitcast.end_ref, s32[26]{0:T(128)S(1)} %stack.107.at_ref, f32[928,128]{1,0:T(8,128)S(1)} %copy-done.32, f32[928,128]{1,0:T(8,128)} %collective-permute-done.32.b_ref.refs_1_, ...), custom_call_target="tpu_custom_call", output_to_operand_aliasing={{0}: (9, {}), {1}: (10, {})} | custom-call | flops 1 | bytes 1 | tf_op jit(solution)/shard_map/final/pallas_call | solution.py:548
  188.7 5.0 %collective-permute-start.44 = (f32[848,128]{1,0:T(8,128)S(1)}, f32[848,128]{1,0:T(8,128)S(1)}, u32[]{:S(2)}, u32[]{:S(2)}) collective-permute-start(f32[848,128]{1,0:T(8,128)S(1)} %get-tuple-element.413), channel_id=1, source_target_pairs={{0,1},{1,0},{2,3},{3,2},{4,5},{5,4},{6,7},{7,6},{8,9},{9,8},{10,11... | collective-permute-start | bytes 1302536 | tf_op jit(solution)/shard_map/ppermute | solution.py:764
  196.1 3.2 %final.10 = (f32[11264,128]{1,0:T(8,128)}, f32[11264,128]{1,0:T(8,128)}) custom-call(s32[1]{0:T(128)} %bitcast.end_ref, s32[26]{0:T(128)S(1)} %stack.107.at_ref, f32[848,128]{1,0:T(8,128)} %collective-permute-done.36.b_ref.refs_0_, f32[848,128]{1,0:T(8,128)S(1)} %collective-permute-done.40.b_ref.refs_1_.refs_0_, ...), custom_call_target="tpu_custom_call", output_to_operand_aliasing={{0}: (9, {}), {1}: (10, {})} | custom-call | flops 1 | bytes 1 | tf_op jit(solution)/shard_map/final/pallas_call | solution.py:548
  206.2 8.8 %collective-permute-start.46 = (f32[848,128]{1,0:T(8,128)S(1)}, f32[848,128]{1,0:T(8,128)S(1)}, u32[]{:S(2)}, u32[]{:S(2)}) collective-permute-start(f32[848,128]{1,0:T(8,128)S(1)} %get-tuple-element.425), channel_id=1, source_target_pairs={{0,1},{1,0},{2,3},{3,2},{4,5},{5,4},{6,7},{7,6},{8,9},{9,8},{10,11... | collective-permute-start | bytes 1302536 | tf_op jit(solution)/shard_map/ppermute | solution.py:764
  215.0 2.7 %final.11 = (f32[11264,128]{1,0:T(8,128)}, f32[11264,128]{1,0:T(8,128)}) custom-call(s32[1]{0:T(128)} %bitcast.end_ref, s32[26]{0:T(128)S(1)} %stack.107.at_ref, f32[848,128]{1,0:T(8,128)S(1)} %collective-permute-done.40.b_ref.refs_1_.refs_0_, f32[848,128]{1,0:T(8,128)S(1)} %collective-permute-done.39.b_ref.refs_1_, ...), custom_call_target="tpu_custom_call", output_to_operand_aliasing={{0}: (11, {}), {1}: (12, {})} | custom-call | flops 1 | bytes 1 | tf_op jit(solution)/shard_map/final/pallas_call | solution.py:548
  221.3 2.8 %final.12 = (f32[11264,128]{1,0:T(8,128)}, f32[11264,128]{1,0:T(8,128)}) custom-call(s32[1]{0:T(128)} %bitcast.end_ref, s32[26]{0:T(128)S(1)} %stack.107.at_ref, f32[848,128]{1,0:T(8,128)S(1)} %collective-permute-done.44.b_ref.refs_2_.refs_0_, ...), custom_call_target="tpu_custom_call", output_to_operand_aliasing={{0}: (9, {}), {1}: (10, {})} | custom-call | flops 1 | bytes 1 | tf_op jit(solution)/shard_map/final/pallas_call | solution.py:548
  225.5 4.7 %collective-permute-done.50.b_ref.refs_2_.refs_0_ = f32[848,128]{1,0:T(8,128)S(1)} collective-permute-done((f32[848,128]{1,0:T(8,128)S(1)}, f32[848,128]{1,0:T(8,128)S(1)}, u32[]{:S(2)}, u32[]{:S(2)}) %collective-permute-start.50) | collective-permute-done | bytes 434208 | tf_op jit(solution)/shard_map/ppermute | solution.py:764
  231.0 4.9 %collective-permute-start.55 = (f32[848,128]{1,0:T(8,128)S(1)}, f32[848,128]{1,0:T(8,128)S(1)}, u32[]{:S(2)}, u32[]{:S(2)}) collective-permute-start(f32[848,128]{1,0:T(8,128)S(1)} %add.121.refs_4_), channel_id=1, source_target_pairs={{0,1},{1,0},{2,3},{3,2},{4,5},{5,4},{6,7},{7,6},{8,9},{9,8},{10,11... | collective-permute-start | bytes 1302536 | tf_op jit(solution)/shard_map/ppermute | solution.py:764
  235.9 5.7 %collective-permute-start.52 = (f32[848,128]{1,0:T(8,128)S(1)}, f32[848,128]{1,0:T(8,128)S(1)}, u32[]{:S(2)}, u32[]{:S(2)}) collective-permute-start(f32[848,128]{1,0:T(8,128)S(1)} %add.123.refs_5_.refs_2_), channel_id=1, source_target_pairs={{0,1},{1,0},{2,3},{3,2},{4,5},{5,4},{6,7},{7,6},{8,9},{9,8},{10,11... | collective-permute-start | bytes 1302536 | tf_op jit(solution)/shard_map/ppermute | solution.py:764
  242.3 2.7 %final.13 = (f32[11264,128]{1,0:T(8,128)}, f32[11264,128]{1,0:T(8,128)}) custom-call(s32[1]{0:T(128)} %bitcast.end_ref, s32[26]{0:T(128)S(1)} %stack.107.at_ref, f32[848,128]{1,0:T(8,128)S(1)} %collective-permute-done.47.b_ref.refs_1_.refs_0_, f32[848,128]{1,0:T(8,128)S(1)} %collective-permute-done.46.b_ref.refs_1_, ...), custom_call_target="tpu_custom_call", output_to_operand_aliasing={{0}: (11, {}), {1}: (12, {})} | custom-call | flops 1 | bytes 1 | tf_op jit(solution)/shard_map/final/pallas_call | solution.py:548
  246.1 4.6 %egrad.5 = f32[1408,512]{1,0:T(8,128)} custom-call(s32[26]{0:T(128)S(1)} %stack.107.at_ref, f32[2816,128]{1,0:T(8,128)S(1)} %copy-done.9, f32[1408,128]{1,0:T(8,128)S(1)} %copy-done.34, f32[1408,128]{1,0:T(8,128)S(1)} %copy-done.36, f32[1408,128]{1,0:T(8,128)S(1)} %copy-done.17, f32[1408,128]{1,0:T(8,128)S(1)} %copy-done.15, ...), custom_call_target="tpu_custom_call" | custom-call | flops 1 | bytes 1 | tf_op jit(solution)/shard_map/egrad/pallas_call | solution.py:369
  252.4 2.7 %final.14 = (f32[11264,128]{1,0:T(8,128)}, f32[11264,128]{1,0:T(8,128)}) custom-call(s32[1]{0:T(128)} %bitcast.end_ref, s32[26]{0:T(128)S(1)} %stack.107.at_ref, f32[848,128]{1,0:T(8,128)S(1)} %collective-permute-done.50.b_ref.refs_2_.refs_0_, f32[848,128]{1,0:T(8,128)S(1)} %collective-permute-done.55.refs_1_, ...), custom_call_target="tpu_custom_call", output_to_operand_aliasing={{0}: (11, {}), {1}: (12, {})} | custom-call | flops 1 | bytes 1 | tf_op jit(solution)/shard_map/final/pallas_call | solution.py:548
  256.9 2.7 %final.15 = (f32[11264,128]{1,0:T(8,128)}, f32[11264,128]{1,0:T(8,128)}) custom-call(s32[1]{0:T(128)} %bitcast.end_ref, s32[26]{0:T(128)S(1)} %stack.107.at_ref, f32[848,128]{1,0:T(8,128)S(1)} %collective-permute-done.52.refs_2_.refs_0_, f32[816,128]{1,0:T(8,128)S(1)} %collective-permute-done.54.refs_1_, ...), custom_call_target="tpu_custom_call", output_to_operand_aliasing={{0}: (9, {}), {1}: (10, {})} | custom-call | flops 1 | bytes 1 | tf_op jit(solution)/shard_map/final/pallas_call | solution.py:548
  (285 shorter events, 148.1 us)
Async XLA Ops:
  0.6 28.9 %collective-permute-start = (f32[1408,512]{1,0:T(8,128)}, f32[1408,512]{1,0:T(8,128)}, u32[]{:S(2)}, u32[]{:S(2)}) collective-permute-start(f32[1408,512]{1,0:T(8,128)} %x_ref), channel_id=1, source_target_pairs={{0,4},{4,0},{8,12},{12,8},{16,20},{20,16},{24,28},{28,24},{1,5},{5... | collective-permute-start | bytes 8650760 | tf_op jit(solution)/shard_map/ppermute | solution.py:603
  17.6 20.1 %collective-permute-start.5 = (f32[1408,128]{1,0:T(8,128)S(1)}, f32[1408,128]{1,0:T(8,128)S(1)}, u32[]{:S(2)}, u32[]{:S(2)}) collective-permute-start(f32[1408,128]{1,0:T(8,128)S(1)} %get-tuple-element.271), channel_id=1, source_target_pairs={{0,24},{4,28},{8,16},{12,20},{16,8},{20,12},{24,0},{28,4},{1,25},{... | collective-permute-start | bytes 2162696 | tf_op jit(solution)/shard_map/ppermute | solution.py:603
  19.1 21.5 %collective-permute-start.4 = (f32[1408,128]{1,0:T(8,128)S(1)}, f32[1408,128]{1,0:T(8,128)S(1)}, u32[]{:S(2)}, u32[]{:S(2)}) collective-permute-start(f32[1408,128]{1,0:T(8,128)S(1)} %join.1), channel_id=1, source_target_pairs={{0,1},{1,0},{2,3},{3,2},{4,5},{5,4},{6,7},{7,6},{8,9},{9,8},{10,11... | collective-permute-start | bytes 2162696 | tf_op jit(solution)/shard_map/ppermute | solution.py:606
  20.6 30.0 %collective-permute-start.3 = (f32[1408,128]{1,0:T(8,128)S(1)}, f32[1408,128]{1,0:T(8,128)S(1)}, u32[]{:S(2)}, u32[]{:S(2)}) collective-permute-start(f32[1408,128]{1,0:T(8,128)S(1)} %get-tuple-element.266), channel_id=1, source_target_pairs={{0,8},{4,12},{8,0},{12,4},{16,24},{20,28},{24,16},{28,20},{1,9},{5... | collective-permute-start | bytes 2162696 | tf_op jit(solution)/shard_map/ppermute | solution.py:603
  21.2 32.5 %collective-permute-start.8 = (f32[1408,128]{1,0:T(8,128)S(1)}, f32[1408,128]{1,0:T(8,128)S(1)}, u32[]{:S(2)}, u32[]{:S(2)}) collective-permute-start(f32[1408,128]{1,0:T(8,128)S(1)} %get-tuple-element.284), channel_id=1, source_target_pairs={{0,16},{4,20},{8,24},{12,28},{16,0},{20,4},{24,8},{28,12},{1,17},{... | collective-permute-start | bytes 2162696 | tf_op jit(solution)/shard_map/ppermute | solution.py:603
  37.6 18.8 %collective-permute-start.10 = (f32[1408,128]{1,0:T(8,128)S(1)}, f32[1408,128]{1,0:T(8,128)S(1)}, u32[]{:S(2)}, u32[]{:S(2)}) collective-permute-start(f32[1408,128]{1,0:T(8,128)S(1)} %collective-permute-done.5.refs_0_.refs_5_.refs_3_), channel_id=1, source_target_pairs={{0,1},{1,0},{2,3},{3,2},{4,5},{5,4},{6,7},{7,6},{8,9},{9,8},{10,11... | collective-permute-start | bytes 2162696 | tf_op jit(solution)/shard_map/ppermute | solution.py:606
  52.1 18.1 %collective-permute-start.7 = (f32[160,512]{1,0:T(8,128)S(1)}, f32[160,512]{1,0:T(8,128)S(1)}, u32[]{:S(2)}, u32[]{:S(2)}) collective-permute-start(f32[160,512]{1,0:T(8,128)S(1)} %pred_.11), channel_id=1, source_target_pairs={{0,8},{4,12},{8,0},{12,4},{16,24},{20,28},{24,16},{28,20},{1,9},{5... | collective-permute-start | bytes 983048 | tf_op jit(solution)/shard_map/ppermute | solution.py:603
  94.9 22.7 %collective-permute-start.22 = (f32[1408,128]{1,0:T(8,128)}, f32[1408,128]{1,0:T(8,128)}, u32[]{:S(2)}, u32[]{:S(2)}) collective-permute-start(f32[1408,128]{1,0:T(8,128)} %get-tuple-element.314), channel_id=1, source_target_pairs={{0,8},{4,12},{8,0},{12,4},{16,24},{20,28},{24,16},{28,20},{1,9},{5... | collective-permute-start | bytes 2162696 | tf_op jit(solution)/shard_map/ppermute | solution.py:603
  97.7 27.1 %collective-permute-start.24 = (f32[1408,128]{1,0:T(8,128)}, f32[1408,128]{1,0:T(8,128)}, u32[]{:S(2)}, u32[]{:S(2)}) collective-permute-start(f32[1408,128]{1,0:T(8,128)} %get-tuple-element.330), channel_id=1, source_target_pairs={{0,16},{4,20},{8,24},{12,28},{16,0},{20,4},{24,8},{28,12},{1,17},{... | collective-permute-start | bytes 2162696 | tf_op jit(solution)/shard_map/ppermute | solution.py:603
  103.8 23.1 %collective-permute-start.28 = (f32[928,128]{1,0:T(8,128)}, f32[928,128]{1,0:T(8,128)}, u32[]{:S(2)}, u32[]{:S(2)}) collective-permute-start(f32[928,128]{1,0:T(8,128)} %dmap.10.a_ref), channel_id=1, source_target_pairs={{0,1},{1,0},{2,3},{3,2},{4,5},{5,4},{6,7},{7,6},{8,9},{9,8},{10,11... | collective-permute-start | bytes 1425416 | tf_op jit(solution)/shard_map/ppermute | solution.py:764
  110.8 19.0 %collective-permute-start.31 = (f32[928,128]{1,0:T(8,128)}, f32[928,128]{1,0:T(8,128)}, u32[]{:S(2)}, u32[]{:S(2)}) collective-permute-start(f32[928,128]{1,0:T(8,128)} %add.109.s_ref), channel_id=1, source_target_pairs={{1,2},{2,1},{5,6},{6,5},{9,10},{10,9},{13,14},{14,13},{17,18},{18,... | collective-permute-start | bytes 1425416 | tf_op jit(solution)/shard_map/ppermute | solution.py:861
  126.1 23.1 %collective-permute-start.25 = (f32[1416,128]{1,0:T(8,128)S(1)}, f32[1416,128]{1,0:T(8,128)S(1)}, u32[]{:S(2)}, u32[]{:S(2)}) collective-permute-start(f32[1416,128]{1,0:T(8,128)S(1)} %get-tuple-element.333), channel_id=1, source_target_pairs={{0,8},{4,12},{8,0},{12,4},{16,24},{20,28},{24,16},{28,20},{1,9},{5... | collective-permute-start | bytes 2174984 | tf_op jit(solution)/shard_map/ppermute | solution.py:603
  128.8 27.0 %collective-permute-start.26 = (f32[1416,128]{1,0:T(8,128)S(1)}, f32[1416,128]{1,0:T(8,128)S(1)}, u32[]{:S(2)}, u32[]{:S(2)}) collective-permute-start(f32[1416,128]{1,0:T(8,128)S(1)} %get-tuple-element.334), channel_id=1, source_target_pairs={{0,16},{4,20},{8,24},{12,28},{16,0},{20,4},{24,8},{28,12},{1,17},{... | collective-permute-start | bytes 2174984 | tf_op jit(solution)/shard_map/ppermute | solution.py:603
  134.7 21.1 %collective-permute-start.27 = (f32[136,512]{1,0:T(8,128)S(1)}, f32[136,512]{1,0:T(8,128)S(1)}, u32[]{:S(2)}, u32[]{:S(2)}) collective-permute-start(f32[136,512]{1,0:T(8,128)S(1)} %get-tuple-element.478.refs_4_.refs_7_.refs_5_), channel_id=1, source_target_pairs={{0,24},{4,28},{8,16},{12,20},{16,8},{20,12},{24,0},{28,4},{1,25},{... | collective-permute-start | bytes 835592 | tf_op jit(solution)/shard_map/ppermute | solution.py:603
  144.3 24.1 %collective-permute-start.32 = (f32[928,128]{1,0:T(8,128)}, f32[928,128]{1,0:T(8,128)}, u32[]{:S(2)}, u32[]{:S(2)}) collective-permute-start(f32[928,128]{1,0:T(8,128)} %get-tuple-element.350), channel_id=1, source_target_pairs={{0,1},{1,0},{2,3},{3,2},{4,5},{5,4},{6,7},{7,6},{8,9},{9,8},{10,11... | collective-permute-start | bytes 1425416 | tf_op jit(solution)/shard_map/ppermute | solution.py:764
  149.2 21.0 %collective-permute-start.37 = (f32[848,128]{1,0:T(8,128)}, f32[848,128]{1,0:T(8,128)}, u32[]{:S(2)}, u32[]{:S(2)}) collective-permute-start(f32[848,128]{1,0:T(8,128)} %add.113.s_ref), channel_id=1, source_target_pairs={{1,2},{2,1},{5,6},{6,5},{9,10},{10,9},{13,14},{14,13},{17,18},{18,... | collective-permute-start | bytes 1302536 | tf_op jit(solution)/shard_map/ppermute | solution.py:861
  154.1 23.3 %collective-permute-start.36 = (f32[848,128]{1,0:T(8,128)}, f32[848,128]{1,0:T(8,128)}, u32[]{:S(2)}, u32[]{:S(2)}) collective-permute-start(f32[848,128]{1,0:T(8,128)} %get-tuple-element.372), channel_id=1, source_target_pairs={{0,1},{1,0},{2,3},{3,2},{4,5},{5,4},{6,7},{7,6},{8,9},{9,8},{10,11... | collective-permute-start | bytes 1302536 | tf_op jit(solution)/shard_map/ppermute | solution.py:764
  158.9 28.5 %collective-permute-start.42 = (f32[1408,128]{1,0:T(8,128)}, f32[1408,128]{1,0:T(8,128)}, u32[]{:S(2)}, u32[]{:S(2)}) collective-permute-start(f32[1408,128]{1,0:T(8,128)} %dmap.12), channel_id=1, source_target_pairs={{0,24},{4,28},{8,16},{12,20},{16,8},{20,12},{24,0},{28,4},{1,25},{... | collective-permute-start | bytes 2162696 | tf_op jit(solution)/shard_map/ppermute | solution.py:603
  179.6 19.7 %collective-permute-start.39 = (f32[848,128]{1,0:T(8,128)S(1)}, f32[848,128]{1,0:T(8,128)S(1)}, u32[]{:S(2)}, u32[]{:S(2)}) collective-permute-start(f32[848,128]{1,0:T(8,128)S(1)} %get-tuple-element.392), channel_id=1, source_target_pairs={{0,1},{1,0},{2,3},{3,2},{4,5},{5,4},{6,7},{7,6},{8,9},{9,8},{10,11... | collective-permute-start | bytes 1302536 | tf_op jit(solution)/shard_map/ppermute | solution.py:764
  183.1 21.5 %collective-permute-start.38 = (f32[1416,128]{1,0:T(8,128)S(1)}, f32[1416,128]{1,0:T(8,128)S(1)}, u32[]{:S(2)}, u32[]{:S(2)}) collective-permute-start(f32[1416,128]{1,0:T(8,128)S(1)} %dmap.13), channel_id=1, source_target_pairs={{0,24},{4,28},{8,16},{12,20},{16,8},{20,12},{24,0},{28,4},{1,25},{... | collective-permute-start | bytes 2174984 | tf_op jit(solution)/shard_map/ppermute | solution.py:603
  204.4 41.6 %collective-permute-start.56 = (f32[704,512]{1,0:T(8,128)S(1)}, f32[704,512]{1,0:T(8,128)S(1)}, u32[]{:S(2)}, u32[]{:S(2)}) collective-permute-start(f32[704,512]{1,0:T(8,128)S(1)} %egrad.3), channel_id=1, source_target_pairs={{0,4},{4,0},{8,12},{12,8},{16,20},{20,16},{24,28},{28,24},{1,5},{5... | collective-permute-start | bytes 4325384 | tf_op jit(solution)/shard_map/ppermute | solution.py:603
  204.5 41.5 %collective-permute-start.57 = (f32[704,512]{1,0:T(8,128)S(1)}, f32[704,512]{1,0:T(8,128)S(1)}, u32[]{:S(2)}, u32[]{:S(2)}) collective-permute-start(f32[704,512]{1,0:T(8,128)S(1)} %egrad.4), channel_id=1, source_target_pairs={{0,4},{4,0},{8,12},{12,8},{16,20},{20,16},{24,28},{28,24},{1,5},{5... | collective-permute-start | bytes 4325384 | tf_op jit(solution)/shard_map/ppermute | solution.py:603
  206.2 18.5 %collective-permute-start.46 = (f32[848,128]{1,0:T(8,128)S(1)}, f32[848,128]{1,0:T(8,128)S(1)}, u32[]{:S(2)}, u32[]{:S(2)}) collective-permute-start(f32[848,128]{1,0:T(8,128)S(1)} %get-tuple-element.425), channel_id=1, source_target_pairs={{0,1},{1,0},{2,3},{3,2},{4,5},{5,4},{6,7},{7,6},{8,9},{9,8},{10,11... | collective-permute-start | bytes 1302536 | tf_op jit(solution)/shard_map/ppermute | solution.py:764
  231.0 19.7 %collective-permute-start.55 = (f32[848,128]{1,0:T(8,128)S(1)}, f32[848,128]{1,0:T(8,128)S(1)}, u32[]{:S(2)}, u32[]{:S(2)}) collective-permute-start(f32[848,128]{1,0:T(8,128)S(1)} %add.121.refs_4_), channel_id=1, source_target_pairs={{0,1},{1,0},{2,3},{3,2},{4,5},{5,4},{6,7},{7,6},{8,9},{9,8},{10,11... | collective-permute-start | bytes 1302536 | tf_op jit(solution)/shard_map/ppermute | solution.py:764
  (96 other events, 1044.8 us)

commit v6 on v5

--- a/solution.py
+++ b/solution.py
@@ -104,7 +104,8 @@
 
 def by_cell_rows(ref, count, step):
     genes = ref.shape[1]
-    return jnp.concatenate([ref[:count, :], ref[count : 2 * count, : step - genes]], axis=1)
+    rest = [ref[count : count + count // 2, at : at + step - genes] for at in (0, genes // 2)]
+    return jnp.concatenate([ref[:count, :], jnp.concatenate(rest, axis=0)], axis=1)
 
 
 def softmax_kernel(spots, scale, step, l_ref, inv_ref, cell_ref, o_ref, buffer, sem):
@@ -121,7 +122,7 @@
     inv_ref[...] = inv
     ones = jnp.ones((16, width), BF16)
 
-    def row(k, square):
+    def row(at, k, square):
         e = jnp.exp(l_ref[at_rows(k, step), :])
         share = e * inv
         buffer[at_rows(k, step), :] = e * scale
@@ -130,11 +131,14 @@
         sums = [lax.dot_general(ones, x, (((1,), (1,)), ((), ())), preferred_element_type=F32) for x in (high, low)]
         sums = (sums[0] + sums[1])[0:1, :] * (1.0 / spots)
         cell_ref[pl.ds(k, 1), :] = sums[:, :genes]
-        cell_ref[pl.ds(count + k, 1), : step - genes] = sums[:, genes:]
+        cell_ref[pl.ds(count + k - at * (count // 2), 1), at * (genes // 2) : at * (genes // 2) + step - genes] = sums[:, genes:]
         return square + jnp.sum((share * share).reshape(step // 8, 8, width), axis=0)
 
-    square = lax.fori_loop(0, count, row, jnp.zeros((8, width), F32))
-    cell_ref[count:, step - genes :] = jnp.full((count, 2 * genes - step), jnp.sum(square), F32)
+    square = lax.fori_loop(0, count // 2, functools.partial(row, 0), jnp.zeros((8, width), F32))
+    square = lax.fori_loop(count // 2, count, functools.partial(row, 1), square)
+    for at in (0, genes // 2):
+        left = genes // 2 - (step - genes)
+        cell_ref[count:, at + step - genes : at + genes // 2] = jnp.full((count // 2, left), jnp.sum(square), F32)
     pltpu.make_async_copy(buffer, o_ref, sem).wait()
 
 
@@ -146,7 +150,7 @@
         out_specs=(VMEM, VMEM, HBM),
         out_shape=(
             jax.ShapeDtypeStruct((1, width), F32),
-            jax.ShapeDtypeStruct((2 * cells // step, genes), F32),
+            jax.ShapeDtypeStruct((3 * cells // (2 * step), genes), F32),
             pltpu.HBM((cells, width), F32),
         ),
         scratch_shapes=[pltpu.VMEM((cells, width), F32), pltpu.SemaphoreType.DMA],
@@ -570,7 +574,7 @@
     by_gene = jnp.where(end_ref[0] == 1, rx_ref[step : step + 8, :], s_ref[step : step + 8, :])
     cosine, fitted, wsum, scos = by_gene[0:1, :], sums[0][2:3, :], by_gene[3:4, :], sums[0][1:2, :]
     loss = -cosine / wsum - scos / spots + kl_ref[0:1, :]
-    rms_map = jnp.sqrt(q_ref[q_ref.shape[0] - 1 :, q_ref.shape[1] - LANES :] / (cells * spots))
+    rms_map = jnp.sqrt(q_ref[q_ref.shape[0] - 1 :, q_ref.shape[1] - 8 :] / (cells * spots))
     rms_pred = jnp.sqrt(fitted / (spots * GENES))
     for ref, value in zip((loss_ref, map_ref, pred_ref), (loss, rms_map, rms_pred), strict=True):
         ref[0, 0] = jnp.max(value)

time: 261 us -> 261 us (level)
  transfers between devices with their start and end apart: 58 -> 58, of which waited for: 18 -> 18; matrix products, arithmetic and copies ran while one was open for 1% -> 1% of each run, Pallas kernels for 33% -> 34%
where the time goes in v6:
time: 261 us; the launch traced here: 259 us
  starting transfers between devices  98.3 us (38%)
  Pallas kernels  93 us (36%)
  waiting for transfers between devices  50 us (19%)
  local copies, waits for them, and re-layouts  15.8 us (6%)
    ppermute x16, starting transfers between devices, send(): got[t] = lax.ppermute(buffer, 'gene', PAIR)  53.3 us
    ppermute x25, waiting for transfers between devices, swap(): return lax.ppermute(x, 'blk', [(i, i ^ m) for i in range(n_blk)])  28.7 us
    ppermute x25, starting transfers between devices, swap(): return lax.ppermute(x, 'blk', [(i, i ^ m) for i in range(n_blk)])  26 us
    pallas_call x8, Pallas kernels, final_block(): pl.pallas_call(functools.partial(final_kernel, place, cuts, step), in_spe...  23.2 us
    ppermute x16, waiting for transfers between devices, send(): got[t] = lax.ppermute(buffer, 'gene', PAIR)  17.3 us
    unnamed x124, local copies, waits for them, and re-layouts  13.7 us
    pallas_call x10, Pallas kernels, next_piece(): pl.pallas_call(functools.partial(next_kernel, cuts), in_specs=[SMEM] + [V...  12.4 us
    ppermute x13, starting transfers between devices, shards(): mid[t] = lax.ppermute(part[t], 'gene', MIDDLE)  11.7 us
  transfers between devices with their start and end apart: 58, of which 18 were waited for; matrix products, arithmetic and copies ran while one was open for 1% of the time, Pallas kernels for 34%

profile of v6, /device:TPU:0, one launch (start us, length us, event | category | flops | bytes accessed | tf_op | source)
XLA Modules:
  0.0 259.0 jit_solution(13668461741341502740)
XLA Ops:
  10.1 2.6 %copy-done.6 = f32[11264,128]{1,0:T(8,128)S(1)} copy-done((f32[11264,128]{1,0:T(8,128)S(1)}, f32[11264,128]{1,0:T(8,128)}, u32[]{:S(2)}) %copy-start.6) | copy-done | bytes 5767192
  22.7 6.9 %softmax.1 = (f32[1,128]{1,0:T(1,128)S(1)}, f32[24,512]{1,0:T(8,128)S(1)}, f32[11264,128]{1,0:T(8,128)}) custom-call(f32[11264,128]{1,0:T(8,128)S(1)} %copy-done.7), custom_call_target="tpu_custom_call" | custom-call | flops 1 | bytes 1 | tf_op jit(solution)/shard_map/softmax/pallas_call | solution.py:147
  42.0 8.6 %collective-permute-done.3.refs_0_.refs_1_ = f32[1408,128]{1,0:T(8,128)S(1)} collective-permute-done((f32[1408,128]{1,0:T(8,128)S(1)}, f32[1408,128]{1,0:T(8,128)S(1)}, u32[]{:S(2)}, u32[]{:S(2)}) %collective-permute-start.3) | collective-permute-done | bytes 720928 | tf_op jit(solution)/shard_map/ppermute | solution.py:607
  58.6 10.9 %collective-permute-done.9.refs_2_ = f32[152,512]{1,0:T(8,128)S(1)} collective-permute-done((f32[152,512]{1,0:T(8,128)S(1)}, f32[152,512]{1,0:T(8,128)S(1)}, u32[]{:S(2)}, u32[]{:S(2)}) %collective-permute-start.9) | collective-permute-done | bytes 311328 | tf_op jit(solution)/shard_map/ppermute | solution.py:607
  77.3 2.6 %collective-permute-start.16 = (f32[8,128]{1,0:T(8,128)S(1)}, f32[8,128]{1,0:T(8,128)S(1)}, u32[]{:S(2)}, u32[]{:S(2)}) collective-permute-start(f32[8,128]{1,0:T(8,128)S(1)} %add_all.1.refs_2_), channel_id=1, source_target_pairs={{0,2},{1,3},{2,0},{3,1},{4,6},{5,7},{6,4},{7,5},{8,10},{9,11},{10,... | collective-permute-start | bytes 12296 | tf_op jit(solution)/shard_map/ppermute | solution.py:610
  103.1 3.6 %collective-permute-start.28 = (f32[928,128]{1,0:T(8,128)}, f32[928,128]{1,0:T(8,128)}, u32[]{:S(2)}, u32[]{:S(2)}) collective-permute-start(f32[928,128]{1,0:T(8,128)} %dmap.10.a_ref), channel_id=1, source_target_pairs={{0,1},{1,0},{2,3},{3,2},{4,5},{5,4},{6,7},{7,6},{8,9},{9,8},{10,11... | collective-permute-start | bytes 1425416 | tf_op jit(solution)/shard_map/ppermute | solution.py:768
  112.6 4.2 %ratio.1 = (f32[11264,128]{1,0:T(8,128)}, f32[16,704]{1,0:T(8,128)S(1)}, f32[8,128]{1,0:T(8,128)S(1)}, f32[8,128]{1,0:T(8,128)S(1)}) custom-call(f32[24,512]{1,0:T(8,128)S(1)} %copy-done.54, f32[16,704]{1,0:T(8,128)S(1)} %reshape.16.density_ref, ...), custom_call_target="tpu_custom_call", output_to_operand_aliasing={{0}: (3, {})} | custom-call | flops 1 | bytes 1 | tf_op jit(solution)/shard_map/ratio/pallas_call | solution.py:413
  119.2 3.6 %collective-permute-start.30 = (f32[968,128]{1,0:T(8,128)S(1)}, f32[968,128]{1,0:T(8,128)S(1)}, u32[]{:S(2)}, u32[]{:S(2)}) collective-permute-start(f32[968,128]{1,0:T(8,128)S(1)} %get-tuple-element.338), channel_id=1, source_target_pairs={{0,1},{1,0},{2,3},{3,2},{4,5},{5,4},{6,7},{7,6},{8,9},{9,8},{10,11... | collective-permute-start | bytes 1486856 | tf_op jit(solution)/shard_map/ppermute | solution.py:768
  138.6 4.9 %collective-permute-done.33.b_ref.refs_1_.refs_0_ = f32[928,128]{1,0:T(8,128)S(1)} collective-permute-done((f32[928,128]{1,0:T(8,128)S(1)}, f32[928,128]{1,0:T(8,128)S(1)}, u32[]{:S(2)}, u32[]{:S(2)}) %collective-permute-start.33) | collective-permute-done | bytes 475168 | tf_op jit(solution)/shard_map/ppermute | solution.py:768
  143.6 4.0 %collective-permute-start.32 = (f32[928,128]{1,0:T(8,128)}, f32[928,128]{1,0:T(8,128)}, u32[]{:S(2)}, u32[]{:S(2)}) collective-permute-start(f32[928,128]{1,0:T(8,128)} %get-tuple-element.350), channel_id=1, source_target_pairs={{0,1},{1,0},{2,3},{3,2},{4,5},{5,4},{6,7},{7,6},{8,9},{9,8},{10,11... | collective-permute-start | bytes 1425416 | tf_op jit(solution)/shard_map/ppermute | solution.py:768
  164.6 3.0 %final.8 = (f32[11264,128]{1,0:T(8,128)}, f32[11264,128]{1,0:T(8,128)}) custom-call(s32[1]{0:T(128)} %bitcast.end_ref, s32[26]{0:T(128)S(1)} %stack.107.at_ref, f32[968,128]{1,0:T(8,128)S(1)} %copy-done.28, f32[928,128]{1,0:T(8,128)S(1)} %copy-done.31, f32[968,128]{1,0:T(8,128)S(1)} %copy-done.39, ...), custom_call_target="tpu_custom_call", output_to_operand_aliasing={{0}: (9, {}), {1}: (10, {})} | custom-call | flops 1 | bytes 1 | tf_op jit(solution)/shard_map/final/pallas_call | solution.py:552
  173.2 3.4 %final.9 = (f32[11264,128]{1,0:T(8,128)}, f32[11264,128]{1,0:T(8,128)}) custom-call(s32[1]{0:T(128)} %bitcast.end_ref, s32[26]{0:T(128)S(1)} %stack.107.at_ref, f32[928,128]{1,0:T(8,128)S(1)} %copy-done.32, f32[928,128]{1,0:T(8,128)} %collective-permute-done.32.b_ref.refs_1_, ...), custom_call_target="tpu_custom_call", output_to_operand_aliasing={{0}: (9, {}), {1}: (10, {})} | custom-call | flops 1 | bytes 1 | tf_op jit(solution)/shard_map/final/pallas_call | solution.py:552
  188.0 5.0 %collective-permute-start.44 = (f32[848,128]{1,0:T(8,128)S(1)}, f32[848,128]{1,0:T(8,128)S(1)}, u32[]{:S(2)}, u32[]{:S(2)}) collective-permute-start(f32[848,128]{1,0:T(8,128)S(1)} %get-tuple-element.413), channel_id=1, source_target_pairs={{0,1},{1,0},{2,3},{3,2},{4,5},{5,4},{6,7},{7,6},{8,9},{9,8},{10,11... | collective-permute-start | bytes 1302536 | tf_op jit(solution)/shard_map/ppermute | solution.py:768
  195.3 3.2 %final.10 = (f32[11264,128]{1,0:T(8,128)}, f32[11264,128]{1,0:T(8,128)}) custom-call(s32[1]{0:T(128)} %bitcast.end_ref, s32[26]{0:T(128)S(1)} %stack.107.at_ref, f32[848,128]{1,0:T(8,128)} %collective-permute-done.36.b_ref.refs_0_, f32[848,128]{1,0:T(8,128)S(1)} %collective-permute-done.40.b_ref.refs_1_.refs_0_, ...), custom_call_target="tpu_custom_call", output_to_operand_aliasing={{0}: (9, {}), {1}: (10, {})} | custom-call | flops 1 | bytes 1 | tf_op jit(solution)/shard_map/final/pallas_call | solution.py:552
  205.5 8.8 %collective-permute-start.46 = (f32[848,128]{1,0:T(8,128)S(1)}, f32[848,128]{1,0:T(8,128)S(1)}, u32[]{:S(2)}, u32[]{:S(2)}) collective-permute-start(f32[848,128]{1,0:T(8,128)S(1)} %get-tuple-element.425), channel_id=1, source_target_pairs={{0,1},{1,0},{2,3},{3,2},{4,5},{5,4},{6,7},{7,6},{8,9},{9,8},{10,11... | collective-permute-start | bytes 1302536 | tf_op jit(solution)/shard_map/ppermute | solution.py:768
  214.3 2.7 %final.11 = (f32[11264,128]{1,0:T(8,128)}, f32[11264,128]{1,0:T(8,128)}) custom-call(s32[1]{0:T(128)} %bitcast.end_ref, s32[26]{0:T(128)S(1)} %stack.107.at_ref, f32[848,128]{1,0:T(8,128)S(1)} %collective-permute-done.40.b_ref.refs_1_.refs_0_, f32[848,128]{1,0:T(8,128)S(1)} %collective-permute-done.39.b_ref.refs_1_, ...), custom_call_target="tpu_custom_call", output_to_operand_aliasing={{0}: (11, {}), {1}: (12, {})} | custom-call | flops 1 | bytes 1 | tf_op jit(solution)/shard_map/final/pallas_call | solution.py:552
  220.5 2.8 %final.12 = (f32[11264,128]{1,0:T(8,128)}, f32[11264,128]{1,0:T(8,128)}) custom-call(s32[1]{0:T(128)} %bitcast.end_ref, s32[26]{0:T(128)S(1)} %stack.107.at_ref, f32[848,128]{1,0:T(8,128)S(1)} %collective-permute-done.44.b_ref.refs_2_.refs_0_, ...), custom_call_target="tpu_custom_call", output_to_operand_aliasing={{0}: (9, {}), {1}: (10, {})} | custom-call | flops 1 | bytes 1 | tf_op jit(solution)/shard_map/final/pallas_call | solution.py:552
  224.7 4.7 %collective-permute-done.50.b_ref.refs_2_.refs_0_ = f32[848,128]{1,0:T(8,128)S(1)} collective-permute-done((f32[848,128]{1,0:T(8,128)S(1)}, f32[848,128]{1,0:T(8,128)S(1)}, u32[]{:S(2)}, u32[]{:S(2)}) %collective-permute-start.50) | collective-permute-done | bytes 434208 | tf_op jit(solution)/shard_map/ppermute | solution.py:768
  230.2 4.9 %collective-permute-start.55 = (f32[848,128]{1,0:T(8,128)S(1)}, f32[848,128]{1,0:T(8,128)S(1)}, u32[]{:S(2)}, u32[]{:S(2)}) collective-permute-start(f32[848,128]{1,0:T(8,128)S(1)} %add.121.refs_4_), channel_id=1, source_target_pairs={{0,1},{1,0},{2,3},{3,2},{4,5},{5,4},{6,7},{7,6},{8,9},{9,8},{10,11... | collective-permute-start | bytes 1302536 | tf_op jit(solution)/shard_map/ppermute | solution.py:768
  235.1 5.7 %collective-permute-start.52 = (f32[848,128]{1,0:T(8,128)S(1)}, f32[848,128]{1,0:T(8,128)S(1)}, u32[]{:S(2)}, u32[]{:S(2)}) collective-permute-start(f32[848,128]{1,0:T(8,128)S(1)} %add.123.refs_5_.refs_2_), channel_id=1, source_target_pairs={{0,1},{1,0},{2,3},{3,2},{4,5},{5,4},{6,7},{7,6},{8,9},{9,8},{10,11... | collective-permute-start | bytes 1302536 | tf_op jit(solution)/shard_map/ppermute | solution.py:768
  241.6 2.8 %final.13 = (f32[11264,128]{1,0:T(8,128)}, f32[11264,128]{1,0:T(8,128)}) custom-call(s32[1]{0:T(128)} %bitcast.end_ref, s32[26]{0:T(128)S(1)} %stack.107.at_ref, f32[848,128]{1,0:T(8,128)S(1)} %collective-permute-done.47.b_ref.refs_1_.refs_0_, f32[848,128]{1,0:T(8,128)S(1)} %collective-permute-done.46.b_ref.refs_1_, ...), custom_call_target="tpu_custom_call", output_to_operand_aliasing={{0}: (11, {}), {1}: (12, {})} | custom-call | flops 1 | bytes 1 | tf_op jit(solution)/shard_map/final/pallas_call | solution.py:552
  245.3 4.6 %egrad.5 = f32[1408,512]{1,0:T(8,128)} custom-call(s32[26]{0:T(128)S(1)} %stack.107.at_ref, f32[2816,128]{1,0:T(8,128)S(1)} %copy-done.9, f32[1408,128]{1,0:T(8,128)S(1)} %copy-done.34, f32[1408,128]{1,0:T(8,128)S(1)} %copy-done.36, f32[1408,128]{1,0:T(8,128)S(1)} %copy-done.17, f32[1408,128]{1,0:T(8,128)S(1)} %copy-done.15, ...), custom_call_target="tpu_custom_call" | custom-call | flops 1 | bytes 1 | tf_op jit(solution)/shard_map/egrad/pallas_call | solution.py:373
  251.7 2.7 %final.14 = (f32[11264,128]{1,0:T(8,128)}, f32[11264,128]{1,0:T(8,128)}) custom-call(s32[1]{0:T(128)} %bitcast.end_ref, s32[26]{0:T(128)S(1)} %stack.107.at_ref, f32[848,128]{1,0:T(8,128)S(1)} %collective-permute-done.50.b_ref.refs_2_.refs_0_, f32[848,128]{1,0:T(8,128)S(1)} %collective-permute-done.55.refs_1_, ...), custom_call_target="tpu_custom_call", output_to_operand_aliasing={{0}: (11, {}), {1}: (12, {})} | custom-call | flops 1 | bytes 1 | tf_op jit(solution)/shard_map/final/pallas_call | solution.py:552
  256.1 2.7 %final.15 = (f32[11264,128]{1,0:T(8,128)}, f32[11264,128]{1,0:T(8,128)}) custom-call(s32[1]{0:T(128)} %bitcast.end_ref, s32[26]{0:T(128)S(1)} %stack.107.at_ref, f32[848,128]{1,0:T(8,128)S(1)} %collective-permute-done.52.refs_2_.refs_0_, f32[816,128]{1,0:T(8,128)S(1)} %collective-permute-done.54.refs_1_, ...), custom_call_target="tpu_custom_call", output_to_operand_aliasing={{0}: (9, {}), {1}: (10, {})} | custom-call | flops 1 | bytes 1 | tf_op jit(solution)/shard_map/final/pallas_call | solution.py:552
  (285 shorter events, 148.2 us)
Async XLA Ops:
  0.6 28.9 %collective-permute-start = (f32[1408,512]{1,0:T(8,128)}, f32[1408,512]{1,0:T(8,128)}, u32[]{:S(2)}, u32[]{:S(2)}) collective-permute-start(f32[1408,512]{1,0:T(8,128)} %x_ref), channel_id=1, source_target_pairs={{0,4},{4,0},{8,12},{12,8},{16,20},{20,16},{24,28},{28,24},{1,5},{5... | collective-permute-start | bytes 8650760 | tf_op jit(solution)/shard_map/ppermute | solution.py:607
  17.6 20.1 %collective-permute-start.5 = (f32[1408,128]{1,0:T(8,128)S(1)}, f32[1408,128]{1,0:T(8,128)S(1)}, u32[]{:S(2)}, u32[]{:S(2)}) collective-permute-start(f32[1408,128]{1,0:T(8,128)S(1)} %get-tuple-element.271), channel_id=1, source_target_pairs={{0,24},{4,28},{8,16},{12,20},{16,8},{20,12},{24,0},{28,4},{1,25},{... | collective-permute-start | bytes 2162696 | tf_op jit(solution)/shard_map/ppermute | solution.py:607
  19.1 21.5 %collective-permute-start.4 = (f32[1408,128]{1,0:T(8,128)S(1)}, f32[1408,128]{1,0:T(8,128)S(1)}, u32[]{:S(2)}, u32[]{:S(2)}) collective-permute-start(f32[1408,128]{1,0:T(8,128)S(1)} %join.1), channel_id=1, source_target_pairs={{0,1},{1,0},{2,3},{3,2},{4,5},{5,4},{6,7},{7,6},{8,9},{9,8},{10,11... | collective-permute-start | bytes 2162696 | tf_op jit(solution)/shard_map/ppermute | solution.py:610
  20.6 30.0 %collective-permute-start.3 = (f32[1408,128]{1,0:T(8,128)S(1)}, f32[1408,128]{1,0:T(8,128)S(1)}, u32[]{:S(2)}, u32[]{:S(2)}) collective-permute-start(f32[1408,128]{1,0:T(8,128)S(1)} %get-tuple-element.266), channel_id=1, source_target_pairs={{0,8},{4,12},{8,0},{12,4},{16,24},{20,28},{24,16},{28,20},{1,9},{5... | collective-permute-start | bytes 2162696 | tf_op jit(solution)/shard_map/ppermute | solution.py:607
  21.2 32.5 %collective-permute-start.8 = (f32[1408,128]{1,0:T(8,128)S(1)}, f32[1408,128]{1,0:T(8,128)S(1)}, u32[]{:S(2)}, u32[]{:S(2)}) collective-permute-start(f32[1408,128]{1,0:T(8,128)S(1)} %get-tuple-element.284), channel_id=1, source_target_pairs={{0,16},{4,20},{8,24},{12,28},{16,0},{20,4},{24,8},{28,12},{1,17},{... | collective-permute-start | bytes 2162696 | tf_op jit(solution)/shard_map/ppermute | solution.py:607
  37.6 18.8 %collective-permute-start.10 = (f32[1408,128]{1,0:T(8,128)S(1)}, f32[1408,128]{1,0:T(8,128)S(1)}, u32[]{:S(2)}, u32[]{:S(2)}) collective-permute-start(f32[1408,128]{1,0:T(8,128)S(1)} %collective-permute-done.5.refs_0_.refs_5_.refs_3_), channel_id=1, source_target_pairs={{0,1},{1,0},{2,3},{3,2},{4,5},{5,4},{6,7},{7,6},{8,9},{9,8},{10,11... | collective-permute-start | bytes 2162696 | tf_op jit(solution)/shard_map/ppermute | solution.py:610
  52.1 17.4 %collective-permute-start.7 = (f32[152,512]{1,0:T(8,128)S(1)}, f32[152,512]{1,0:T(8,128)S(1)}, u32[]{:S(2)}, u32[]{:S(2)}) collective-permute-start(f32[152,512]{1,0:T(8,128)S(1)} %pred_.11), channel_id=1, source_target_pairs={{0,8},{4,12},{8,0},{12,4},{16,24},{20,28},{24,16},{28,20},{1,9},{5... | collective-permute-start | bytes 933896 | tf_op jit(solution)/shard_map/ppermute | solution.py:607
  94.2 22.6 %collective-permute-start.22 = (f32[1408,128]{1,0:T(8,128)}, f32[1408,128]{1,0:T(8,128)}, u32[]{:S(2)}, u32[]{:S(2)}) collective-permute-start(f32[1408,128]{1,0:T(8,128)} %get-tuple-element.314), channel_id=1, source_target_pairs={{0,8},{4,12},{8,0},{12,4},{16,24},{20,28},{24,16},{28,20},{1,9},{5... | collective-permute-start | bytes 2162696 | tf_op jit(solution)/shard_map/ppermute | solution.py:607
  97.0 27.0 %collective-permute-start.24 = (f32[1408,128]{1,0:T(8,128)}, f32[1408,128]{1,0:T(8,128)}, u32[]{:S(2)}, u32[]{:S(2)}) collective-permute-start(f32[1408,128]{1,0:T(8,128)} %get-tuple-element.330), channel_id=1, source_target_pairs={{0,16},{4,20},{8,24},{12,28},{16,0},{20,4},{24,8},{28,12},{1,17},{... | collective-permute-start | bytes 2162696 | tf_op jit(solution)/shard_map/ppermute | solution.py:607
  103.1 23.1 %collective-permute-start.28 = (f32[928,128]{1,0:T(8,128)}, f32[928,128]{1,0:T(8,128)}, u32[]{:S(2)}, u32[]{:S(2)}) collective-permute-start(f32[928,128]{1,0:T(8,128)} %dmap.10.a_ref), channel_id=1, source_target_pairs={{0,1},{1,0},{2,3},{3,2},{4,5},{5,4},{6,7},{7,6},{8,9},{9,8},{10,11... | collective-permute-start | bytes 1425416 | tf_op jit(solution)/shard_map/ppermute | solution.py:768
  110.1 19.0 %collective-permute-start.31 = (f32[928,128]{1,0:T(8,128)}, f32[928,128]{1,0:T(8,128)}, u32[]{:S(2)}, u32[]{:S(2)}) collective-permute-start(f32[928,128]{1,0:T(8,128)} %add.109.s_ref), channel_id=1, source_target_pairs={{1,2},{2,1},{5,6},{6,5},{9,10},{10,9},{13,14},{14,13},{17,18},{18,... | collective-permute-start | bytes 1425416 | tf_op jit(solution)/shard_map/ppermute | solution.py:865
  125.3 23.1 %collective-permute-start.25 = (f32[1416,128]{1,0:T(8,128)S(1)}, f32[1416,128]{1,0:T(8,128)S(1)}, u32[]{:S(2)}, u32[]{:S(2)}) collective-permute-start(f32[1416,128]{1,0:T(8,128)S(1)} %get-tuple-element.333), channel_id=1, source_target_pairs={{0,8},{4,12},{8,0},{12,4},{16,24},{20,28},{24,16},{28,20},{1,9},{5... | collective-permute-start | bytes 2174984 | tf_op jit(solution)/shard_map/ppermute | solution.py:607
  128.1 27.0 %collective-permute-start.26 = (f32[1416,128]{1,0:T(8,128)S(1)}, f32[1416,128]{1,0:T(8,128)S(1)}, u32[]{:S(2)}, u32[]{:S(2)}) collective-permute-start(f32[1416,128]{1,0:T(8,128)S(1)} %get-tuple-element.334), channel_id=1, source_target_pairs={{0,16},{4,20},{8,24},{12,28},{16,0},{20,4},{24,8},{28,12},{1,17},{... | collective-permute-start | bytes 2174984 | tf_op jit(solution)/shard_map/ppermute | solution.py:607
  134.0 21.1 %collective-permute-start.27 = (f32[136,512]{1,0:T(8,128)S(1)}, f32[136,512]{1,0:T(8,128)S(1)}, u32[]{:S(2)}, u32[]{:S(2)}) collective-permute-start(f32[136,512]{1,0:T(8,128)S(1)} %get-tuple-element.478.refs_4_.refs_7_.refs_5_), channel_id=1, source_target_pairs={{0,24},{4,28},{8,16},{12,20},{16,8},{20,12},{24,0},{28,4},{1,25},{... | collective-permute-start | bytes 835592 | tf_op jit(solution)/shard_map/ppermute | solution.py:607
  143.6 24.1 %collective-permute-start.32 = (f32[928,128]{1,0:T(8,128)}, f32[928,128]{1,0:T(8,128)}, u32[]{:S(2)}, u32[]{:S(2)}) collective-permute-start(f32[928,128]{1,0:T(8,128)} %get-tuple-element.350), channel_id=1, source_target_pairs={{0,1},{1,0},{2,3},{3,2},{4,5},{5,4},{6,7},{7,6},{8,9},{9,8},{10,11... | collective-permute-start | bytes 1425416 | tf_op jit(solution)/shard_map/ppermute | solution.py:768
  148.5 21.0 %collective-permute-start.37 = (f32[848,128]{1,0:T(8,128)}, f32[848,128]{1,0:T(8,128)}, u32[]{:S(2)}, u32[]{:S(2)}) collective-permute-start(f32[848,128]{1,0:T(8,128)} %add.113.s_ref), channel_id=1, source_target_pairs={{1,2},{2,1},{5,6},{6,5},{9,10},{10,9},{13,14},{14,13},{17,18},{18,... | collective-permute-start | bytes 1302536 | tf_op jit(solution)/shard_map/ppermute | solution.py:865
  153.4 23.2 %collective-permute-start.36 = (f32[848,128]{1,0:T(8,128)}, f32[848,128]{1,0:T(8,128)}, u32[]{:S(2)}, u32[]{:S(2)}) collective-permute-start(f32[848,128]{1,0:T(8,128)} %get-tuple-element.372), channel_id=1, source_target_pairs={{0,1},{1,0},{2,3},{3,2},{4,5},{5,4},{6,7},{7,6},{8,9},{9,8},{10,11... | collective-permute-start | bytes 1302536 | tf_op jit(solution)/shard_map/ppermute | solution.py:768
  158.2 28.6 %collective-permute-start.42 = (f32[1408,128]{1,0:T(8,128)}, f32[1408,128]{1,0:T(8,128)}, u32[]{:S(2)}, u32[]{:S(2)}) collective-permute-start(f32[1408,128]{1,0:T(8,128)} %dmap.12), channel_id=1, source_target_pairs={{0,24},{4,28},{8,16},{12,20},{16,8},{20,12},{24,0},{28,4},{1,25},{... | collective-permute-start | bytes 2162696 | tf_op jit(solution)/shard_map/ppermute | solution.py:607
  178.8 19.7 %collective-permute-start.39 = (f32[848,128]{1,0:T(8,128)S(1)}, f32[848,128]{1,0:T(8,128)S(1)}, u32[]{:S(2)}, u32[]{:S(2)}) collective-permute-start(f32[848,128]{1,0:T(8,128)S(1)} %get-tuple-element.392), channel_id=1, source_target_pairs={{0,1},{1,0},{2,3},{3,2},{4,5},{5,4},{6,7},{7,6},{8,9},{9,8},{10,11... | collective-permute-start | bytes 1302536 | tf_op jit(solution)/shard_map/ppermute | solution.py:768
  182.3 21.4 %collective-permute-start.38 = (f32[1416,128]{1,0:T(8,128)S(1)}, f32[1416,128]{1,0:T(8,128)S(1)}, u32[]{:S(2)}, u32[]{:S(2)}) collective-permute-start(f32[1416,128]{1,0:T(8,128)S(1)} %dmap.13), channel_id=1, source_target_pairs={{0,24},{4,28},{8,16},{12,20},{16,8},{20,12},{24,0},{28,4},{1,25},{... | collective-permute-start | bytes 2174984 | tf_op jit(solution)/shard_map/ppermute | solution.py:607
  203.7 41.7 %collective-permute-start.56 = (f32[704,512]{1,0:T(8,128)S(1)}, f32[704,512]{1,0:T(8,128)S(1)}, u32[]{:S(2)}, u32[]{:S(2)}) collective-permute-start(f32[704,512]{1,0:T(8,128)S(1)} %egrad.3), channel_id=1, source_target_pairs={{0,4},{4,0},{8,12},{12,8},{16,20},{20,16},{24,28},{28,24},{1,5},{5... | collective-permute-start | bytes 4325384 | tf_op jit(solution)/shard_map/ppermute | solution.py:607
  203.7 41.6 %collective-permute-start.57 = (f32[704,512]{1,0:T(8,128)S(1)}, f32[704,512]{1,0:T(8,128)S(1)}, u32[]{:S(2)}, u32[]{:S(2)}) collective-permute-start(f32[704,512]{1,0:T(8,128)S(1)} %egrad.4), channel_id=1, source_target_pairs={{0,4},{4,0},{8,12},{12,8},{16,20},{20,16},{24,28},{28,24},{1,5},{5... | collective-permute-start | bytes 4325384 | tf_op jit(solution)/shard_map/ppermute | solution.py:607
  205.5 18.5 %collective-permute-start.46 = (f32[848,128]{1,0:T(8,128)S(1)}, f32[848,128]{1,0:T(8,128)S(1)}, u32[]{:S(2)}, u32[]{:S(2)}) collective-permute-start(f32[848,128]{1,0:T(8,128)S(1)} %get-tuple-element.425), channel_id=1, source_target_pairs={{0,1},{1,0},{2,3},{3,2},{4,5},{5,4},{6,7},{7,6},{8,9},{9,8},{10,11... | collective-permute-start | bytes 1302536 | tf_op jit(solution)/shard_map/ppermute | solution.py:768
  230.2 19.8 %collective-permute-start.55 = (f32[848,128]{1,0:T(8,128)S(1)}, f32[848,128]{1,0:T(8,128)S(1)}, u32[]{:S(2)}, u32[]{:S(2)}) collective-permute-start(f32[848,128]{1,0:T(8,128)S(1)} %add.121.refs_4_), channel_id=1, source_target_pairs={{0,1},{1,0},{2,3},{3,2},{4,5},{5,4},{6,7},{7,6},{8,9},{9,8},{10,11... | collective-permute-start | bytes 1302536 | tf_op jit(solution)/shard_map/ppermute | solution.py:768
  (96 other events, 1038.7 us)

commit v7 on v6

--- a/solution.py
+++ b/solution.py
@@ -247,8 +247,9 @@
     ones = jnp.ones((8, genes), F32)
     rows = lax.broadcasted_iota(jnp.int32, (8, LANES), 0)
     spot = jnp.where(rows == 3, jnp.sum(weights_of(mask_ref, counts_ref)), 0.0)
+    wide_ref[3 * SLIDES :, :] = jnp.zeros((16 - 3 * SLIDES, genes), F32)
     for k, product in enumerate((pred * spatial, pred * pred, spatial * spatial)):
-        wide_ref[8 * k : 8 * k + 8, :] = exact(onehot, product, ((1,), (0,)))
+        wide_ref[SLIDES * k : SLIDES * (k + 1), :] = exact(onehot, product, ((1,), (0,)))[:SLIDES, :]
         spot = jnp.where(rows == k, exact(ones, product, ((1,), (1,))), spot)
     spot_ref[...] = spot
 
@@ -260,7 +261,7 @@
         functools.partial(sums_kernel, n_parts),
         out_shape=(
             jax.ShapeDtypeStruct((width, genes), F32),
-            jax.ShapeDtypeStruct((24, genes), F32),
+            jax.ShapeDtypeStruct((16, genes), F32),
             jax.ShapeDtypeStruct((8, width), F32),
             jax.ShapeDtypeStruct(by_cell.shape, F32),
         ),
@@ -275,7 +276,9 @@
     pred_ref, spatial_ref, ids_ref, mask_ref, counts_ref, inv_ref, d_ref, tot_ref = refs
     weights = weights_of(mask_ref, counts_ref)
     genes = pred_ref.shape[1]
-    a, b, c = (wides[0][8 * k : 8 * k + 8, :] + wides[1][8 * k : 8 * k + 8, :] for k in range(3))
+    sums = wides[0][...] + wides[1][...]
+    none = jnp.zeros((8 - SLIDES, genes), F32)
+    a, b, c = (jnp.concatenate([sums[SLIDES * k : SLIDES * (k + 1), :], none], axis=0) for k in range(3))
     e, f, h, wsum = (spot[k : k + 1, :] for k in range(4))
     wsum = jnp.max(wsum)
     gain = weights / wsum

time: 261 us -> 260 us (level)
  no operation moved by 1% of the time
where the time goes in v7:
time: 260 us; the launch traced here: 259 us
  starting transfers between devices  98.4 us (38%)
  Pallas kernels  93 us (36%)
  waiting for transfers between devices  49.7 us (19%)
  local copies, waits for them, and re-layouts  15.8 us (6%)
    ppermute x16, starting transfers between devices, send(): got[t] = lax.ppermute(buffer, 'gene', PAIR)  53.4 us
    ppermute x25, waiting for transfers between devices, swap(): return lax.ppermute(x, 'blk', [(i, i ^ m) for i in range(n_blk)])  28.7 us
    ppermute x25, starting transfers between devices, swap(): return lax.ppermute(x, 'blk', [(i, i ^ m) for i in range(n_blk)])  25.9 us
    pallas_call x8, Pallas kernels, final_block(): pl.pallas_call(functools.partial(final_kernel, place, cuts, step), in_spe...  23.2 us
    ppermute x16, waiting for transfers between devices, send(): got[t] = lax.ppermute(buffer, 'gene', PAIR)  17.1 us
    unnamed x124, local copies, waits for them, and re-layouts  13.7 us
    pallas_call x10, Pallas kernels, next_piece(): pl.pallas_call(functools.partial(next_kernel, cuts), in_specs=[SMEM] + [V...  12.4 us
    ppermute x13, starting transfers between devices, shards(): mid[t] = lax.ppermute(part[t], 'gene', MIDDLE)  11.9 us
  transfers between devices with their start and end apart: 58, of which 18 were waited for; matrix products, arithmetic and copies ran while one was open for 1% of the time, Pallas kernels for 34%

profile of v7, /device:TPU:0, one launch (start us, length us, event | category | flops | bytes accessed | tf_op | source)
XLA Modules:
  0.0 258.9 jit_solution(12165713917608475732)
XLA Ops:
  10.1 2.6 %copy-done.6 = f32[11264,128]{1,0:T(8,128)S(1)} copy-done((f32[11264,128]{1,0:T(8,128)S(1)}, f32[11264,128]{1,0:T(8,128)}, u32[]{:S(2)}) %copy-start.6) | copy-done | bytes 5767192
  22.7 6.9 %softmax.1 = (f32[1,128]{1,0:T(1,128)S(1)}, f32[24,512]{1,0:T(8,128)S(1)}, f32[11264,128]{1,0:T(8,128)}) custom-call(f32[11264,128]{1,0:T(8,128)S(1)} %copy-done.7), custom_call_target="tpu_custom_call" | custom-call | flops 1 | bytes 1 | tf_op jit(solution)/shard_map/softmax/pallas_call | solution.py:147
  42.0 8.6 %collective-permute-done.3.refs_0_.refs_1_ = f32[1408,128]{1,0:T(8,128)S(1)} collective-permute-done((f32[1408,128]{1,0:T(8,128)S(1)}, f32[1408,128]{1,0:T(8,128)S(1)}, u32[]{:S(2)}, u32[]{:S(2)}) %collective-permute-start.3) | collective-permute-done | bytes 720928 | tf_op jit(solution)/shard_map/ppermute | solution.py:610
  58.6 10.9 %collective-permute-done.9.refs_2_ = f32[152,512]{1,0:T(8,128)S(1)} collective-permute-done((f32[152,512]{1,0:T(8,128)S(1)}, f32[152,512]{1,0:T(8,128)S(1)}, u32[]{:S(2)}, u32[]{:S(2)}) %collective-permute-start.9) | collective-permute-done | bytes 311328 | tf_op jit(solution)/shard_map/ppermute | solution.py:610
  77.2 2.6 %collective-permute-start.16 = (f32[8,128]{1,0:T(8,128)S(1)}, f32[8,128]{1,0:T(8,128)S(1)}, u32[]{:S(2)}, u32[]{:S(2)}) collective-permute-start(f32[8,128]{1,0:T(8,128)S(1)} %add_all.1.refs_2_), channel_id=1, source_target_pairs={{0,2},{1,3},{2,0},{3,1},{4,6},{5,7},{6,4},{7,5},{8,10},{9,11},{10,... | collective-permute-start | bytes 12296 | tf_op jit(solution)/shard_map/ppermute | solution.py:613
  103.2 3.6 %collective-permute-start.28 = (f32[928,128]{1,0:T(8,128)}, f32[928,128]{1,0:T(8,128)}, u32[]{:S(2)}, u32[]{:S(2)}) collective-permute-start(f32[928,128]{1,0:T(8,128)} %dmap.10.a_ref), channel_id=1, source_target_pairs={{0,1},{1,0},{2,3},{3,2},{4,5},{5,4},{6,7},{7,6},{8,9},{9,8},{10,11... | collective-permute-start | bytes 1425416 | tf_op jit(solution)/shard_map/ppermute | solution.py:771
  112.6 4.2 %ratio.1 = (f32[11264,128]{1,0:T(8,128)}, f32[16,704]{1,0:T(8,128)S(1)}, f32[8,128]{1,0:T(8,128)S(1)}, f32[8,128]{1,0:T(8,128)S(1)}) custom-call(f32[24,512]{1,0:T(8,128)S(1)} %copy-done.54, f32[16,704]{1,0:T(8,128)S(1)} %reshape.16.density_ref, ...), custom_call_target="tpu_custom_call", output_to_operand_aliasing={{0}: (3, {})} | custom-call | flops 1 | bytes 1 | tf_op jit(solution)/shard_map/ratio/pallas_call | solution.py:416
  119.1 3.6 %collective-permute-start.30 = (f32[968,128]{1,0:T(8,128)S(1)}, f32[968,128]{1,0:T(8,128)S(1)}, u32[]{:S(2)}, u32[]{:S(2)}) collective-permute-start(f32[968,128]{1,0:T(8,128)S(1)} %get-tuple-element.338), channel_id=1, source_target_pairs={{0,1},{1,0},{2,3},{3,2},{4,5},{5,4},{6,7},{7,6},{8,9},{9,8},{10,11... | collective-permute-start | bytes 1486856 | tf_op jit(solution)/shard_map/ppermute | solution.py:771
  138.6 4.7 %collective-permute-done.33.b_ref.refs_1_.refs_0_ = f32[928,128]{1,0:T(8,128)S(1)} collective-permute-done((f32[928,128]{1,0:T(8,128)S(1)}, f32[928,128]{1,0:T(8,128)S(1)}, u32[]{:S(2)}, u32[]{:S(2)}) %collective-permute-start.33) | collective-permute-done | bytes 475168 | tf_op jit(solution)/shard_map/ppermute | solution.py:771
  143.3 4.2 %collective-permute-start.32 = (f32[928,128]{1,0:T(8,128)}, f32[928,128]{1,0:T(8,128)}, u32[]{:S(2)}, u32[]{:S(2)}) collective-permute-start(f32[928,128]{1,0:T(8,128)} %get-tuple-element.350), channel_id=1, source_target_pairs={{0,1},{1,0},{2,3},{3,2},{4,5},{5,4},{6,7},{7,6},{8,9},{9,8},{10,11... | collective-permute-start | bytes 1425416 | tf_op jit(solution)/shard_map/ppermute | solution.py:771
  164.5 3.0 %final.8 = (f32[11264,128]{1,0:T(8,128)}, f32[11264,128]{1,0:T(8,128)}) custom-call(s32[1]{0:T(128)} %bitcast.end_ref, s32[26]{0:T(128)S(1)} %stack.107.at_ref, f32[968,128]{1,0:T(8,128)S(1)} %copy-done.28, f32[928,128]{1,0:T(8,128)S(1)} %copy-done.31, f32[968,128]{1,0:T(8,128)S(1)} %copy-done.39, ...), custom_call_target="tpu_custom_call", output_to_operand_aliasing={{0}: (9, {}), {1}: (10, {})} | custom-call | flops 1 | bytes 1 | tf_op jit(solution)/shard_map/final/pallas_call | solution.py:555
  173.0 3.4 %final.9 = (f32[11264,128]{1,0:T(8,128)}, f32[11264,128]{1,0:T(8,128)}) custom-call(s32[1]{0:T(128)} %bitcast.end_ref, s32[26]{0:T(128)S(1)} %stack.107.at_ref, f32[928,128]{1,0:T(8,128)S(1)} %copy-done.32, f32[928,128]{1,0:T(8,128)} %collective-permute-done.32.b_ref.refs_1_, ...), custom_call_target="tpu_custom_call", output_to_operand_aliasing={{0}: (9, {}), {1}: (10, {})} | custom-call | flops 1 | bytes 1 | tf_op jit(solution)/shard_map/final/pallas_call | solution.py:555
  187.9 4.9 %collective-permute-start.44 = (f32[848,128]{1,0:T(8,128)S(1)}, f32[848,128]{1,0:T(8,128)S(1)}, u32[]{:S(2)}, u32[]{:S(2)}) collective-permute-start(f32[848,128]{1,0:T(8,128)S(1)} %get-tuple-element.413), channel_id=1, source_target_pairs={{0,1},{1,0},{2,3},{3,2},{4,5},{5,4},{6,7},{7,6},{8,9},{9,8},{10,11... | collective-permute-start | bytes 1302536 | tf_op jit(solution)/shard_map/ppermute | solution.py:771
  195.2 3.2 %final.10 = (f32[11264,128]{1,0:T(8,128)}, f32[11264,128]{1,0:T(8,128)}) custom-call(s32[1]{0:T(128)} %bitcast.end_ref, s32[26]{0:T(128)S(1)} %stack.107.at_ref, f32[848,128]{1,0:T(8,128)} %collective-permute-done.36.b_ref.refs_0_, f32[848,128]{1,0:T(8,128)S(1)} %collective-permute-done.40.b_ref.refs_1_.refs_0_, ...), custom_call_target="tpu_custom_call", output_to_operand_aliasing={{0}: (9, {}), {1}: (10, {})} | custom-call | flops 1 | bytes 1 | tf_op jit(solution)/shard_map/final/pallas_call | solution.py:555
  205.3 8.8 %collective-permute-start.46 = (f32[848,128]{1,0:T(8,128)S(1)}, f32[848,128]{1,0:T(8,128)S(1)}, u32[]{:S(2)}, u32[]{:S(2)}) collective-permute-start(f32[848,128]{1,0:T(8,128)S(1)} %get-tuple-element.425), channel_id=1, source_target_pairs={{0,1},{1,0},{2,3},{3,2},{4,5},{5,4},{6,7},{7,6},{8,9},{9,8},{10,11... | collective-permute-start | bytes 1302536 | tf_op jit(solution)/shard_map/ppermute | solution.py:771
  214.2 2.7 %final.11 = (f32[11264,128]{1,0:T(8,128)}, f32[11264,128]{1,0:T(8,128)}) custom-call(s32[1]{0:T(128)} %bitcast.end_ref, s32[26]{0:T(128)S(1)} %stack.107.at_ref, f32[848,128]{1,0:T(8,128)S(1)} %collective-permute-done.40.b_ref.refs_1_.refs_0_, f32[848,128]{1,0:T(8,128)S(1)} %collective-permute-done.39.b_ref.refs_1_, ...), custom_call_target="tpu_custom_call", output_to_operand_aliasing={{0}: (11, {}), {1}: (12, {})} | custom-call | flops 1 | bytes 1 | tf_op jit(solution)/shard_map/final/pallas_call | solution.py:555
  220.4 2.8 %final.12 = (f32[11264,128]{1,0:T(8,128)}, f32[11264,128]{1,0:T(8,128)}) custom-call(s32[1]{0:T(128)} %bitcast.end_ref, s32[26]{0:T(128)S(1)} %stack.107.at_ref, f32[848,128]{1,0:T(8,128)S(1)} %collective-permute-done.44.b_ref.refs_2_.refs_0_, ...), custom_call_target="tpu_custom_call", output_to_operand_aliasing={{0}: (9, {}), {1}: (10, {})} | custom-call | flops 1 | bytes 1 | tf_op jit(solution)/shard_map/final/pallas_call | solution.py:555
  224.6 4.8 %collective-permute-done.50.b_ref.refs_2_.refs_0_ = f32[848,128]{1,0:T(8,128)S(1)} collective-permute-done((f32[848,128]{1,0:T(8,128)S(1)}, f32[848,128]{1,0:T(8,128)S(1)}, u32[]{:S(2)}, u32[]{:S(2)}) %collective-permute-start.50) | collective-permute-done | bytes 434208 | tf_op jit(solution)/shard_map/ppermute | solution.py:771
  230.1 4.9 %collective-permute-start.55 = (f32[848,128]{1,0:T(8,128)S(1)}, f32[848,128]{1,0:T(8,128)S(1)}, u32[]{:S(2)}, u32[]{:S(2)}) collective-permute-start(f32[848,128]{1,0:T(8,128)S(1)} %add.121.refs_4_), channel_id=1, source_target_pairs={{0,1},{1,0},{2,3},{3,2},{4,5},{5,4},{6,7},{7,6},{8,9},{9,8},{10,11... | collective-permute-start | bytes 1302536 | tf_op jit(solution)/shard_map/ppermute | solution.py:771
  235.0 5.7 %collective-permute-start.52 = (f32[848,128]{1,0:T(8,128)S(1)}, f32[848,128]{1,0:T(8,128)S(1)}, u32[]{:S(2)}, u32[]{:S(2)}) collective-permute-start(f32[848,128]{1,0:T(8,128)S(1)} %add.123.refs_5_.refs_2_), channel_id=1, source_target_pairs={{0,1},{1,0},{2,3},{3,2},{4,5},{5,4},{6,7},{7,6},{8,9},{9,8},{10,11... | collective-permute-start | bytes 1302536 | tf_op jit(solution)/shard_map/ppermute | solution.py:771
  241.4 2.8 %final.13 = (f32[11264,128]{1,0:T(8,128)}, f32[11264,128]{1,0:T(8,128)}) custom-call(s32[1]{0:T(128)} %bitcast.end_ref, s32[26]{0:T(128)S(1)} %stack.107.at_ref, f32[848,128]{1,0:T(8,128)S(1)} %collective-permute-done.47.b_ref.refs_1_.refs_0_, f32[848,128]{1,0:T(8,128)S(1)} %collective-permute-done.46.b_ref.refs_1_, ...), custom_call_target="tpu_custom_call", output_to_operand_aliasing={{0}: (11, {}), {1}: (12, {})} | custom-call | flops 1 | bytes 1 | tf_op jit(solution)/shard_map/final/pallas_call | solution.py:555
  245.2 4.6 %egrad.5 = f32[1408,512]{1,0:T(8,128)} custom-call(s32[26]{0:T(128)S(1)} %stack.107.at_ref, f32[2816,128]{1,0:T(8,128)S(1)} %copy-done.9, f32[1408,128]{1,0:T(8,128)S(1)} %copy-done.34, f32[1408,128]{1,0:T(8,128)S(1)} %copy-done.36, f32[1408,128]{1,0:T(8,128)S(1)} %copy-done.17, f32[1408,128]{1,0:T(8,128)S(1)} %copy-done.15, ...), custom_call_target="tpu_custom_call" | custom-call | flops 1 | bytes 1 | tf_op jit(solution)/shard_map/egrad/pallas_call | solution.py:376
  251.5 2.7 %final.14 = (f32[11264,128]{1,0:T(8,128)}, f32[11264,128]{1,0:T(8,128)}) custom-call(s32[1]{0:T(128)} %bitcast.end_ref, s32[26]{0:T(128)S(1)} %stack.107.at_ref, f32[848,128]{1,0:T(8,128)S(1)} %collective-permute-done.50.b_ref.refs_2_.refs_0_, f32[848,128]{1,0:T(8,128)S(1)} %collective-permute-done.55.refs_1_, ...), custom_call_target="tpu_custom_call", output_to_operand_aliasing={{0}: (11, {}), {1}: (12, {})} | custom-call | flops 1 | bytes 1 | tf_op jit(solution)/shard_map/final/pallas_call | solution.py:555
  256.0 2.7 %final.15 = (f32[11264,128]{1,0:T(8,128)}, f32[11264,128]{1,0:T(8,128)}) custom-call(s32[1]{0:T(128)} %bitcast.end_ref, s32[26]{0:T(128)S(1)} %stack.107.at_ref, f32[848,128]{1,0:T(8,128)S(1)} %collective-permute-done.52.refs_2_.refs_0_, f32[816,128]{1,0:T(8,128)S(1)} %collective-permute-done.54.refs_1_, ...), custom_call_target="tpu_custom_call", output_to_operand_aliasing={{0}: (9, {}), {1}: (10, {})} | custom-call | flops 1 | bytes 1 | tf_op jit(solution)/shard_map/final/pallas_call | solution.py:555
  (285 shorter events, 148.1 us)
Async XLA Ops:
  0.6 28.9 %collective-permute-start = (f32[1408,512]{1,0:T(8,128)}, f32[1408,512]{1,0:T(8,128)}, u32[]{:S(2)}, u32[]{:S(2)}) collective-permute-start(f32[1408,512]{1,0:T(8,128)} %x_ref), channel_id=1, source_target_pairs={{0,4},{4,0},{8,12},{12,8},{16,20},{20,16},{24,28},{28,24},{1,5},{5... | collective-permute-start | bytes 8650760 | tf_op jit(solution)/shard_map/ppermute | solution.py:610
  17.6 20.1 %collective-permute-start.5 = (f32[1408,128]{1,0:T(8,128)S(1)}, f32[1408,128]{1,0:T(8,128)S(1)}, u32[]{:S(2)}, u32[]{:S(2)}) collective-permute-start(f32[1408,128]{1,0:T(8,128)S(1)} %get-tuple-element.271), channel_id=1, source_target_pairs={{0,24},{4,28},{8,16},{12,20},{16,8},{20,12},{24,0},{28,4},{1,25},{... | collective-permute-start | bytes 2162696 | tf_op jit(solution)/shard_map/ppermute | solution.py:610
  19.1 21.5 %collective-permute-start.4 = (f32[1408,128]{1,0:T(8,128)S(1)}, f32[1408,128]{1,0:T(8,128)S(1)}, u32[]{:S(2)}, u32[]{:S(2)}) collective-permute-start(f32[1408,128]{1,0:T(8,128)S(1)} %join.1), channel_id=1, source_target_pairs={{0,1},{1,0},{2,3},{3,2},{4,5},{5,4},{6,7},{7,6},{8,9},{9,8},{10,11... | collective-permute-start | bytes 2162696 | tf_op jit(solution)/shard_map/ppermute | solution.py:613
  20.6 30.0 %collective-permute-start.3 = (f32[1408,128]{1,0:T(8,128)S(1)}, f32[1408,128]{1,0:T(8,128)S(1)}, u32[]{:S(2)}, u32[]{:S(2)}) collective-permute-start(f32[1408,128]{1,0:T(8,128)S(1)} %get-tuple-element.266), channel_id=1, source_target_pairs={{0,8},{4,12},{8,0},{12,4},{16,24},{20,28},{24,16},{28,20},{1,9},{5... | collective-permute-start | bytes 2162696 | tf_op jit(solution)/shard_map/ppermute | solution.py:610
  21.2 32.5 %collective-permute-start.8 = (f32[1408,128]{1,0:T(8,128)S(1)}, f32[1408,128]{1,0:T(8,128)S(1)}, u32[]{:S(2)}, u32[]{:S(2)}) collective-permute-start(f32[1408,128]{1,0:T(8,128)S(1)} %get-tuple-element.284), channel_id=1, source_target_pairs={{0,16},{4,20},{8,24},{12,28},{16,0},{20,4},{24,8},{28,12},{1,17},{... | collective-permute-start | bytes 2162696 | tf_op jit(solution)/shard_map/ppermute | solution.py:610
  37.6 18.8 %collective-permute-start.10 = (f32[1408,128]{1,0:T(8,128)S(1)}, f32[1408,128]{1,0:T(8,128)S(1)}, u32[]{:S(2)}, u32[]{:S(2)}) collective-permute-start(f32[1408,128]{1,0:T(8,128)S(1)} %collective-permute-done.5.refs_0_.refs_5_.refs_3_), channel_id=1, source_target_pairs={{0,1},{1,0},{2,3},{3,2},{4,5},{5,4},{6,7},{7,6},{8,9},{9,8},{10,11... | collective-permute-start | bytes 2162696 | tf_op jit(solution)/shard_map/ppermute | solution.py:613
  52.1 17.4 %collective-permute-start.7 = (f32[152,512]{1,0:T(8,128)S(1)}, f32[152,512]{1,0:T(8,128)S(1)}, u32[]{:S(2)}, u32[]{:S(2)}) collective-permute-start(f32[152,512]{1,0:T(8,128)S(1)} %pred_.11), channel_id=1, source_target_pairs={{0,8},{4,12},{8,0},{12,4},{16,24},{20,28},{24,16},{28,20},{1,9},{5... | collective-permute-start | bytes 933896 | tf_op jit(solution)/shard_map/ppermute | solution.py:610
  94.1 22.7 %collective-permute-start.22 = (f32[1408,128]{1,0:T(8,128)}, f32[1408,128]{1,0:T(8,128)}, u32[]{:S(2)}, u32[]{:S(2)}) collective-permute-start(f32[1408,128]{1,0:T(8,128)} %get-tuple-element.314), channel_id=1, source_target_pairs={{0,8},{4,12},{8,0},{12,4},{16,24},{20,28},{24,16},{28,20},{1,9},{5... | collective-permute-start | bytes 2162696 | tf_op jit(solution)/shard_map/ppermute | solution.py:610
  96.9 27.1 %collective-permute-start.24 = (f32[1408,128]{1,0:T(8,128)}, f32[1408,128]{1,0:T(8,128)}, u32[]{:S(2)}, u32[]{:S(2)}) collective-permute-start(f32[1408,128]{1,0:T(8,128)} %get-tuple-element.330), channel_id=1, source_target_pairs={{0,16},{4,20},{8,24},{12,28},{16,0},{20,4},{24,8},{28,12},{1,17},{... | collective-permute-start | bytes 2162696 | tf_op jit(solution)/shard_map/ppermute | solution.py:610
  103.2 22.9 %collective-permute-start.28 = (f32[928,128]{1,0:T(8,128)}, f32[928,128]{1,0:T(8,128)}, u32[]{:S(2)}, u32[]{:S(2)}) collective-permute-start(f32[928,128]{1,0:T(8,128)} %dmap.10.a_ref), channel_id=1, source_target_pairs={{0,1},{1,0},{2,3},{3,2},{4,5},{5,4},{6,7},{7,6},{8,9},{9,8},{10,11... | collective-permute-start | bytes 1425416 | tf_op jit(solution)/shard_map/ppermute | solution.py:771
  110.1 18.8 %collective-permute-start.31 = (f32[928,128]{1,0:T(8,128)}, f32[928,128]{1,0:T(8,128)}, u32[]{:S(2)}, u32[]{:S(2)}) collective-permute-start(f32[928,128]{1,0:T(8,128)} %add.109.s_ref), channel_id=1, source_target_pairs={{1,2},{2,1},{5,6},{6,5},{9,10},{10,9},{13,14},{14,13},{17,18},{18,... | collective-permute-start | bytes 1425416 | tf_op jit(solution)/shard_map/ppermute | solution.py:868
  125.3 23.0 %collective-permute-start.25 = (f32[1416,128]{1,0:T(8,128)S(1)}, f32[1416,128]{1,0:T(8,128)S(1)}, u32[]{:S(2)}, u32[]{:S(2)}) collective-permute-start(f32[1416,128]{1,0:T(8,128)S(1)} %get-tuple-element.333), channel_id=1, source_target_pairs={{0,8},{4,12},{8,0},{12,4},{16,24},{20,28},{24,16},{28,20},{1,9},{5... | collective-permute-start | bytes 2174984 | tf_op jit(solution)/shard_map/ppermute | solution.py:610
  128.0 27.0 %collective-permute-start.26 = (f32[1416,128]{1,0:T(8,128)S(1)}, f32[1416,128]{1,0:T(8,128)S(1)}, u32[]{:S(2)}, u32[]{:S(2)}) collective-permute-start(f32[1416,128]{1,0:T(8,128)S(1)} %get-tuple-element.334), channel_id=1, source_target_pairs={{0,16},{4,20},{8,24},{12,28},{16,0},{20,4},{24,8},{28,12},{1,17},{... | collective-permute-start | bytes 2174984 | tf_op jit(solution)/shard_map/ppermute | solution.py:610
  133.7 21.3 %collective-permute-start.27 = (f32[136,512]{1,0:T(8,128)S(1)}, f32[136,512]{1,0:T(8,128)S(1)}, u32[]{:S(2)}, u32[]{:S(2)}) collective-permute-start(f32[136,512]{1,0:T(8,128)S(1)} %get-tuple-element.478.refs_4_.refs_7_.refs_5_), channel_id=1, source_target_pairs={{0,24},{4,28},{8,16},{12,20},{16,8},{20,12},{24,0},{28,4},{1,25},{... | collective-permute-start | bytes 835592 | tf_op jit(solution)/shard_map/ppermute | solution.py:610
  143.3 24.2 %collective-permute-start.32 = (f32[928,128]{1,0:T(8,128)}, f32[928,128]{1,0:T(8,128)}, u32[]{:S(2)}, u32[]{:S(2)}) collective-permute-start(f32[928,128]{1,0:T(8,128)} %get-tuple-element.350), channel_id=1, source_target_pairs={{0,1},{1,0},{2,3},{3,2},{4,5},{5,4},{6,7},{7,6},{8,9},{9,8},{10,11... | collective-permute-start | bytes 1425416 | tf_op jit(solution)/shard_map/ppermute | solution.py:771
  148.3 21.0 %collective-permute-start.37 = (f32[848,128]{1,0:T(8,128)}, f32[848,128]{1,0:T(8,128)}, u32[]{:S(2)}, u32[]{:S(2)}) collective-permute-start(f32[848,128]{1,0:T(8,128)} %add.113.s_ref), channel_id=1, source_target_pairs={{1,2},{2,1},{5,6},{6,5},{9,10},{10,9},{13,14},{14,13},{17,18},{18,... | collective-permute-start | bytes 1302536 | tf_op jit(solution)/shard_map/ppermute | solution.py:868
  153.3 23.2 %collective-permute-start.36 = (f32[848,128]{1,0:T(8,128)}, f32[848,128]{1,0:T(8,128)}, u32[]{:S(2)}, u32[]{:S(2)}) collective-permute-start(f32[848,128]{1,0:T(8,128)} %get-tuple-element.372), channel_id=1, source_target_pairs={{0,1},{1,0},{2,3},{3,2},{4,5},{5,4},{6,7},{7,6},{8,9},{9,8},{10,11... | collective-permute-start | bytes 1302536 | tf_op jit(solution)/shard_map/ppermute | solution.py:771
  158.1 28.5 %collective-permute-start.42 = (f32[1408,128]{1,0:T(8,128)}, f32[1408,128]{1,0:T(8,128)}, u32[]{:S(2)}, u32[]{:S(2)}) collective-permute-start(f32[1408,128]{1,0:T(8,128)} %dmap.12), channel_id=1, source_target_pairs={{0,24},{4,28},{8,16},{12,20},{16,8},{20,12},{24,0},{28,4},{1,25},{... | collective-permute-start | bytes 2162696 | tf_op jit(solution)/shard_map/ppermute | solution.py:610
  178.6 19.7 %collective-permute-start.39 = (f32[848,128]{1,0:T(8,128)S(1)}, f32[848,128]{1,0:T(8,128)S(1)}, u32[]{:S(2)}, u32[]{:S(2)}) collective-permute-start(f32[848,128]{1,0:T(8,128)S(1)} %get-tuple-element.392), channel_id=1, source_target_pairs={{0,1},{1,0},{2,3},{3,2},{4,5},{5,4},{6,7},{7,6},{8,9},{9,8},{10,11... | collective-permute-start | bytes 1302536 | tf_op jit(solution)/shard_map/ppermute | solution.py:771
  182.2 21.4 %collective-permute-start.38 = (f32[1416,128]{1,0:T(8,128)S(1)}, f32[1416,128]{1,0:T(8,128)S(1)}, u32[]{:S(2)}, u32[]{:S(2)}) collective-permute-start(f32[1416,128]{1,0:T(8,128)S(1)} %dmap.13), channel_id=1, source_target_pairs={{0,24},{4,28},{8,16},{12,20},{16,8},{20,12},{24,0},{28,4},{1,25},{... | collective-permute-start | bytes 2174984 | tf_op jit(solution)/shard_map/ppermute | solution.py:610
  203.5 41.7 %collective-permute-start.56 = (f32[704,512]{1,0:T(8,128)S(1)}, f32[704,512]{1,0:T(8,128)S(1)}, u32[]{:S(2)}, u32[]{:S(2)}) collective-permute-start(f32[704,512]{1,0:T(8,128)S(1)} %egrad.3), channel_id=1, source_target_pairs={{0,4},{4,0},{8,12},{12,8},{16,20},{20,16},{24,28},{28,24},{1,5},{5... | collective-permute-start | bytes 4325384 | tf_op jit(solution)/shard_map/ppermute | solution.py:610
  203.6 41.6 %collective-permute-start.57 = (f32[704,512]{1,0:T(8,128)S(1)}, f32[704,512]{1,0:T(8,128)S(1)}, u32[]{:S(2)}, u32[]{:S(2)}) collective-permute-start(f32[704,512]{1,0:T(8,128)S(1)} %egrad.4), channel_id=1, source_target_pairs={{0,4},{4,0},{8,12},{12,8},{16,20},{20,16},{24,28},{28,24},{1,5},{5... | collective-permute-start | bytes 4325384 | tf_op jit(solution)/shard_map/ppermute | solution.py:610
  205.3 18.5 %collective-permute-start.46 = (f32[848,128]{1,0:T(8,128)S(1)}, f32[848,128]{1,0:T(8,128)S(1)}, u32[]{:S(2)}, u32[]{:S(2)}) collective-permute-start(f32[848,128]{1,0:T(8,128)S(1)} %get-tuple-element.425), channel_id=1, source_target_pairs={{0,1},{1,0},{2,3},{3,2},{4,5},{5,4},{6,7},{7,6},{8,9},{9,8},{10,11... | collective-permute-start | bytes 1302536 | tf_op jit(solution)/shard_map/ppermute | solution.py:771
  230.1 19.7 %collective-permute-start.55 = (f32[848,128]{1,0:T(8,128)S(1)}, f32[848,128]{1,0:T(8,128)S(1)}, u32[]{:S(2)}, u32[]{:S(2)}) collective-permute-start(f32[848,128]{1,0:T(8,128)S(1)} %add.121.refs_4_), channel_id=1, source_target_pairs={{0,1},{1,0},{2,3},{3,2},{4,5},{5,4},{6,7},{7,6},{8,9},{9,8},{10,11... | collective-permute-start | bytes 1302536 | tf_op jit(solution)/shard_map/ppermute | solution.py:771
  (96 other events, 1045.6 us)
